TPU v7x, 256 devices: a whole 4x4x8 slice. The times are simulated.
256 devices in a mesh: tgt: 16 (over y, x), src: 8 (over z_lo, core), head: 2 (over z_hi).
Axes of the slice: x: 4, y: 4, z: 8 (z_hi: 2, z_lo: 4; z = z_hi * 4 + z_lo), core: 2. Of those that a mesh axis runs over, the one named last changes fastest.
Arguments:
- queries: bfloat16 [8192, 4096], P(('tgt', 'src'), 'head'), may hold values from -84 to 84
- keys: bfloat16 [4096, 4096], P(('src', 'tgt'), 'head'), may hold values from -3 to 3
- values: bfloat16 [4096, 4096], P(('src', 'tgt'), 'head'), may hold values from -6 to 6
- out_grad: bfloat16 [8192, 4096], P(('tgt', 'src'), 'head'), may hold values from -4 to 4
- read_points: int32 [8192], P('tgt'), may hold values from 1 to 4096, as said below
- block_mask: int32 [64, 32], replicated, may hold values from 0 to 1, as said below
Outputs:
- query_grad: bfloat16 [8192, 4096], P(('tgt', 'src'), 'head')
- key_grad: bfloat16 [4096, 4096], P(('src', 'tgt'), 'head')
- value_grad: bfloat16 [4096, 4096], P(('src', 'tgt'), 'head')
Inputs may be any that keep to these rules, and one draw needn't show every extreme that they name: `read_points`: nondecreasing along the target positions; the first is 1 and the last is 4096. `block_mask`: every entry of column 0 is 1.
All inputs are finite; a program needn't handle non-finite values.
Results may differ from a plain program's by a relative error of at most 0.015.
Values may be sent and summed in bfloat16 or wider, within the bound.
No kernel may reach another device: no remote copies, remote signals or barrier semaphores. Data moves between devices by JAX's collectives and lax.ppermute only.
A program may use at most 128 MiB of HBM per device.

v0:
```python
from functools import partial

import jax
import jax.numpy as jnp
from jax import lax
from jax.sharding import PartitionSpec as P

HEAD_DIM = 128
TILE = 128


MASKED_SCORE = -1e30
CONTRACT_ROWS = (((0,), (0,)), ((), ()))
CONTRACT_COLUMNS = (((1,), (1,)), ((), ()))


def combined_all(part, axis, combine):
    gathered = jax.tree.map(lambda a: lax.all_gather(a, axis), part)

    def take(source):
        return jax.tree.map(lambda a: lax.dynamic_index_in_dim(a, source, 0, False), gathered)

    return lax.fori_loop(
        1, lax.axis_size(axis), lambda source, state: combine(state, take(source)), take(0)
    )


def column(tensor, head_index):
    return lax.dynamic_slice_in_dim(tensor, head_index * HEAD_DIM, HEAD_DIM, 1)


def allowed_block(read_rows, block_mask, row_start, col_start, width):
    row_total = read_rows.shape[0]
    tile_block = lax.dynamic_slice(
        block_mask, (row_start // TILE, col_start // TILE), (row_total // TILE, width // TILE)
    )
    tile_flags = jnp.broadcast_to(
        tile_block[:, None, :, None], (row_total // TILE, TILE, width // TILE, TILE)
    ).reshape(row_total, width)
    columns = col_start + lax.broadcasted_iota(jnp.int32, (row_total, width), 1)
    return (columns < read_rows[:, None]) & (tile_flags == 1)


def head_logits(query_rows, key_rows, head_index, allowed, softmax_scale):
    product = lax.dot_general(
        column(query_rows, head_index),
        column(key_rows, head_index),
        CONTRACT_COLUMNS,
        preferred_element_type=jnp.float32,
    )
    return jnp.where(allowed, product * softmax_scale, MASKED_SCORE)


def grad_probs(grad_rows, value_rows, head_index):
    return lax.dot_general(
        column(grad_rows, head_index),
        column(value_rows, head_index),
        CONTRACT_COLUMNS,
        preferred_element_type=jnp.float32,
    )


def head_probs(query_rows, key_rows, head_index, allowed, softmax_scale, highest, totals):
    logits = head_logits(query_rows, key_rows, head_index, allowed, softmax_scale)
    weights = jnp.where(allowed, jnp.exp(logits - highest[head_index][:, None]), 0.0)
    return weights / totals[head_index][:, None]


def local_stats(query_rows, key_rows, allowed, softmax_scale):
    head_total = query_rows.shape[1] // HEAD_DIM
    empty = jnp.zeros((head_total, query_rows.shape[0]), jnp.float32)

    def local_per_head(head_index, state_tuple):
        highest, totals, mixture = state_tuple
        logits = head_logits(query_rows, key_rows, head_index, allowed, softmax_scale)
        row_max = jnp.max(logits, axis=1)
        weights = jnp.where(allowed, jnp.exp(logits - row_max[:, None]), 0.0)
        highest = highest.at[head_index].set(row_max)
        totals = totals.at[head_index].set(jnp.sum(weights, axis=1))
        return (highest, totals, mixture)

    return lax.fori_loop(0, head_total, local_per_head, (empty, empty, empty))


def combine_two(first, second):
    highest = jnp.maximum(first[0], second[0])
    first_weight = jnp.exp(first[0] - highest)
    second_weight = jnp.exp(second[0] - highest)
    rescaled = tuple(
        (
            left_term * first_weight + right_term * second_weight
            for left_term, right_term in zip(first[1:], second[1:])
        )
    )
    return (highest,) + rescaled


def delta_terms(
    query_rows, grad_rows, key_rows, value_rows, allowed, softmax_scale, highest, totals
):

    def delta_per_head(head_index, partial_sums):
        probs = head_probs(
            query_rows, key_rows, head_index, allowed, softmax_scale, highest, totals
        )
        return partial_sums.at[head_index].set(
            jnp.sum(probs * grad_probs(grad_rows, value_rows, head_index), axis=1)
        )

    return lax.fori_loop(0, highest.shape[0], delta_per_head, jnp.zeros_like(highest))


def head_grads(
    query_rows,
    grad_rows,
    key_rows,
    value_rows,
    allowed,
    softmax_scale,
    highest,
    totals,
    delta_rows,
    head_index,
):
    probs = head_probs(query_rows, key_rows, head_index, allowed, softmax_scale, highest, totals)
    grad_logit = probs * (
        grad_probs(grad_rows, value_rows, head_index) - delta_rows[head_index][:, None]
    )
    probs_low = probs.astype(jnp.bfloat16)
    grad_low = grad_logit.astype(jnp.bfloat16)
    query_grad = (
        jnp.dot(grad_low, column(key_rows, head_index), preferred_element_type=jnp.float32)
        * softmax_scale
    ).astype(jnp.bfloat16)
    key_grad = (
        lax.dot_general(
            grad_low,
            column(query_rows, head_index),
            CONTRACT_ROWS,
            preferred_element_type=jnp.float32,
        )
        * softmax_scale
    )
    value_grad = lax.dot_general(
        probs_low, column(grad_rows, head_index), CONTRACT_ROWS, preferred_element_type=jnp.float32
    )
    return (query_grad, key_grad, value_grad)


def row_statistics(stats_of, delta_of):
    highest, totals, unused = stats_of(False)
    highest, totals = combined_all((highest, totals), "src", combine_two)
    delta_rows = lax.psum(delta_of(highest, totals), "src")
    return (highest, totals, delta_rows)


def tiles_layout(
    query_rows, grad_rows, key_rows, value_rows, read_points, block_mask, softmax_scale, head_group
):
    block_rows = query_rows.shape[0]
    row_start = lax.axis_index("tgt") * block_rows
    col_start = lax.axis_index("src") * key_rows.shape[0]
    allowed = allowed_block(read_points, block_mask, row_start, col_start, key_rows.shape[0])

    def stats_of(with_mixture):
        return local_stats(query_rows, key_rows, allowed, softmax_scale)

    def delta_of(highest, totals):
        return delta_terms(
            query_rows, grad_rows, key_rows, value_rows, allowed, softmax_scale, highest, totals
        )

    highest, totals, delta_rows = row_statistics(stats_of, delta_of)
    grads_for = partial(
        head_grads,
        query_rows,
        grad_rows,
        key_rows,
        value_rows,
        allowed,
        softmax_scale,
        highest,
        totals,
        delta_rows,
    )
    query_start = jnp.zeros(query_rows.shape, jnp.bfloat16)
    key_start = jnp.zeros((key_rows.shape[0], head_group * HEAD_DIM), jnp.float32)

    def tiles_per_head(head_index, buffers):
        query_acc, key_acc, value_acc = buffers
        current = grads_for(head_index)
        query_acc = lax.dynamic_update_slice_in_dim(query_acc, current[0], head_index * HEAD_DIM, 1)
        key_acc = lax.dynamic_update_slice_in_dim(key_acc, current[1], head_index * HEAD_DIM, 1)
        value_acc = lax.dynamic_update_slice_in_dim(value_acc, current[2], head_index * HEAD_DIM, 1)
        return (query_acc, key_acc, value_acc)

    query_acc, key_acc, value_acc = lax.fori_loop(
        0, head_group, tiles_per_head, (query_start, key_start, key_start)
    )
    key_grad, value_grad = (
        lax.psum_scatter(key_acc, "tgt", scatter_dimension=0, tiled=True),
        lax.psum_scatter(value_acc, "tgt", scatter_dimension=0, tiled=True),
    )
    return (query_acc, key_grad.astype(jnp.bfloat16), value_grad.astype(jnp.bfloat16))


def shards(queries, keys, values, out_grad, read_points, block_mask):
    softmax_scale = float(HEAD_DIM) ** (-0.5)
    head_group = keys.shape[1] // HEAD_DIM
    query_rows, grad_rows = (
        lax.all_gather(queries, "src", axis=0, tiled=True),
        lax.all_gather(out_grad, "src", axis=0, tiled=True),
    )
    key_rows, value_rows = (
        lax.all_gather(keys, "tgt", axis=0, tiled=True),
        lax.all_gather(values, "tgt", axis=0, tiled=True),
    )
    query_part, key_grad, value_grad = tiles_layout(
        query_rows,
        grad_rows,
        key_rows,
        value_rows,
        read_points,
        block_mask,
        softmax_scale,
        head_group,
    )
    query_grad = lax.psum_scatter(query_part, "src", scatter_dimension=0, tiled=True).astype(
        jnp.float32
    )
    return (query_grad.astype(jnp.bfloat16), key_grad, value_grad)


def solution(mesh):
    in_specs = (
        P(("tgt", "src"), "head"),
        P(("src", "tgt"), "head"),
        P(("src", "tgt"), "head"),
        P(("tgt", "src"), "head"),
        P("tgt"),
        P(),
    )
    out_specs = (P(("tgt", "src"), "head"), P(("src", "tgt"), "head"), P(("src", "tgt"), "head"))
    return jax.shard_map(shards, mesh=mesh, in_specs=in_specs, out_specs=out_specs, check_vma=False)
```

profile of v0, /device:TPU:32, one launch (start us, length us, event | category | flops | bytes accessed | tf_op | source)
XLA Modules:
  0.0 666.5 jit_solution(2388159238601776497)
XLA Ops:
  11.1 37.7 %all-gather.7.cloned.1.call-done = bf16[512,2048]{1,0:T(8,128)(2,1)} async-done(((bf16[64,2048]{1,0:T(8,128)(2,1)}), bf16[512,2048]{1,0:T(8,128)(2,1)}) %all-gather.7.cloned.1.call-update) | async-done | bytes 2097168 | tf_op jit(solution)/shard_map/all_gather | solution.py:211
  48.8 54.6 %all-gather.9.cloned.1.call-done = bf16[512,2048]{1,0:T(8,128)(2,1)} async-done(((bf16[32,2048]{1,0:T(8,128)(2,1)}), bf16[512,2048]{1,0:T(8,128)(2,1)}) %all-gather.9.cloned.1.call-update) | async-done | bytes 2097168 | tf_op jit(solution)/shard_map/all_gather | solution.py:215
  103.4 69.5 %while.69 = (s32[]{:T(128)}, f32[16,512]{1,0:T(8,128)S(1)}, f32[16,512]{1,0:T(8,128)S(1)}, bf16[512,2048]{1,0:T(8,128)(2,1)}, bf16[512,2048]{1,0:T(8,128)(2,1)},...) while((s32[]{:T(128)}, f32[16,512]{1,0:T(8,128)S(1)}, ...), condition=%wide.region_4.5_spmd.clone, body=%wide.region_0.4_spmd.clone.sunk | while | flops 69730320 | bytes 3190021 | solution.py:82
  172.9 14.4 %all-gather.1 = f32[128,512]{1,0:T(8,128)S(1)} all-gather(f32[16,512]{1,0:T(8,128)S(1)} %get-tuple-element.668), channel_id=3, replica_groups=mesh['tgt'=16,'src'=8,'head'=2] {'src'}, dimensions={0}, use_global_device_ids=true | all-gather | bytes 294912 | tf_op jit(solution)/shard_map/all_gather | solution.py:18
  187.3 14.2 %all-gather = f32[128,512]{1,0:T(8,128)S(1)} all-gather(f32[16,512]{1,0:T(8,128)S(1)} %get-tuple-element.667), channel_id=2, replica_groups=mesh['tgt'=16,'src'=8,'head'=2] {'src'}, dimensions={0}, use_global_device_ids=true | all-gather | bytes 294912 | tf_op jit(solution)/shard_map/all_gather | solution.py:18
  202.0 84.9 %while.70 = (s32[]{:T(128)}, f32[16,512]{1,0:T(8,128)S(1)}, bf16[512,2048]{1,0:T(8,128)(2,1)}, bf16[512,2048]{1,0:T(8,128)(2,1)}, f32[16,512]{1,0:T(8,128)S(1)},...) while((s32[]{:T(128)}, f32[16,512]{1,0:T(8,128)S(1)}, ...), condition=%wide.region_10.11_spmd.clone, body=%wide.region_7.10_spmd.clone.sunk | while | flops 136577040 | bytes 3176705 | solution.py:110
  286.9 25.5 %psum.7 = f32[16,512]{1,0:T(8,128)S(1)} all-reduce(f32[16,512]{1,0:T(8,128)S(1)} %get-tuple-element.671), channel_id=1, replica_groups=mesh['tgt'=16,'src'=8,'head'=2] {'src'}, use_global_device_ids=true, to_apply=%region_11.12 | all-reduce | flops 8192 | bytes 65536 | tf_op jit(solution)/shard_map/psum | solution.py:153
  312.7 2.5 broadcast_in_dim.67.clone
  315.2 2.5 broadcast_in_dim.67
  317.6 133.0 %while.71 = (s32[]{:T(128)}, bf16[512,2048]{1,0:T(8,128)(2,1)S(1)}, f32[512,2048]{1,0:T(8,128)}, f32[512,2048]{1,0:T(8,128)}, bf16[512,2048]{1,0:T(8,128)(2,1)},...) while((s32[]{:T(128)}, bf16[512,2048]{1,0:T(8,128)(2,1)S(1)}, ...), condition=%wide.region_13.14_spmd.clone, body=%wide.region_12.13_spmd.clone.sunk | while | flops 338624512 | bytes 6843635 | solution.py:197
  330.3 2.0 convolution_dynamic-update-slice_fusion.2
  338.6 2.0 convolution_dynamic-update-slice_fusion.2
  340.6 2.0 fusion.93
  346.9 2.0 convolution_dynamic-update-slice_fusion.2
  348.9 2.0 fusion.93
  355.2 2.0 convolution_dynamic-update-slice_fusion.2
  357.2 2.0 fusion.93
  380.1 2.0 convolution_dynamic-update-slice_fusion.2
  382.1 2.0 fusion.93
  388.5 2.0 convolution_dynamic-update-slice_fusion.2
  396.8 2.0 convolution_dynamic-update-slice_fusion.2
  398.8 2.0 fusion.93
  405.1 2.0 convolution_dynamic-update-slice_fusion.2
  407.1 2.0 fusion.93
  415.4 2.0 fusion.93
  421.7 2.0 convolution_dynamic-update-slice_fusion.2
  423.7 2.0 fusion.93
  438.4 2.0 convolution_dynamic-update-slice_fusion.2
  446.7 2.0 convolution_dynamic-update-slice_fusion.2
  453.3 80.5 %reduce-scatter.8.cloned.1.call-done = f32[32,2048]{1,0:T(8,128)} async-done(((f32[512,2048]{1,0:T(8,128)}), f32[32,2048]{1,0:T(8,128)}) %reduce-scatter.8.cloned.1.call-update) | async-done | bytes 262160 | tf_op jit(solution)/shard_map/reduce_scatter | solution.py:202
  535.4 84.4 %reduce-scatter.6.cloned.1.call-done = f32[32,2048]{1,0:T(8,128)} async-done(((f32[512,2048]{1,0:T(8,128)}), f32[32,2048]{1,0:T(8,128)}) %reduce-scatter.6.cloned.1.call-update) | async-done | bytes 262160 | tf_op jit(solution)/shard_map/reduce_scatter | solution.py:201
  621.5 38.2 %reduce-scatter.4.cloned.1.call-done = bf16[64,2048]{1,0:T(8,128)(2,1)} async-done(((bf16[512,2048]{1,0:T(8,128)(2,1)}), bf16[64,2048]{1,0:T(8,128)(2,1)}) %reduce-scatter.4.cloned.1.call-update) | async-done | bytes 262160 | tf_op jit(solution)/shard_map/reduce_scatter | solution.py:228
  (406 shorter events, 257.6 us)
Async XLA Ops:
  7.2 41.6 %all-gather.7.cloned.1.call-start = ((), (), s32[]{:S(2)}) async-start(), calls=%async_computation.3 | async-start | bytes 2359296 | tf_op jit(solution)/shard_map/all_gather | solution.py:211
  7.9 95.5 %all-gather.9.cloned.1.call-start = ((), (), s32[]{:S(2)}) async-start(), calls=%async_computation.4 | async-start | bytes 2228224 | tf_op jit(solution)/shard_map/all_gather | solution.py:215
  8.6 193.3 %all-gather.11.cloned.1.call-start = ((), (), s32[]{:S(2)}) async-start(), calls=%async_computation.5 | async-start | bytes 2359296 | tf_op jit(solution)/shard_map/all_gather | solution.py:212
  9.4 192.6 %all-gather.13.cloned.1.call-start = ((), (), s32[]{:S(2)}) async-start(), calls=%async_computation.6 | async-start | bytes 2228224 | tf_op jit(solution)/shard_map/all_gather | solution.py:216
  10.0 523.9 %reduce-scatter.8.cloned.1.call-start = ((), (), s32[]{:S(2)}) async-start(), calls=%async_computation.9 | async-start | bytes 4456448 | tf_op jit(solution)/shard_map/reduce_scatter | solution.py:202
  103.4 3.1 copy-start.1
  107.7 3.1 copy-start.1
  112.1 3.1 copy-start.1
  116.4 3.1 copy-start.1
  120.8 3.1 copy-start.1
  125.1 3.1 copy-start.1
  129.5 3.1 copy-start.1
  133.8 3.1 copy-start.1
  138.2 3.1 copy-start.1
  142.5 3.1 copy-start.1
  146.9 3.1 copy-start.1
  151.2 3.1 copy-start.1
  155.5 3.1 copy-start.1
  159.9 3.1 copy-start.1
  164.2 3.1 copy-start.1
  168.6 3.1 copy-start.1
  315.2 2.5 copy-start.2
  450.6 1.4 copy-start
  452.0 167.9 %reduce-scatter.6.cloned.1.call-start = ((), (), s32[]{:S(2)}) async-start(), calls=%async_computation.8 | async-start | bytes 4456448 | tf_op jit(solution)/shard_map/reduce_scatter | solution.py:201
  452.5 207.2 %reduce-scatter.4.cloned.1.call-start = ((), (), s32[]{:S(2)}) async-start(), calls=%async_computation.7 | async-start | bytes 2359296 | tf_op jit(solution)/shard_map/reduce_scatter | solution.py:228
Sparse Core Ops, SparseCore 0:
  9.8 38.9 all-gather.6
  51.2 52.1 all-gather.8
  105.2 35.7 all-gather.10
  143.3 52.2 all-gather.12
  450.7 83.0 reduce-scatter.7
  537.7 82.0 reduce-scatter.5
  623.0 36.6 reduce-scatter.3
where the time goes:
time: 674 us; the launch traced here: 667 us
  waiting for transfers between devices  299 us (44%)
  matrix products  197 us (29%)
  other arithmetic  78.3 us (12%)
  blocking collectives  54.2 us (8%)
  local copies, waits for them, and re-layouts  20.9 us (3%)
  between operations  14.2 us (2%)
    reduce_scatter x1, waiting for transfers between devices, tiles_layout(): lax.psum_scatter(key_acc, 'tgt', scatter_dimension=0, tiled=True)  84.4 us
    reduce_scatter x1, waiting for transfers between devices, tiles_layout(): lax.psum_scatter(value_acc, 'tgt', scatter_dimension=0, tiled=True)  80.5 us
    dot_general x48, matrix products, head_logits(): lax.dot_general(column(query_rows, head_index), column(key_rows, head_ind...  72.3 us
    another operation x64, other arithmetic  68.5 us
    all_gather x1, waiting for transfers between devices, shards(): lax.all_gather(keys, 'tgt', axis=0, tiled=True)  54.6 us
    dot_general x32, matrix products, grad_probs(): lax.dot_general(column(grad_rows, head_index), column(value_rows, head_in...  41 us
    reduce_scatter x1, waiting for transfers between devices, shards(): lax.psum_scatter(query_part, 'src', scatter_dimension=0, tiled=True)  38.2 us
    all_gather x1, waiting for transfers between devices, shards(): lax.all_gather(queries, 'src', axis=0, tiled=True)  37.7 us
  transfers between devices with their start and end apart: 7, of which 5 were waited for; matrix products, arithmetic and copies ran while one was open for 11% of the time, Pallas kernels for 0%

commit v1 on v0

v1 whole, which is shorter than its diff:
```python
import functools

import jax
import jax.numpy as jnp
from jax import lax
from jax.experimental import pallas as pl
from jax.experimental.pallas import tpu as pltpu
from jax.sharding import PartitionSpec as P

DIM = 128
TILE = 128
CHUNK = 512
TILES = 16
PAIRS = TILES // 2
WIDE = 2 * TILE
ROWS = TILES * TILE
HALF = TILE // 2
MASKED = -1e30
FLOOR = -1e29
SCALE = float(DIM) ** -0.5
LOG2E = 1.4426950408889634
CHUNKS = 4
NT = (((1,), (1,)), ((), ()))
LIMIT = 48 * 1024 * 1024


def dot_nt(a, b):
    return lax.dot_general(a, b, NT, preferred_element_type=jnp.float32)


def dot_nn(a, b):
    return jnp.dot(a, b, preferred_element_type=jnp.float32)


def pair_rows(own, other, pair, low):
    parts = []
    for half in range(2):
        for ref in (own, other):
            parts.append(ref[2 * pair + half, low : low + HALF, :])
    return jnp.concatenate(parts, axis=0)


def sub_rows(kv, j, low):
    return kv[4 * j : 4 * j + 4, low : low + 32, :].reshape(TILE, DIM)


def masked_scores(kv, lim, chunk, j, x, lanes, steps):
    scores = dot_nt(sub_rows(kv, j, 0), x) * (SCALE * LOG2E)
    return jnp.where(steps < lim[4 * chunk + j, lanes][None, :], scores, MASKED)


def stats_kernel(first, lim, own, other, kv0, kv1, kv2, kv3, out):
    kvs = (kv0, kv1, kv2, kv3)
    steps = lax.broadcasted_iota(jnp.int32, (TILE, WIDE), 0)
    out[...] = jnp.zeros_like(out)
    out[0:1, :] = jnp.full((1, ROWS), MASKED, jnp.float32)
    for chunk in range(CHUNKS):
        kv = kvs[chunk]

        def unit(pair, carry):
            lanes = pl.ds(pl.multiple_of(pair * WIDE, WIDE), WIDE)
            x = pair_rows(own, other, pair, 0)
            g = pair_rows(own, other, pair, HALF)
            scores = [masked_scores(kv, lim, chunk, j, x, lanes, steps) for j in range(4)]
            top = functools.reduce(jnp.maximum, scores).max(axis=0, keepdims=True)
            old = out[0:1, lanes]
            high = jnp.maximum(old, top)
            base = jnp.maximum(high, FLOOR)
            total = jnp.zeros((1, WIDE), jnp.float32)
            mixed = jnp.zeros((1, WIDE), jnp.float32)
            for j in range(4):
                weights = jnp.exp2(scores[j] - base)
                prods = dot_nt(sub_rows(kv, j, 32), g)
                total += weights.sum(axis=0, keepdims=True)
                mixed += (weights * prods).sum(axis=0, keepdims=True)
            fade = jnp.exp2(old - high)
            out[0:1, lanes] = high
            out[1:2, lanes] = out[1:2, lanes] * fade + total
            out[2:3, lanes] = out[2:3, lanes] * fade + mixed
            return carry

        lax.fori_loop(first[chunk], PAIRS, unit, 0)


def grads_kernel(chunks, start, end, *refs):
    first, lim, own, other, mine, theirs = refs[:6]
    refs = refs[6:]
    kvs, refs = refs[: len(chunks)], refs[len(chunks) :]
    if not start:
        query_in, refs = refs[0], refs[1:]
    outs, refs = refs[: len(chunks)], refs[len(chunks) :]
    if end:
        keep, send, query_acc, refs = refs[0], refs[1], refs[2], refs[3:]
    else:
        query_acc, refs = refs[0], refs[1:]
    shift, delta, key_acc, value_acc, key_t = refs
    steps = lax.broadcasted_iota(jnp.int32, (TILE, WIDE), 0)
    for tile in range(TILES):
        lanes = slice(tile * TILE, (tile + 1) * TILE)
        a = mine[:, lanes]
        b = pltpu.roll(theirs[:, lanes], HALF, 1)
        high = jnp.maximum(a[0:1], b[0:1])
        wa = jnp.exp2(a[0:1] - high)
        wb = jnp.exp2(b[0:1] - high)
        total = a[1:2] * wa + b[1:2] * wb
        mixed = a[2:3] * wa + b[2:3] * wb
        shift[0:1, lanes] = high + jnp.log2(total)
        delta[0:1, lanes] = mixed / total
    if start:
        query_acc[...] = jnp.zeros_like(query_acc)
    else:
        query_acc[...] = query_in[...]
    for index, chunk in enumerate(chunks):
        kv = kvs[index]
        for j in range(4):
            block = sub_rows(kv, j, 0).astype(jnp.float32)
            key_t[:, j * TILE : (j + 1) * TILE] = block.T.astype(jnp.bfloat16)
        key_acc[...] = jnp.zeros_like(key_acc)
        value_acc[...] = jnp.zeros_like(value_acc)

        def unit(pair, carry):
            lanes = pl.ds(pl.multiple_of(pair * WIDE, WIDE), WIDE)
            x = pair_rows(own, other, pair, 0)
            g = pair_rows(own, other, pair, HALF)
            base = shift[0:1, lanes]
            center = delta[0:1, lanes]
            lows = []
            for j in range(4):
                rows = slice(j * TILE, (j + 1) * TILE)
                scores = masked_scores(kv, lim, chunk, j, x, lanes, steps)
                probs = jnp.exp2(scores - base)
                prods = dot_nt(sub_rows(kv, j, 32), g)
                low = (probs * (prods - center)).astype(jnp.bfloat16)
                value_acc[rows, :] += dot_nn(probs.astype(jnp.bfloat16), g)
                key_acc[rows, :] += dot_nn(low, x)
                lows.append(low)
            query_acc[:, lanes] += dot_nn(key_t[...], jnp.concatenate(lows, axis=0))
            return carry

        lax.fori_loop(first[chunk], PAIRS, unit, 0)
        out = outs[index]
        out[:, 0:32, :] = (key_acc[...] * SCALE).astype(jnp.bfloat16).reshape(TILES, 32, DIM)
        out[:, 32:64, :] = value_acc[...].astype(jnp.bfloat16).reshape(TILES, 32, DIM)
    if end:
        for tile in range(TILES):
            block = query_acc[:, tile * TILE : (tile + 1) * TILE].T * SCALE
            keep[tile] = block[0:HALF]
            send[tile] = block[HALF:TILE].astype(jnp.bfloat16)


SMEM = pl.BlockSpec(memory_space=pltpu.SMEM)
VMEM = pl.BlockSpec(memory_space=pltpu.VMEM)
PARAMS = pltpu.CompilerParams(vmem_limit_bytes=LIMIT)


def cost(units, dots):
    flops = units * dots * 2 * CHUNK * WIDE * DIM
    return pl.CostEstimate(flops=flops, bytes_accessed=4 * 2**20, transcendentals=units * CHUNK * WIDE)


def row_stats(first, lim, own, other, kvs):
    return pl.pallas_call(
        stats_kernel,
        out_shape=jax.ShapeDtypeStruct((8, ROWS), jnp.float32),
        in_specs=[SMEM] + [VMEM] * 7,
        out_specs=VMEM,
        compiler_params=PARAMS,
        cost_estimate=cost(20, 4),
        name="stats",
    )(first, lim, own, other, *kvs)


def chunk_grads(chunks, start, end, first, lim, own, other, mine, theirs, kvs, query_in):
    piece = jax.ShapeDtypeStruct((TILES, 64, DIM), jnp.bfloat16)
    shapes = [piece] * len(chunks)
    scratch = [
        pltpu.VMEM((8, ROWS), jnp.float32),
        pltpu.VMEM((8, ROWS), jnp.float32),
        pltpu.VMEM((CHUNK, DIM), jnp.float32),
        pltpu.VMEM((CHUNK, DIM), jnp.float32),
        pltpu.VMEM((DIM, CHUNK), jnp.bfloat16),
    ]
    accumulator = (DIM, ROWS)
    if end:
        shapes += [jax.ShapeDtypeStruct((TILES, HALF, DIM), jnp.float32), piece]
        scratch = [pltpu.VMEM(accumulator, jnp.float32)] + scratch
    else:
        shapes += [jax.ShapeDtypeStruct(accumulator, jnp.float32)]
    operands = [first, lim, own, other, mine, theirs] + [kvs[c] for c in chunks]
    if not start:
        operands.append(query_in)
    return pl.pallas_call(
        functools.partial(grads_kernel, chunks, start, end),
        out_shape=shapes,
        in_specs=[SMEM] + [VMEM] * (len(operands) - 1),
        out_specs=[VMEM] * len(shapes),
        scratch_shapes=scratch,
        compiler_params=PARAMS,
        cost_estimate=cost(5 * len(chunks), 5),
        name="grads",
    )(*operands)


def shards(queries, keys, values, out_grad, read_points, block_mask):
    place = lax.axis_index("src")
    level, core = place // 2, place % 2

    def swap(a, mask):
        return lax.ppermute(a, "src", [(i, i ^ mask) for i in range(8)])

    def by_head(a):
        return lax.all_to_all(a, "tgt", 1, 0, tiled=True).reshape(TILES, a.shape[0], DIM)

    kv = by_head(jnp.concatenate([keys, values], axis=0))
    reads = lax.dynamic_slice_in_dim(read_points, level * TILE, TILE)
    digits = jnp.stack([reads // 64, reads % 64]).astype(jnp.bfloat16)
    digits = jnp.pad(jnp.tile(digits, (1, TILES)), ((0, 14), (0, 0)))
    packed = jnp.concatenate([queries, out_grad, digits], axis=0)
    packed, kv = lax.optimization_barrier((packed, kv))
    kvs = [kv] + [swap(kv, 2 * k) for k in range(1, CHUNKS)]
    own = by_head(packed)
    other = swap(own, 1)

    reads = own[:, 2 * HALF, :].astype(jnp.int32) * 64 + own[:, 2 * HALF + 1, :].astype(jnp.int32)
    owners = jnp.stack([level ^ k for k in range(CHUNKS)])
    starts = (owners * 2 + core) * CHUNK
    first = jnp.sum(reads[1::2, -1][None, :] <= starts[:, None], axis=1).astype(jnp.int32)
    ordered = jnp.where(core == 0, reads, jnp.roll(reads, HALF, axis=1))
    flags = block_mask.reshape(TILES, CHUNKS, CHUNKS, 2, 4)
    flags = lax.dynamic_index_in_dim(flags, level, 1, False)
    flags = lax.dynamic_index_in_dim(flags, core, 2, False)
    flags = jnp.stack([lax.dynamic_index_in_dim(flags, level ^ k, 1, False) for k in range(CHUNKS)])
    flags = flags.transpose(0, 2, 1)
    begins = starts[:, None] + TILE * jnp.arange(4, dtype=jnp.int32)[None, :]
    lim = jnp.where(flags[..., None] == 1, ordered[None, None], 0) - begins[:, :, None, None]
    lim = lim.reshape(TILES, ROWS)

    mine = row_stats(first, lim, own, other, kvs)
    theirs = swap(mine, 1)
    common = (first, lim, own, other, mine, theirs, kvs)
    part3, query_acc = chunk_grads((3,), True, False, *common, None)
    got3 = swap(part3, 6)
    part2, query_acc = chunk_grads((2,), False, False, *common, query_acc)
    got2 = swap(part2, 4)
    part1, part0, keep, send = chunk_grads((1, 0), False, True, *common, query_acc)
    got1 = swap(part1, 2)
    query = keep + swap(send, 1).astype(jnp.float32)
    sums = functools.reduce(jnp.add, [p.astype(jnp.float32) for p in (part0, got1, got2, got3)])
    result = jnp.concatenate([query, sums], axis=1).astype(jnp.bfloat16)
    result = lax.all_to_all(result, "tgt", 0, 0, tiled=True)
    result = result.transpose(1, 0, 2).reshape(128, TILES * DIM)
    return result[0:64], result[64:96], result[96:128]


def solution(mesh):
    in_specs = (
        P(("tgt", "src"), "head"),
        P(("src", "tgt"), "head"),
        P(("src", "tgt"), "head"),
        P(("tgt", "src"), "head"),
        P("tgt"),
        P(),
    )
    out_specs = (P(("tgt", "src"), "head"), P(("src", "tgt"), "head"), P(("src", "tgt"), "head"))
    return jax.shard_map(shards, mesh=mesh, in_specs=in_specs, out_specs=out_specs, check_vma=False)
```

time: 674 us -> 126 us (0.19); the launches traced: 667 us -> 126 us
  waiting for transfers between devices: 299 us -> 49.8 us
  matrix products: 197 us -> 0 us
  other arithmetic: 78.3 us -> 3.49 us
  blocking collectives: 54.2 us -> 18 us
  Pallas kernels: 0 us -> 29.1 us
  starting transfers between devices: 0.23 us -> 21 us
  local copies, waits for them, and re-layouts: 20.9 us -> 3.53 us
  between operations: 14.2 us -> 0.92 us
    reduce_scatter x3 -> x0, waiting for transfers between devices: 203 us -> none  [the longest x1 84.4 us: tiles_layout(): lax.psum_scatter(key_acc, 'tgt', scatter_dimension=0, tiled=True)]
    dot_general x128 -> x0, matrix products: 197 us -> none  [the longest x48 72.3 us: head_logits(): lax.dot_general(column(query_rows, head_index), column(key_rows, head_ind...]
    all_gather x4 -> x0, waiting for transfers between devices: 92.4 us -> none  [the longest x1 54.6 us: shards(): lax.all_gather(keys, 'tgt', axis=0, tiled=True)]
    another operation x64 -> x5, other arithmetic: 68.5 us -> 1.02 us  [the longest x3 0.79 us: shards(): digits = jnp.stack([reads // 64, reads % 64]).astype(jnp.bfloat16)]
    ppermute x0 -> x9, waiting for transfers between devices: none -> 36.8 us  [swap(): return lax.ppermute(a, 'src', [(i, i ^ mask) for i in range(8)])]
    pallas_call x0 -> x4, Pallas kernels: none -> 29.1 us  [the longest x3 20.9 us: chunk_grads(): pl.pallas_call(functools.partial(grads_kernel, chunks, start, end), out_s...]
    all_gather x2 -> x0, blocking collectives: 28.6 us -> none  [combined_all(): gathered = jax.tree.map(lambda a: lax.all_gather(a, axis), part)]
    psum x1 -> x0, blocking collectives: 25.5 us -> none  [row_statistics(): delta_rows = lax.psum(delta_of(highest, totals), 'src')]
  transfers between devices with their start and end apart: 7 -> 11, of which waited for: 5 -> 8; matrix products, arithmetic and copies ran while one was open for 11% -> 2% of each run, Pallas kernels for 0% -> 0%
where the time goes in v1:
time: 126 us
  waiting for transfers between devices  49.8 us (40%)
  Pallas kernels  29.1 us (23%)
  starting transfers between devices  21 us (17%)
  blocking collectives  18 us (14%)
  local copies, waits for them, and re-layouts  3.53 us (3%)
  other arithmetic  3.49 us (3%)
    ppermute x9, waiting for transfers between devices, swap(): return lax.ppermute(a, 'src', [(i, i ^ mask) for i in range(8)])  36.8 us
    pallas_call x3, Pallas kernels, chunk_grads(): pl.pallas_call(functools.partial(grads_kernel, chunks, start, end), out_s...  20.9 us
    all_to_all x1, blocking collectives, shards(): result = lax.all_to_all(result, 'tgt', 0, 0, tiled=True)  18 us
    all_to_all x2, waiting for transfers between devices, by_head(): lax.all_to_all(a, 'tgt', 1, 0, tiled=True).reshape(TILES, a.shape[0], DIM)  13 us
    all_to_all x2, starting transfers between devices, by_head(): lax.all_to_all(a, 'tgt', 1, 0, tiled=True).reshape(TILES, a.shape[0], DIM)  10.6 us
    ppermute x9, starting transfers between devices, swap(): return lax.ppermute(a, 'src', [(i, i ^ mask) for i in range(8)])  10.4 us
    pallas_call x1, Pallas kernels, row_stats(): pl.pallas_call(stats_kernel, out_shape=jax.ShapeDtypeStruct((8, ROWS), jn...  8.12 us
  transfers between devices with their start and end apart: 11, of which 8 were waited for; matrix products, arithmetic and copies ran while one was open for 2% of the time, Pallas kernels for 0%

profile of v1, /device:TPU:32, one launch (start us, length us, event | category | flops | bytes accessed | tf_op | source)
XLA Modules:
  0.0 125.7 jit_solution(5226228439787497575)
XLA Ops:
  0.7 1.8 %copy_bitcast_fusion.2 = bf16[64,16,128]{2,0,1:T(8,128)(2,1)} fusion(bf16[32,2048]{1,0:T(8,128)(2,1)} %param.8, bf16[32,2048]{1,0:T(8,128)(2,1)} %param.7), kind=kLoop, calls=%fused_computation.8 | loop fusion | flops 524288 | bytes 524288 | tf_op jit(solution)/shard_map/all_to_all | solution.py:212
  2.4 7.0 %all-to-all-start = ((bf16[64,16,128]{2,0,1:T(8,128)(2,1)}), bf16[64,16,128]{2,0,1:T(8,128)(2,1)S(1)}, u32[]{:S(2)}, u32[]{:S(2)}) async-start(bf16[64,16,128]{2,0,1:T(8,128)(2,1)} %copy_bitcast_fusion.2), calls=%async_computation | async-start | bytes 524288 | tf_op jit(solution)/shard_map/all_to_all | solution.py:212
  9.5 0.8 convert_bitcast_fusion
  10.4 7.8 %all-to-all-done = bf16[64,16,128]{2,0,1:T(8,128)(2,1)S(1)} async-done(((bf16[64,16,128]{2,0,1:T(8,128)(2,1)}), bf16[64,16,128]{2,0,1:T(8,128)(2,1)S(1)}, u32[]{:S(2)}, u32[]{:S(2)}) %all-to-all-start) | async-done | bytes 262176 | tf_op jit(solution)/shard_map/all_to_all | solution.py:212
  18.2 0.9 copy_bitcast_fusion
  19.1 3.6 %all-to-all-start.1 = ((bf16[144,16,128]{2,0,1:T(8,128)(2,1)}), bf16[144,16,128]{2,0,1:T(8,128)(2,1)S(1)}, u32[]{:S(2)}, u32[]{:S(2)}) async-start(bf16[144,16,128]{2,0,1:T(8,128)(2,1)} %copy_bitcast_fusion), calls=%async_computation.1 | async-start | bytes 1179648 | tf_op jit(solution)/shard_map/all_to_all | solution.py:212
  23.1 0.2 reshape.165
  23.3 0.5 dynamic-slice_reduce_fusion.3
  23.7 2.0 %collective-permute-start.3 = (bf16[16,64,128]{2,1,0:T(8,128)(2,1)S(1)}, bf16[16,64,128]{2,1,0:T(8,128)(2,1)S(1)}, u32[]{:S(2)}, u32[]{:S(2)}) collective-permute-start(bf16[16,64,128]{2,1,0:T(8,128)(2,1)S(1)} %bitcast.69), channel_id=1, source_target_pairs={{0,12},{2,14},{4,8},{6,10},{8,4},{10,6},{12,0},{14,2},{1,13},{3,15... | collective-permute-start | bytes 786440 | tf_op jit(solution)/shard_map/ppermute | solution.py:209
  25.8 1.5 %collective-permute-start.2 = (bf16[16,64,128]{2,1,0:T(8,128)(2,1)S(1)}, bf16[16,64,128]{2,1,0:T(8,128)(2,1)S(1)}, u32[]{:S(2)}, u32[]{:S(2)}) collective-permute-start(bf16[16,64,128]{2,1,0:T(8,128)(2,1)S(1)} %bitcast.70), channel_id=1, source_target_pairs={{0,8},{2,10},{4,12},{6,14},{8,0},{10,2},{12,4},{14,6},{1,9},{3,11}... | collective-permute-start | bytes 786440 | tf_op jit(solution)/shard_map/ppermute | solution.py:209
  27.2 1.4 %collective-permute-start.1 = (bf16[16,64,128]{2,1,0:T(8,128)(2,1)S(1)}, bf16[16,64,128]{2,1,0:T(8,128)(2,1)S(1)}, u32[]{:S(2)}, u32[]{:S(2)}) collective-permute-start(bf16[16,64,128]{2,1,0:T(8,128)(2,1)S(1)} %bitcast.71), channel_id=1, source_target_pairs={{0,4},{2,6},{4,0},{6,2},{8,12},{10,14},{12,8},{14,10},{1,5},{3,7},... | collective-permute-start | bytes 786440 | tf_op jit(solution)/shard_map/ppermute | solution.py:209
  28.6 5.2 %all-to-all-done.1 = bf16[144,16,128]{2,0,1:T(8,128)(2,1)S(1)} async-done(((bf16[144,16,128]{2,0,1:T(8,128)(2,1)}), bf16[144,16,128]{2,0,1:T(8,128)(2,1)S(1)}, u32[]{:S(2)}, u32[]{:S(2)}) %all-to-all-start.1) | async-done | bytes 589856 | tf_op jit(solution)/shard_map/all_to_all | solution.py:212
  34.1 0.1 broadcast_in_dim.28
  34.3 0.1 reduce
  34.5 0.2 convert_reduce_fusion.first.refs_0_
  34.7 8.9 %collective-permute-done.3.kv3.refs_6_ = bf16[16,64,128]{2,1,0:T(8,128)(2,1)S(1)} collective-permute-done((bf16[16,64,128]{2,1,0:T(8,128)(2,1)S(1)}, bf16[16,64,128]{2,1,0:T(8,128)(2,1)S(1)}, u32[]{:S(2)}, u32[]{:S(2)}) %collective-permute-start.3) | collective-permute-done | bytes 262176 | tf_op jit(solution)/shard_map/ppermute | solution.py:209
  43.5 3.2 %collective-permute-done.2.kv2.refs_6_ = bf16[16,64,128]{2,1,0:T(8,128)(2,1)S(1)} collective-permute-done((bf16[16,64,128]{2,1,0:T(8,128)(2,1)S(1)}, bf16[16,64,128]{2,1,0:T(8,128)(2,1)S(1)}, u32[]{:S(2)}, u32[]{:S(2)}) %collective-permute-start.2) | collective-permute-done | bytes 262176 | tf_op jit(solution)/shard_map/ppermute | solution.py:209
  46.7 8.1 %stats.1.refs_4_ = f32[8,2048]{1,0:T(8,128)S(1)} custom-call(s32[4]{0:T(128)S(1)} %convert_reduce_fusion.first.refs_0_, s32[16,2048]{1,0:T(8,128)S(1)} %select_subtract_fusion.lim.refs_1_, bf16[16,144,128]{2,1,0:T(8,128)(2,1)S(1)} %bitcast.65, bf16[16,144,128]{2,1,0:T(8,128)(2,1)S(1)} %collective-permute-done.other.refs_3_, ...), custom_call_target="tpu_custom_call" | custom-call | flops 2684354560 | bytes 4194304 | tf_op jit(solution)/shard_map/stats/pallas_call | solution.py:162
  55.0 1.2 collective-permute-done.4.refs_5_
  56.2 4.4 %grads.3 = (bf16[16,64,128]{2,1,0:T(8,128)(2,1)S(1)}, f32[128,2048]{1,0:T(8,128)S(1)}) custom-call(s32[4]{0:T(128)S(1)} %convert_reduce_fusion.first.refs_0_, s32[16,2048]{1,0:T(8,128)S(1)} %select_subtract_fusion.lim.refs_1_, bf16[16,144,128]{2,1,0:T(8,128)(2,1)S(1)} %bitcast.66, bf16[16,144,128]{2,1,0:T(8,128)(2,1)S(1)} %collective-permute-done.other.refs_3_, ...), custom_call_target="tpu_custom_call" | custom-call | flops 838860800 | bytes 4194304 | tf_op jit(solution)/shard_map/grads/pallas_call | solution.py:192
  60.6 2.6 %grads.4 = (bf16[16,64,128]{2,1,0:T(8,128)(2,1)S(1)}, f32[128,2048]{1,0:T(8,128)S(1)}) custom-call(s32[4]{0:T(128)S(1)} %convert_reduce_fusion.first.refs_0_, s32[16,2048]{1,0:T(8,128)S(1)} %select_subtract_fusion.lim.refs_1_, bf16[16,144,128]{2,1,0:T(8,128)(2,1)S(1)} %bitcast.67, bf16[16,144,128]{2,1,0:T(8,128)(2,1)S(1)} %collective-permute-done.other.refs_3_, ...), custom_call_target="tpu_custom_call" | custom-call | flops 838860800 | bytes 4194304 | tf_op jit(solution)/shard_map/grads/pallas_call | solution.py:192
  63.2 13.9 %grads.5 = (bf16[16,64,128]{2,1,0:T(8,128)(2,1)S(1)}, bf16[16,64,128]{2,1,0:T(8,128)(2,1)S(1)}, f32[16,64,128]{2,1,0:T(8,128)S(1)}, bf16[16,64,128]{2,1,0:T(8,128)(2,1)S(1)}) custom-call(s32[4]{0:T(128)S(1)} %convert_reduce_fusion.first.refs_0_, s32[16,2048]{1,0:T(8,128)S(1)} %select_subtract_fusion.lim.refs_1_, bf16[16,144,128]{2,1,0:T(8,128)(2,1)S(1)} %bitcast.68, ...), custom_call_target="tpu_custom_call" | custom-call | flops 1677721600 | bytes 4194304 | tf_op jit(solution)/shard_map/grads/pallas_call | solution.py:192
  77.3 2.3 %collective-permute-start.6 = (bf16[16,64,128]{2,1,0:T(8,128)(2,1)S(1)}, bf16[16,64,128]{2,1,0:T(8,128)(2,1)S(1)}, u32[]{:S(2)}, u32[]{:S(2)}) collective-permute-start(bf16[16,64,128]{2,1,0:T(8,128)(2,1)S(1)} %get-tuple-element.20), channel_id=1, source_target_pairs={{0,4},{2,6},{4,0},{6,2},{8,12},{10,14},{12,8},{14,10},{1,5},{3,7},... | collective-permute-start | bytes 786440 | tf_op jit(solution)/shard_map/ppermute | solution.py:209
  79.6 2.5 %collective-permute-start.7 = (bf16[16,64,128]{2,1,0:T(8,128)(2,1)S(1)}, bf16[16,64,128]{2,1,0:T(8,128)(2,1)S(1)}, u32[]{:S(2)}, u32[]{:S(2)}) collective-permute-start(bf16[16,64,128]{2,1,0:T(8,128)(2,1)S(1)} %get-tuple-element.21), channel_id=1, source_target_pairs={{0,8},{2,10},{4,12},{6,14},{8,0},{10,2},{12,4},{14,6},{1,9},{3,11}... | collective-permute-start | bytes 786440 | tf_op jit(solution)/shard_map/ppermute | solution.py:209
  82.1 0.5 collective-permute-start.8
  82.6 8.3 %collective-permute-done.6 = bf16[16,64,128]{2,1,0:T(8,128)(2,1)S(1)} collective-permute-done((bf16[16,64,128]{2,1,0:T(8,128)(2,1)S(1)}, bf16[16,64,128]{2,1,0:T(8,128)(2,1)S(1)}, u32[]{:S(2)}, u32[]{:S(2)}) %collective-permute-start.6) | collective-permute-done | bytes 262176 | tf_op jit(solution)/shard_map/ppermute | solution.py:209
  91.0 9.1 %collective-permute-done.7 = bf16[16,64,128]{2,1,0:T(8,128)(2,1)S(1)} collective-permute-done((bf16[16,64,128]{2,1,0:T(8,128)(2,1)S(1)}, bf16[16,64,128]{2,1,0:T(8,128)(2,1)S(1)}, u32[]{:S(2)}, u32[]{:S(2)}) %collective-permute-start.7) | collective-permute-done | bytes 262176 | tf_op jit(solution)/shard_map/ppermute | solution.py:209
  100.0 6.0 %collective-permute-done.8 = bf16[16,64,128]{2,1,0:T(8,128)(2,1)S(1)} collective-permute-done((bf16[16,64,128]{2,1,0:T(8,128)(2,1)S(1)}, bf16[16,64,128]{2,1,0:T(8,128)(2,1)S(1)}, u32[]{:S(2)}, u32[]{:S(2)}) %collective-permute-start.8) | collective-permute-done | bytes 262176 | tf_op jit(solution)/shard_map/ppermute | solution.py:209
  106.1 0.2 add_convert_fusion
  106.3 18.0 %all_to_all.37 = bf16[16,128,128]{2,1,0:T(8,128)(2,1)S(1)} all-to-all(bf16[16,128,128]{2,1,0:T(8,128)(2,1)S(1)} %pad_maximum_fusion), channel_id=1, replica_groups=mesh['tgt'=16,'src'=8,'head'=2] {'tgt'}, dimensions={0} | all-to-all | bytes 1048576 | tf_op jit(solution)/shard_map/all_to_all | solution.py:250
  124.3 0.7 copy_bitcast_fusion.1
  125.0 0.7 copy_bitcast_fusion.3
  (33 shorter events, 1.2 us)
Async XLA Ops:
  0.6 9.7 %copy-start = (bf16[64,2048]{1,0:T(8,128)(2,1)S(1)}, bf16[64,2048]{1,0:T(8,128)(2,1)}, u32[]{:S(2)}) copy-start(bf16[64,2048]{1,0:T(8,128)(2,1)} %param.9) | copy-start | bytes 786436
  0.6 9.7 %copy-start.1 = (bf16[64,2048]{1,0:T(8,128)(2,1)S(1)}, bf16[64,2048]{1,0:T(8,128)(2,1)}, u32[]{:S(2)}) copy-start(bf16[64,2048]{1,0:T(8,128)(2,1)} %param.6) | copy-start | bytes 786436
  2.4 15.7 %all-to-all-start = ((bf16[64,16,128]{2,0,1:T(8,128)(2,1)}), bf16[64,16,128]{2,0,1:T(8,128)(2,1)S(1)}, u32[]{:S(2)}, u32[]{:S(2)}) async-start(bf16[64,16,128]{2,0,1:T(8,128)(2,1)} %copy_bitcast_fusion.2), calls=%async_computation | async-start | bytes 524288 | tf_op jit(solution)/shard_map/all_to_all | solution.py:212
  18.2 4.9 %copy-start.2 = (s32[64,32]{0,1:T(8,128)S(1)}, s32[64,32]{0,1:T(8,128)}, u32[]{:S(2)}) copy-start(s32[64,32]{0,1:T(8,128)} %param.11) | copy-start | bytes 24580
  19.1 14.7 %all-to-all-start.1 = ((bf16[144,16,128]{2,0,1:T(8,128)(2,1)}), bf16[144,16,128]{2,0,1:T(8,128)(2,1)S(1)}, u32[]{:S(2)}, u32[]{:S(2)}) async-start(bf16[144,16,128]{2,0,1:T(8,128)(2,1)} %copy_bitcast_fusion), calls=%async_computation.1 | async-start | bytes 1179648 | tf_op jit(solution)/shard_map/all_to_all | solution.py:212
  23.7 19.8 %collective-permute-start.3 = (bf16[16,64,128]{2,1,0:T(8,128)(2,1)S(1)}, bf16[16,64,128]{2,1,0:T(8,128)(2,1)S(1)}, u32[]{:S(2)}, u32[]{:S(2)}) collective-permute-start(bf16[16,64,128]{2,1,0:T(8,128)(2,1)S(1)} %bitcast.69), channel_id=1, source_target_pairs={{0,12},{2,14},{4,8},{6,10},{8,4},{10,6},{12,0},{14,2},{1,13},{3,15... | collective-permute-start | bytes 786440 | tf_op jit(solution)/shard_map/ppermute | solution.py:209
  25.8 21.0 %collective-permute-start.2 = (bf16[16,64,128]{2,1,0:T(8,128)(2,1)S(1)}, bf16[16,64,128]{2,1,0:T(8,128)(2,1)S(1)}, u32[]{:S(2)}, u32[]{:S(2)}) collective-permute-start(bf16[16,64,128]{2,1,0:T(8,128)(2,1)S(1)} %bitcast.70), channel_id=1, source_target_pairs={{0,8},{2,10},{4,12},{6,14},{8,0},{10,2},{12,4},{14,6},{1,9},{3,11}... | collective-permute-start | bytes 786440 | tf_op jit(solution)/shard_map/ppermute | solution.py:209
  27.2 19.5 %collective-permute-start.1 = (bf16[16,64,128]{2,1,0:T(8,128)(2,1)S(1)}, bf16[16,64,128]{2,1,0:T(8,128)(2,1)S(1)}, u32[]{:S(2)}, u32[]{:S(2)}) collective-permute-start(bf16[16,64,128]{2,1,0:T(8,128)(2,1)S(1)} %bitcast.71), channel_id=1, source_target_pairs={{0,4},{2,6},{4,0},{6,2},{8,12},{10,14},{12,8},{14,10},{1,5},{3,7},... | collective-permute-start | bytes 786440 | tf_op jit(solution)/shard_map/ppermute | solution.py:209
  33.8 12.9 %collective-permute-start = (bf16[16,144,128]{2,1,0:T(8,128)(2,1)S(1)}, bf16[16,144,128]{2,1,0:T(8,128)(2,1)S(1)}, u32[]{:S(2)}, u32[]{:S(2)}) collective-permute-start(bf16[16,144,128]{2,1,0:T(8,128)(2,1)S(1)} %bitcast.64), channel_id=1, source_target_pairs={{0,2},{2,0},{4,6},{6,4},{8,10},{10,8},{12,14},{14,12},{1,3},{3,1},... | collective-permute-start | bytes 1769480 | tf_op jit(solution)/shard_map/ppermute | solution.py:209
  54.9 1.3 %collective-permute-start.4 = (f32[8,2048]{1,0:T(8,128)S(1)}, f32[8,2048]{1,0:T(8,128)S(1)}, u32[]{:S(2)}, u32[]{:S(2)}) collective-permute-start(f32[8,2048]{1,0:T(8,128)S(1)} %stats.1.refs_4_), channel_id=1, source_target_pairs={{0,2},{2,0},{4,6},{6,4},{8,10},{10,8},{12,14},{14,12},{1,3},{3,1},... | collective-permute-start | bytes 196616 | tf_op jit(solution)/shard_map/ppermute | solution.py:209
  77.2 5.4 %collective-permute-start.5 = (bf16[16,64,128]{2,1,0:T(8,128)(2,1)S(1)}, bf16[16,64,128]{2,1,0:T(8,128)(2,1)S(1)}, u32[]{:S(2)}, u32[]{:S(2)}) collective-permute-start(bf16[16,64,128]{2,1,0:T(8,128)(2,1)S(1)} %get-tuple-element.18), channel_id=1, source_target_pairs={{0,2},{2,0},{4,6},{6,4},{8,10},{10,8},{12,14},{14,12},{1,3},{3,1},... | collective-permute-start | bytes 786440 | tf_op jit(solution)/shard_map/ppermute | solution.py:209
  77.3 13.7 %collective-permute-start.6 = (bf16[16,64,128]{2,1,0:T(8,128)(2,1)S(1)}, bf16[16,64,128]{2,1,0:T(8,128)(2,1)S(1)}, u32[]{:S(2)}, u32[]{:S(2)}) collective-permute-start(bf16[16,64,128]{2,1,0:T(8,128)(2,1)S(1)} %get-tuple-element.20), channel_id=1, source_target_pairs={{0,4},{2,6},{4,0},{6,2},{8,12},{10,14},{12,8},{14,10},{1,5},{3,7},... | collective-permute-start | bytes 786440 | tf_op jit(solution)/shard_map/ppermute | solution.py:209
  79.6 20.5 %collective-permute-start.7 = (bf16[16,64,128]{2,1,0:T(8,128)(2,1)S(1)}, bf16[16,64,128]{2,1,0:T(8,128)(2,1)S(1)}, u32[]{:S(2)}, u32[]{:S(2)}) collective-permute-start(bf16[16,64,128]{2,1,0:T(8,128)(2,1)S(1)} %get-tuple-element.21), channel_id=1, source_target_pairs={{0,8},{2,10},{4,12},{6,14},{8,0},{10,2},{12,4},{14,6},{1,9},{3,11}... | collective-permute-start | bytes 786440 | tf_op jit(solution)/shard_map/ppermute | solution.py:209
  82.1 24.0 %collective-permute-start.8 = (bf16[16,64,128]{2,1,0:T(8,128)(2,1)S(1)}, bf16[16,64,128]{2,1,0:T(8,128)(2,1)S(1)}, u32[]{:S(2)}, u32[]{:S(2)}) collective-permute-start(bf16[16,64,128]{2,1,0:T(8,128)(2,1)S(1)} %get-tuple-element.22), channel_id=1, source_target_pairs={{0,12},{2,14},{4,8},{6,10},{8,4},{10,6},{12,0},{14,2},{1,13},{3,15... | collective-permute-start | bytes 786440 | tf_op jit(solution)/shard_map/ppermute | solution.py:209

commit v2 on v1

v2 whole, which is shorter than its diff:
```python
import functools

import jax
import jax.numpy as jnp
from jax import lax
from jax.experimental import pallas as pl
from jax.experimental.pallas import tpu as pltpu
from jax.sharding import PartitionSpec as P

DIM = 128
TILE = 128
SIDE = 4
TILES = SIDE * SIDE
WIDE = SIDE * TILE
ROWS = TILES * TILE
HALF = TILE // 2
PIECE = 32
QUERY = 0
GRAD = QUERY + HALF
DIGIT = GRAD + HALF
PACKED = DIGIT + 16
MASKED = -1e30
FLOOR = -1e29
SCALE = float(DIM) ** -0.5
LOG2E = 1.4426950408889634
LIMIT = 32 * 1024 * 1024


def dot(a, b, left, right):
    dims = (((left,), (right,)), ((), ()))
    return lax.dot_general(a, b, dims, preferred_element_type=jnp.float32)


def unit_rows(own, other, unit, low):
    parts = []
    for level in range(SIDE):
        for ref in (own, other):
            parts.append(ref[SIDE * level + unit, low : low + HALF, :])
    return jnp.concatenate(parts, axis=0)


def source_rows(kvs, level, low):
    parts = []
    for row in range(SIDE):
        for kv in kvs:
            parts.append(kv[SIDE * level + row, low : low + PIECE, :])
    return jnp.concatenate(parts, axis=0)


def source_steps(scalars, chunks):
    step = lax.broadcasted_iota(jnp.int32, (PIECE, WIDE), 0)
    return jnp.concatenate([step + scalars[SIDE + chunk] for chunk in chunks], axis=0)


def masked(block, steps, lim, level, row, lanes):
    size = steps.shape[0]
    part = block[row * size : (row + 1) * size]
    return jnp.where(steps < lim[SIDE * level + row, lanes][None, :], part, MASKED)


def unit_lanes(unit):
    return pl.ds(pl.multiple_of(unit * WIDE, WIDE), WIDE)


def stats_kernel(chunks, start, *refs):
    scalars, lim, own, other = refs[:4]
    kvs, refs = refs[4 : 4 + len(chunks)], refs[4 + len(chunks) :]
    out = refs[-1]
    if start:
        out[...] = jnp.zeros_like(out)
        out[0:1, :] = jnp.full((1, ROWS), MASKED, jnp.float32)
    else:
        out[...] = refs[0][...]
    size = PIECE * len(chunks)
    for level in range(SIDE):

        def unit_stats(unit, carry):
            lanes = unit_lanes(unit)
            steps = source_steps(scalars, chunks)
            x = unit_rows(own, other, unit, QUERY)
            g = unit_rows(own, other, unit, GRAD)
            product = dot(source_rows(kvs, level, 0), x, 1, 1)
            prods = dot(source_rows(kvs, level, PIECE), g, 1, 1)
            scores = [masked(product, steps, lim, level, row, lanes) for row in range(SIDE)]
            top = functools.reduce(jnp.maximum, scores).max(axis=0, keepdims=True)
            old = out[0:1, lanes]
            high = jnp.maximum(old, top * (SCALE * LOG2E))
            base = jnp.maximum(high, FLOOR)
            total = jnp.zeros((size, WIDE), jnp.float32)
            mixed = jnp.zeros((size, WIDE), jnp.float32)
            for row in range(SIDE):
                weights = jnp.exp2(scores[row] * (SCALE * LOG2E) - base)
                total += weights
                mixed += weights * prods[row * size : (row + 1) * size]
            fade = jnp.exp2(old - high)
            out[0:1, lanes] = high
            out[1:2, lanes] = out[1:2, lanes] * fade + total.sum(axis=0, keepdims=True)
            out[2:3, lanes] = out[2:3, lanes] * fade + mixed.sum(axis=0, keepdims=True)
            return carry

        lax.fori_loop(scalars[level], SIDE, unit_stats, 0)


def source_grads_kernel(scalars, lim, own, other, mine, theirs, kv0, kv1, kv2, kv3, *refs):
    kvs = (kv0, kv1, kv2, kv3)
    outs, (lows, shift, delta, key_acc, value_acc) = refs[:SIDE], refs[SIDE:]
    for tile in range(TILES):
        lanes = slice(tile * TILE, (tile + 1) * TILE)
        a = mine[:, lanes]
        b = pltpu.roll(theirs[:, lanes], HALF, 1)
        high = jnp.maximum(a[0:1], b[0:1])
        wa = jnp.exp2(a[0:1] - high)
        wb = jnp.exp2(b[0:1] - high)
        total = a[1:2] * wa + b[1:2] * wb
        mixed = a[2:3] * wa + b[2:3] * wb
        shift[0:1, lanes] = high + jnp.log2(total)
        delta[0:1, lanes] = mixed / total
    for level in range(SIDE):
        key_acc[...] = jnp.zeros_like(key_acc)
        value_acc[...] = jnp.zeros_like(value_acc)

        def unit_grads(unit, carry):
            lanes = unit_lanes(unit)
            steps = source_steps(scalars, range(SIDE))
            x = unit_rows(own, other, unit, QUERY)
            g = unit_rows(own, other, unit, GRAD)
            scores = dot(source_rows(kvs, level, 0), x, 1, 1) * (SCALE * LOG2E) - shift[0:1, lanes]
            prods = dot(source_rows(kvs, level, PIECE), g, 1, 1) - delta[0:1, lanes]
            highs = []
            parts = []
            for row in range(SIDE):
                probs = jnp.exp2(masked(scores, steps, lim, level, row, lanes))
                highs.append(probs.astype(jnp.bfloat16))
                parts.append((probs * prods[row * TILE : (row + 1) * TILE]).astype(jnp.bfloat16))
            low = jnp.concatenate(parts, axis=0)
            lows[SIDE * level + unit] = low
            value_acc[...] += dot(jnp.concatenate(highs, axis=0), g, 1, 0)
            key_acc[...] += dot(low, x, 1, 0)
            return carry

        lax.fori_loop(scalars[level], SIDE, unit_grads, 0)
        for row in range(SIDE):
            for index, out in enumerate(outs):
                begin = row * TILE + index * PIECE
                rows = slice(begin, begin + PIECE)
                tile = SIDE * level + row
                out[tile, 0:PIECE, :] = (key_acc[rows, :] * SCALE).astype(jnp.bfloat16)
                out[tile, PIECE : 2 * PIECE, :] = value_acc[rows, :].astype(jnp.bfloat16)


def query_grads_kernel(scalars, kv0, kv1, kv2, kv3, lows, keep, send, acc):
    kvs = (kv0, kv1, kv2, kv3)
    acc[...] = jnp.zeros_like(acc)
    for level in range(SIDE):

        def unit_grads(unit, carry):
            keys = source_rows(kvs, level, 0)
            acc[unit_lanes(unit), :] += dot(lows[SIDE * level + unit], keys, 0, 0)
            return carry

        lax.fori_loop(scalars[level], SIDE, unit_grads, 0)
    for unit in range(SIDE):
        for level in range(SIDE):
            begin = (SIDE * unit + level) * TILE
            tile = SIDE * level + unit
            keep[tile] = acc[begin : begin + HALF, :] * SCALE
            send[tile] = (acc[begin + HALF : begin + TILE, :] * SCALE).astype(jnp.bfloat16)


def pack_kernel(sums, keep, returned, out):
    out[:, : 2 * PIECE, :] = sums[...]
    out[:, 2 * PIECE :, :] = (keep[...] + returned[...].astype(jnp.float32)).astype(jnp.bfloat16)


SMEM = pl.BlockSpec(memory_space=pltpu.SMEM)
VMEM = pl.BlockSpec(memory_space=pltpu.VMEM)
PARAMS = pltpu.CompilerParams(vmem_limit_bytes=LIMIT)


def cost(chunks, dots):
    flops = 10 * len(chunks) * dots * 2 * PIECE * SIDE * WIDE * DIM
    return pl.CostEstimate(flops=flops, bytes_accessed=2**20, transcendentals=0)


def row_stats(chunks, scalars, lim, own, other, kvs, previous):
    operands = [scalars, lim, own, other] + [kvs[c] for c in chunks]
    if previous is not None:
        operands.append(previous)
    return pl.pallas_call(
        functools.partial(stats_kernel, chunks, previous is None),
        out_shape=jax.ShapeDtypeStruct((8, ROWS), jnp.float32),
        in_specs=[SMEM] + [VMEM] * (len(operands) - 1),
        out_specs=VMEM,
        compiler_params=PARAMS,
        cost_estimate=cost(chunks, 4),
        name="stats",
    )(*operands)


def source_grads(scalars, lim, own, other, mine, theirs, kvs):
    piece = jax.ShapeDtypeStruct((TILES, 2 * PIECE, DIM), jnp.bfloat16)
    lows = jax.ShapeDtypeStruct((TILES, WIDE, WIDE), jnp.bfloat16)
    operands = (scalars, lim, own, other, mine, theirs, *kvs)
    return pl.pallas_call(
        source_grads_kernel,
        out_shape=[piece] * SIDE + [lows],
        in_specs=[SMEM] + [VMEM] * (len(operands) - 1),
        out_specs=[VMEM] * (SIDE + 1),
        scratch_shapes=[
            pltpu.VMEM((8, ROWS), jnp.float32),
            pltpu.VMEM((8, ROWS), jnp.float32),
            pltpu.VMEM((WIDE, DIM), jnp.float32),
            pltpu.VMEM((WIDE, DIM), jnp.float32),
        ],
        compiler_params=PARAMS,
        cost_estimate=cost((0, 1, 2, 3), 4),
        name="source_grads",
    )(*operands)


def query_grads(scalars, kvs, lows):
    shape = (TILES, HALF, DIM)
    return pl.pallas_call(
        query_grads_kernel,
        out_shape=[jax.ShapeDtypeStruct(shape, jnp.float32), jax.ShapeDtypeStruct(shape, jnp.bfloat16)],
        in_specs=[SMEM] + [VMEM] * 5,
        out_specs=[VMEM] * 2,
        scratch_shapes=[pltpu.VMEM((ROWS, DIM), jnp.float32)],
        compiler_params=PARAMS,
        cost_estimate=cost((0, 1, 2, 3), 1),
        name="query_grads",
    )(scalars, *kvs, lows)


def pack_result(sums, keep, returned):
    return pl.pallas_call(
        pack_kernel,
        out_shape=jax.ShapeDtypeStruct((TILES, 2 * PIECE + HALF, DIM), jnp.bfloat16),
        in_specs=[VMEM] * 3,
        out_specs=VMEM,
        compiler_params=PARAMS,
        name="pack",
    )(sums, keep, returned)


def gather_kernel(*refs):
    out = refs[-1]
    for tile in range(TILES):
        low = 0
        for ref in refs[:-1]:
            high = low + ref.shape[0]
            wide = ref.shape[1] > DIM
            out[tile, low:high, :] = ref[:, tile * DIM : (tile + 1) * DIM] if wide else ref[...]
            low = high


def by_head(*arrays):
    rows = sum(a.shape[0] for a in arrays)
    return pl.pallas_call(
        gather_kernel,
        out_shape=jax.ShapeDtypeStruct((TILES, rows, DIM), jnp.bfloat16),
        in_specs=[VMEM] * len(arrays),
        out_specs=VMEM,
        compiler_params=PARAMS,
        name="by_head",
    )(*arrays)


def by_row_kernel(heads, keys, values, queries):
    for tile in range(TILES):
        columns = slice(tile * DIM, (tile + 1) * DIM)
        keys[:, columns] = heads[tile, :PIECE, :]
        values[:, columns] = heads[tile, PIECE : 2 * PIECE, :]
        queries[:, columns] = heads[tile, 2 * PIECE :, :]


def by_row(heads):
    rows = (PIECE, PIECE, HALF)
    return pl.pallas_call(
        by_row_kernel,
        out_shape=[jax.ShapeDtypeStruct((n, TILES * DIM), jnp.bfloat16) for n in rows],
        in_specs=[VMEM],
        out_specs=[VMEM] * 3,
        compiler_params=PARAMS,
        name="by_row",
    )(heads)


def device(row, column, level, core):
    return (row * SIDE + column) * 2 * SIDE + level * 2 + core


GROUPS = [
    [device(row, column, level, core) for level in range(SIDE) for row in range(SIDE)]
    for column in range(SIDE)
    for core in range(2)
]


def exchange(a):
    return lax.all_to_all(a, ("tgt", "src"), 0, 0, axis_index_groups=GROUPS, tiled=True)


def swap_cores(a):
    return lax.ppermute(a, "src", [(i, i ^ 1) for i in range(2 * SIDE)])


def along(a, shift):
    def target(i):
        return i - i % SIDE + (i + shift) % SIDE

    return lax.ppermute(a, "tgt", [(i, target(i)) for i in range(TILES)])


def shards(queries, keys, values, out_grad, read_points, block_mask):
    place = lax.axis_index("src")
    level, core = place // 2, place % 2
    column = lax.axis_index("tgt") % SIDE

    reads = lax.dynamic_slice_in_dim(read_points, level * TILE, TILE)
    digits = jnp.stack([reads // 64, reads % 64]).astype(jnp.bfloat16)
    digits = jnp.pad(digits, ((0, 14), (0, 0)))
    kv = exchange(by_head(keys, values))
    kvs = [kv] + [along(kv, k) for k in (1, 3, 2)]
    own = exchange(by_head(queries, out_grad, digits))
    other = swap_cores(own)

    reads = own[:, DIGIT].astype(jnp.int32) * 64 + own[:, DIGIT + 1].astype(jnp.int32)
    begins = (
        jnp.arange(SIDE, dtype=jnp.int32)[:, None] * (2 * WIDE)
        + core * WIDE
        + jnp.arange(SIDE, dtype=jnp.int32)[None, :] * TILE
    )
    tops = reads[TILES - SIDE :, -1]
    first = jnp.sum(tops[None, :] <= begins[:, :1], axis=1)
    offsets = jnp.stack([(column - k) % SIDE * PIECE for k in (0, 1, 3, 2)])
    scalars = jnp.concatenate([first, offsets]).astype(jnp.int32)
    ordered = jnp.where(core == 0, reads, jnp.roll(reads, HALF, axis=1))
    ordered = ordered.reshape(SIDE, SIDE, TILE).transpose(1, 0, 2)
    flags = block_mask.reshape(SIDE, SIDE, SIDE, SIDE, 2, SIDE)
    flags = lax.dynamic_index_in_dim(flags, column, 1, False)
    flags = lax.dynamic_index_in_dim(flags, core, 3, False).transpose(2, 3, 0, 1)
    lim = jnp.where(flags[..., None] == 1, ordered[None, None], 0) - begins[:, :, None, None, None]
    lim = lim.reshape(TILES, ROWS)

    common = (scalars, lim, own, other)
    mine = row_stats((0, 1, 2, 3), *common, kvs, None)
    theirs = swap_cores(mine)
    common += (mine, theirs, kvs)
    part0, part1, part2, part3, lows = source_grads(*common)
    got3, got1, got2 = along(part3, 2), along(part1, 3), along(part2, 1)
    keep, send = query_grads(scalars, kvs, lows)
    returned = swap_cores(send)
    sums = functools.reduce(jnp.add, [p.astype(jnp.float32) for p in (part0, got1, got2, got3)])
    result = pack_result(sums.astype(jnp.bfloat16), keep, returned)
    key_grad, value_grad, query_grad = by_row(exchange(result))
    return query_grad, key_grad, value_grad


def solution(mesh):
    in_specs = (
        P(("tgt", "src"), "head"),
        P(("src", "tgt"), "head"),
        P(("src", "tgt"), "head"),
        P(("tgt", "src"), "head"),
        P("tgt"),
        P(),
    )
    out_specs = (P(("tgt", "src"), "head"), P(("src", "tgt"), "head"), P(("src", "tgt"), "head"))
    return jax.shard_map(shards, mesh=mesh, in_specs=in_specs, out_specs=out_specs, check_vma=False)
```

time: 126 us -> 98.6 us (0.78)
  waiting for transfers between devices: 49.8 us -> 23.4 us
  Pallas kernels: 29.1 us -> 22.1 us
  starting transfers between devices: 21 us -> 27.6 us
  local copies, waits for them, and re-layouts: 3.53 us -> 6.1 us
  blocking collectives: 18 us -> 15.7 us
  other arithmetic: 3.49 us -> 1.41 us
    ppermute x9, waiting for transfers between devices: 36.8 us -> 9.63 us  [the longest x6 6.67 us: along(): return lax.ppermute(a, 'tgt', [(i, target(i)) for i in range(TILES)])]
    pallas_call x4 -> x7, Pallas kernels: 29.1 us -> 22.1 us  [the longest x1 8.75 us: source_grads(): pl.pallas_call(source_grads_kernel, out_shape=[piece] * SIDE + [lows], in...]
    unnamed x9, local copies, waits for them, and re-layouts: 0.04 us -> 3.9 us
    ppermute x9, starting transfers between devices: 10.4 us -> 13.9 us  [the longest x6 13.6 us: along(): return lax.ppermute(a, 'tgt', [(i, target(i)) for i in range(TILES)])]
    all_to_all x2, starting transfers between devices: 10.6 us -> 13.8 us  [exchange(): lax.all_to_all(a, ('tgt', 'src'), 0, 0, axis_index_groups=GROUPS, tiled=T...]
    all_to_all x1, blocking collectives: 18 us -> 15.7 us  [exchange(): lax.all_to_all(a, ('tgt', 'src'), 0, 0, axis_index_groups=GROUPS, tiled=T...]
    all_to_all x1 -> x0, other arithmetic: 1.79 us -> none  [by_head(): lax.all_to_all(a, 'tgt', 1, 0, tiled=True).reshape(TILES, a.shape[0], DIM)]
  transfers between devices with their start and end apart: 11 -> 11, of which waited for: 8 -> 7; matrix products, arithmetic and copies ran while one was open for 2% -> 4% of each run, Pallas kernels for 0% -> 5%
where the time goes in v2:
time: 98.6 us; the launch traced here: 97.2 us
  starting transfers between devices  27.6 us (28%)
  waiting for transfers between devices  23.4 us (24%)
  Pallas kernels  22.1 us (22%)
  blocking collectives  15.7 us (16%)
  local copies, waits for them, and re-layouts  6.1 us (6%)
  other arithmetic  1.41 us (1%)
    all_to_all x1, blocking collectives, exchange(): lax.all_to_all(a, ('tgt', 'src'), 0, 0, axis_index_groups=GROUPS, tiled=T...  15.7 us
    all_to_all x2, waiting for transfers between devices, exchange(): lax.all_to_all(a, ('tgt', 'src'), 0, 0, axis_index_groups=GROUPS, tiled=T...  13.8 us
    all_to_all x2, starting transfers between devices, exchange(): lax.all_to_all(a, ('tgt', 'src'), 0, 0, axis_index_groups=GROUPS, tiled=T...  13.8 us
    ppermute x6, starting transfers between devices, along(): return lax.ppermute(a, 'tgt', [(i, target(i)) for i in range(TILES)])  13.6 us
    pallas_call x1, Pallas kernels, source_grads(): pl.pallas_call(source_grads_kernel, out_shape=[piece] * SIDE + [lows], in...  8.75 us
    ppermute x6, waiting for transfers between devices, along(): return lax.ppermute(a, 'tgt', [(i, target(i)) for i in range(TILES)])  6.67 us
    pallas_call x1, Pallas kernels, row_stats(): pl.pallas_call(functools.partial(stats_kernel, chunks, previous is None),...  6.41 us
    pallas_call x1, Pallas kernels, query_grads(): pl.pallas_call(query_grads_kernel, out_shape=[jax.ShapeDtypeStruct(shape,...  4.31 us
  transfers between devices with their start and end apart: 11, of which 7 were waited for; matrix products, arithmetic and copies ran while one was open for 4% of the time, Pallas kernels for 5%

profile of v2, /device:TPU:32, one launch (start us, length us, event | category | flops | bytes accessed | tf_op | source)
XLA Modules:
  0.0 97.2 jit_solution(17502607242128309770)
XLA Ops:
  0.6 0.9 copy-done.2
  1.5 0.9 copy-done.3
  2.4 0.7 by_head.3
  3.2 8.7 %all-to-all-start.1 = ((bf16[16,64,128]{2,1,0:T(8,128)(2,1)}), bf16[16,64,128]{2,1,0:T(8,128)(2,1)S(1)}, u32[]{:S(2)}, u32[]{:S(2)}) async-start(bf16[16,64,128]{2,1,0:T(8,128)(2,1)} %by_head.3), calls=%async_computation.1 | async-start | bytes 524288 | tf_op jit(solution)/shard_map/all_to_all | solution.py:301
  11.8 0.8 convert_bitcast_fusion
  12.6 0.9 copy-done
  13.6 0.9 copy-done.1
  14.5 0.9 by_head.2
  15.5 5.7 %all-to-all-done.1.refs_4_.kv0 = bf16[16,64,128]{2,1,0:T(8,128)(2,1)S(1)} async-done(((bf16[16,64,128]{2,1,0:T(8,128)(2,1)}), bf16[16,64,128]{2,1,0:T(8,128)(2,1)S(1)}, u32[]{:S(2)}, u32[]{:S(2)}) %all-to-all-start.1) | async-done | bytes 262176 | tf_op jit(solution)/shard_map/all_to_all | solution.py:301
  21.2 5.1 %all-to-all-start = ((bf16[16,144,128]{2,1,0:T(8,128)(2,1)}), bf16[16,144,128]{2,1,0:T(8,128)(2,1)S(1)}, u32[]{:S(2)}, u32[]{:S(2)}) async-start(bf16[16,144,128]{2,1,0:T(8,128)(2,1)} %by_head.2), calls=%async_computation | async-start | bytes 1179648 | tf_op jit(solution)/shard_map/all_to_all | solution.py:301
  26.6 1.1 %reshape.73 = s32[4,4,4,4,2,4]{2,1,0,5,4,3:T(4,128)S(1)} reshape(s32[64,32]{0,1:T(8,128)} %param.11) | data formatting | bytes 16384 | tf_op jit(solution)/shard_map/reshape | solution.py:340
  27.7 0.2 copy.19
  27.9 0.2 copy.15
  28.1 0.1 broadcast_in_dim.29
  28.5 3.1 %collective-permute-start.3 = (bf16[16,64,128]{2,1,0:T(8,128)(2,1)S(1)}, bf16[16,64,128]{2,1,0:T(8,128)(2,1)S(1)}, u32[]{:S(2)}, u32[]{:S(2)}) collective-permute-start(bf16[16,64,128]{2,1,0:T(8,128)(2,1)S(1)} %all-to-all-done.1.refs_4_.kv0), channel_id=1, source_target_pairs={{0,32},{16,48},{32,0},{48,16},{64,96},{80,112},{96,64},{112,80},{1... | collective-permute-start | bytes 786440 | tf_op jit(solution)/shard_map/ppermute | solution.py:312
  31.6 1.1 %collective-permute-start.2 = (bf16[16,64,128]{2,1,0:T(8,128)(2,1)S(1)}, bf16[16,64,128]{2,1,0:T(8,128)(2,1)S(1)}, u32[]{:S(2)}, u32[]{:S(2)}) collective-permute-start(bf16[16,64,128]{2,1,0:T(8,128)(2,1)S(1)} %all-to-all-done.1.refs_4_.kv0), channel_id=1, source_target_pairs={{0,48},{16,0},{32,16},{48,32},{64,112},{80,64},{96,80},{112,96},{1... | collective-permute-start | bytes 786440 | tf_op jit(solution)/shard_map/ppermute | solution.py:312
  32.7 0.9 collective-permute-start.1
  33.6 8.0 %all-to-all-done.refs_2_.own = bf16[16,144,128]{2,1,0:T(8,128)(2,1)S(1)} async-done(((bf16[16,144,128]{2,1,0:T(8,128)(2,1)}), bf16[16,144,128]{2,1,0:T(8,128)(2,1)S(1)}, u32[]{:S(2)}, u32[]{:S(2)}) %all-to-all-start) | async-done | bytes 589856 | tf_op jit(solution)/shard_map/all_to_all | solution.py:301
  41.7 0.2 slice_reduce_fusion
  42.0 0.2 convert_reduce_fusion
  42.6 1.7 %collective-permute-done.refs_3_.other = bf16[16,144,128]{2,1,0:T(8,128)(2,1)S(1)} collective-permute-done((bf16[16,144,128]{2,1,0:T(8,128)(2,1)S(1)}, bf16[16,144,128]{2,1,0:T(8,128)(2,1)S(1)}, u32[]{:S(2)}, u32[]{:S(2)}) %collective-permute-start) | collective-permute-done | bytes 589856 | tf_op jit(solution)/shard_map/ppermute | solution.py:305
  44.3 6.4 %stats.1.mine = f32[8,2048]{1,0:T(8,128)S(1)} custom-call(s32[8]{0:T(128)S(1)} %concatenate.12.refs_0_.scalars, s32[16,2048]{1,0:T(8,128)S(1)} %select_subtract_fusion.refs_1_.lim, bf16[16,144,128]{2,1,0:T(8,128)(2,1)S(1)} %all-to-all-done.refs_2_.own, bf16[16,144,128]{2,1,0:T(8,128)(2,1)S(1)} %collective-permute-done.refs_3_.other, ...), custom_call_target="tpu_custom_call" | custom-call | flops 2684354560 | bytes 1048576 | tf_op jit(solution)/shard_map/stats/pallas_call | solution.py:189
  50.8 1.2 %collective-permute-done.4.theirs = f32[8,2048]{1,0:T(8,128)S(1)} collective-permute-done((f32[8,2048]{1,0:T(8,128)S(1)}, f32[8,2048]{1,0:T(8,128)S(1)}, u32[]{:S(2)}, u32[]{:S(2)}) %collective-permute-start.4) | collective-permute-done | bytes 65568 | tf_op jit(solution)/shard_map/ppermute | solution.py:305
  52.0 8.7 %source_grads.1 = (bf16[16,64,128]{2,1,0:T(8,128)(2,1)S(1)}, bf16[16,64,128]{2,1,0:T(8,128)(2,1)S(1)}, bf16[16,64,128]{2,1,0:T(8,128)(2,1)S(1)}, bf16[16,64,128]...) custom-call(s32[8]{0:T(128)S(1)} %concatenate.12.refs_0_.scalars, s32[16,2048]{1,0:T(8,128)S(1)} %select_subtract_fusion.refs_1_.lim, ...), custom_call_target="tpu_custom_call" | custom-call | flops 2684354560 | bytes 1048576 | tf_op jit(solution)/shard_map/source_grads/pallas_call | solution.py:204
  60.8 7.0 %collective-permute-start.5 = (bf16[16,64,128]{2,1,0:T(8,128)(2,1)S(1)}, bf16[16,64,128]{2,1,0:T(8,128)(2,1)S(1)}, u32[]{:S(2)}, u32[]{:S(2)}) collective-permute-start(bf16[16,64,128]{2,1,0:T(8,128)(2,1)S(1)} %get-tuple-element.14), channel_id=1, source_target_pairs={{0,48},{16,0},{32,16},{48,32},{64,112},{80,64},{96,80},{112,96},{1... | collective-permute-start | bytes 786440 | tf_op jit(solution)/shard_map/ppermute | solution.py:312
  67.8 1.6 %collective-permute-start.7 = (bf16[16,64,128]{2,1,0:T(8,128)(2,1)S(1)}, bf16[16,64,128]{2,1,0:T(8,128)(2,1)S(1)}, u32[]{:S(2)}, u32[]{:S(2)}) collective-permute-start(bf16[16,64,128]{2,1,0:T(8,128)(2,1)S(1)} %get-tuple-element.16), channel_id=1, source_target_pairs={{0,32},{16,48},{32,0},{48,16},{64,96},{80,112},{96,64},{112,80},{1... | collective-permute-start | bytes 786440 | tf_op jit(solution)/shard_map/ppermute | solution.py:312
  69.3 4.3 %query_grads.1 = (f32[16,64,128]{2,1,0:T(8,128)S(1)}, bf16[16,64,128]{2,1,0:T(8,128)(2,1)S(1)}) custom-call(s32[8]{0:T(128)S(1)} %concatenate.12.refs_0_.scalars, bf16[16,64,128]{2,1,0:T(8,128)(2,1)S(1)} %all-to-all-done.1.refs_4_.kv0, bf16[16,64,128]{2,1,0:T(8,128)(2,1)S(1)} %collective-permute-done.1.refs_5_.kv1, ...), custom_call_target="tpu_custom_call" | custom-call | flops 671088640 | bytes 1048576 | tf_op jit(solution)/shard_map/query_grads/pallas_call | solution.py:223
  73.7 3.3 %collective-permute-done.5 = bf16[16,64,128]{2,1,0:T(8,128)(2,1)S(1)} collective-permute-done((bf16[16,64,128]{2,1,0:T(8,128)(2,1)S(1)}, bf16[16,64,128]{2,1,0:T(8,128)(2,1)S(1)}, u32[]{:S(2)}, u32[]{:S(2)}) %collective-permute-start.5) | collective-permute-done | bytes 262176 | tf_op jit(solution)/shard_map/ppermute | solution.py:312
  77.0 3.2 %collective-permute-done.6 = bf16[16,64,128]{2,1,0:T(8,128)(2,1)S(1)} collective-permute-done((bf16[16,64,128]{2,1,0:T(8,128)(2,1)S(1)}, bf16[16,64,128]{2,1,0:T(8,128)(2,1)S(1)}, u32[]{:S(2)}, u32[]{:S(2)}) %collective-permute-start.6) | collective-permute-done | bytes 262176 | tf_op jit(solution)/shard_map/ppermute | solution.py:312
  80.3 0.2 add_convert_fusion.sums
  80.6 15.7 %all_to_all.15.heads = bf16[16,128,128]{2,1,0:T(8,128)(2,1)S(1)} all-to-all(bf16[16,128,128]{2,1,0:T(8,128)(2,1)S(1)} %pack.1), channel_id=1, replica_groups={{0,64,128,192,4,68,132,196,8,72,136,200,12,76,140,204},{2,66,130,194,6,..., dimensions={0} | all-to-all | bytes 1048576 | tf_op jit(solution)/shard_map/all_to_all | solution.py:301
  96.3 0.9 by_row.1
  (34 shorter events, 1.3 us)
Async XLA Ops:
  0.6 0.9 copy-start.2
  1.5 0.9 copy-start.3
  3.2 18.0 %all-to-all-start.1 = ((bf16[16,64,128]{2,1,0:T(8,128)(2,1)}), bf16[16,64,128]{2,1,0:T(8,128)(2,1)S(1)}, u32[]{:S(2)}, u32[]{:S(2)}) async-start(bf16[16,64,128]{2,1,0:T(8,128)(2,1)} %by_head.3), calls=%async_computation.1 | async-start | bytes 524288 | tf_op jit(solution)/shard_map/all_to_all | solution.py:301
  12.6 1.0 copy-start
  13.6 0.9 copy-start.1
  21.2 20.5 %all-to-all-start = ((bf16[16,144,128]{2,1,0:T(8,128)(2,1)}), bf16[16,144,128]{2,1,0:T(8,128)(2,1)S(1)}, u32[]{:S(2)}, u32[]{:S(2)}) async-start(bf16[16,144,128]{2,1,0:T(8,128)(2,1)} %by_head.2), calls=%async_computation | async-start | bytes 1179648 | tf_op jit(solution)/shard_map/all_to_all | solution.py:301
  28.5 13.9 %collective-permute-start.3 = (bf16[16,64,128]{2,1,0:T(8,128)(2,1)S(1)}, bf16[16,64,128]{2,1,0:T(8,128)(2,1)S(1)}, u32[]{:S(2)}, u32[]{:S(2)}) collective-permute-start(bf16[16,64,128]{2,1,0:T(8,128)(2,1)S(1)} %all-to-all-done.1.refs_4_.kv0), channel_id=1, source_target_pairs={{0,32},{16,48},{32,0},{48,16},{64,96},{80,112},{96,64},{112,80},{1... | collective-permute-start | bytes 786440 | tf_op jit(solution)/shard_map/ppermute | solution.py:312
  31.6 10.9 %collective-permute-start.2 = (bf16[16,64,128]{2,1,0:T(8,128)(2,1)S(1)}, bf16[16,64,128]{2,1,0:T(8,128)(2,1)S(1)}, u32[]{:S(2)}, u32[]{:S(2)}) collective-permute-start(bf16[16,64,128]{2,1,0:T(8,128)(2,1)S(1)} %all-to-all-done.1.refs_4_.kv0), channel_id=1, source_target_pairs={{0,48},{16,0},{32,16},{48,32},{64,112},{80,64},{96,80},{112,96},{1... | collective-permute-start | bytes 786440 | tf_op jit(solution)/shard_map/ppermute | solution.py:312
  32.7 9.8 %collective-permute-start.1 = (bf16[16,64,128]{2,1,0:T(8,128)(2,1)S(1)}, bf16[16,64,128]{2,1,0:T(8,128)(2,1)S(1)}, u32[]{:S(2)}, u32[]{:S(2)}) collective-permute-start(bf16[16,64,128]{2,1,0:T(8,128)(2,1)S(1)} %all-to-all-done.1.refs_4_.kv0), channel_id=1, source_target_pairs={{0,16},{16,32},{32,48},{48,0},{64,80},{80,96},{96,112},{112,64},{1... | collective-permute-start | bytes 786440 | tf_op jit(solution)/shard_map/ppermute | solution.py:312
  42.2 2.0 %collective-permute-start = (bf16[16,144,128]{2,1,0:T(8,128)(2,1)S(1)}, bf16[16,144,128]{2,1,0:T(8,128)(2,1)S(1)}, u32[]{:S(2)}, u32[]{:S(2)}) collective-permute-start(bf16[16,144,128]{2,1,0:T(8,128)(2,1)S(1)} %all-to-all-done.refs_2_.own), channel_id=1, source_target_pairs={{0,2},{2,0},{4,6},{6,4},{8,10},{10,8},{12,14},{14,12},{1,3},{3,1},... | collective-permute-start | bytes 1769480 | tf_op jit(solution)/shard_map/ppermute | solution.py:305
  50.7 1.3 %collective-permute-start.4 = (f32[8,2048]{1,0:T(8,128)S(1)}, f32[8,2048]{1,0:T(8,128)S(1)}, u32[]{:S(2)}, u32[]{:S(2)}) collective-permute-start(f32[8,2048]{1,0:T(8,128)S(1)} %stats.1.mine), channel_id=1, source_target_pairs={{0,2},{2,0},{4,6},{6,4},{8,10},{10,8},{12,14},{14,12},{1,3},{3,1},... | collective-permute-start | bytes 196616 | tf_op jit(solution)/shard_map/ppermute | solution.py:305
  60.8 16.3 %collective-permute-start.5 = (bf16[16,64,128]{2,1,0:T(8,128)(2,1)S(1)}, bf16[16,64,128]{2,1,0:T(8,128)(2,1)S(1)}, u32[]{:S(2)}, u32[]{:S(2)}) collective-permute-start(bf16[16,64,128]{2,1,0:T(8,128)(2,1)S(1)} %get-tuple-element.14), channel_id=1, source_target_pairs={{0,48},{16,0},{32,16},{48,32},{64,112},{80,64},{96,80},{112,96},{1... | collective-permute-start | bytes 786440 | tf_op jit(solution)/shard_map/ppermute | solution.py:312
  67.7 12.5 %collective-permute-start.6 = (bf16[16,64,128]{2,1,0:T(8,128)(2,1)S(1)}, bf16[16,64,128]{2,1,0:T(8,128)(2,1)S(1)}, u32[]{:S(2)}, u32[]{:S(2)}) collective-permute-start(bf16[16,64,128]{2,1,0:T(8,128)(2,1)S(1)} %get-tuple-element.15), channel_id=1, source_target_pairs={{0,16},{16,32},{32,48},{48,0},{64,80},{80,96},{96,112},{112,64},{1... | collective-permute-start | bytes 786440 | tf_op jit(solution)/shard_map/ppermute | solution.py:312
  67.8 12.5 %collective-permute-start.7 = (bf16[16,64,128]{2,1,0:T(8,128)(2,1)S(1)}, bf16[16,64,128]{2,1,0:T(8,128)(2,1)S(1)}, u32[]{:S(2)}, u32[]{:S(2)}) collective-permute-start(bf16[16,64,128]{2,1,0:T(8,128)(2,1)S(1)} %get-tuple-element.16), channel_id=1, source_target_pairs={{0,32},{16,48},{32,0},{48,16},{64,96},{80,112},{96,64},{112,80},{1... | collective-permute-start | bytes 786440 | tf_op jit(solution)/shard_map/ppermute | solution.py:312
  73.6 6.8 %collective-permute-start.8 = (bf16[16,64,128]{2,1,0:T(8,128)(2,1)S(1)}, bf16[16,64,128]{2,1,0:T(8,128)(2,1)S(1)}, u32[]{:S(2)}, u32[]{:S(2)}) collective-permute-start(bf16[16,64,128]{2,1,0:T(8,128)(2,1)S(1)} %get-tuple-element.19), channel_id=1, source_target_pairs={{0,2},{2,0},{4,6},{6,4},{8,10},{10,8},{12,14},{14,12},{1,3},{3,1},... | collective-permute-start | bytes 786440 | tf_op jit(solution)/shard_map/ppermute | solution.py:305

commit v3 on v2

--- a/solution.py
+++ b/solution.py
@@ -18,7 +18,6 @@
 QUERY = 0
 GRAD = QUERY + HALF
 DIGIT = GRAD + HALF
-PACKED = DIGIT + 16
 MASKED = -1e30
 FLOOR = -1e29
 SCALE = float(DIM) ** -0.5
@@ -47,14 +46,13 @@
     return jnp.concatenate(parts, axis=0)
 
 
-def source_steps(scalars, chunks):
+def source_steps(scalars):
     step = lax.broadcasted_iota(jnp.int32, (PIECE, WIDE), 0)
-    return jnp.concatenate([step + scalars[SIDE + chunk] for chunk in chunks], axis=0)
+    return jnp.concatenate([step + scalars[SIDE + chunk] for chunk in range(SIDE)], axis=0)
 
 
 def masked(block, steps, lim, level, row, lanes):
-    size = steps.shape[0]
-    part = block[row * size : (row + 1) * size]
+    part = block[row * TILE : (row + 1) * TILE]
     return jnp.where(steps < lim[SIDE * level + row, lanes][None, :], part, MASKED)
 
 
@@ -62,43 +60,45 @@
     return pl.ds(pl.multiple_of(unit * WIDE, WIDE), WIDE)
 
 
-def stats_kernel(chunks, start, *refs):
-    scalars, lim, own, other = refs[:4]
-    kvs, refs = refs[4 : 4 + len(chunks)], refs[4 + len(chunks) :]
-    out = refs[-1]
-    if start:
-        out[...] = jnp.zeros_like(out)
-        out[0:1, :] = jnp.full((1, ROWS), MASKED, jnp.float32)
-    else:
-        out[...] = refs[0][...]
-    size = PIECE * len(chunks)
+def stats_kernel(scalars, lim, own, other, kv0, kv1, kv2, kv3, out, acc):
+    kvs = (kv0, kv1, kv2, kv3)
+    acc[...] = jnp.zeros_like(acc)
+    acc[0:8, :] = jnp.full((8, ROWS), MASKED, jnp.float32)
     for level in range(SIDE):
 
         def unit_stats(unit, carry):
             lanes = unit_lanes(unit)
-            steps = source_steps(scalars, chunks)
+            steps = source_steps(scalars)
             x = unit_rows(own, other, unit, QUERY)
             g = unit_rows(own, other, unit, GRAD)
             product = dot(source_rows(kvs, level, 0), x, 1, 1)
             prods = dot(source_rows(kvs, level, PIECE), g, 1, 1)
-            scores = [masked(product, steps, lim, level, row, lanes) for row in range(SIDE)]
-            top = functools.reduce(jnp.maximum, scores).max(axis=0, keepdims=True)
-            old = out[0:1, lanes]
-            high = jnp.maximum(old, top * (SCALE * LOG2E))
-            base = jnp.maximum(high, FLOOR)
-            total = jnp.zeros((size, WIDE), jnp.float32)
-            mixed = jnp.zeros((size, WIDE), jnp.float32)
+            high = acc[0:8, lanes]
+            total = acc[8:16, lanes]
+            mixed = acc[16:24, lanes]
+            shape = (TILE // 8, 8, WIDE)
             for row in range(SIDE):
-                weights = jnp.exp2(scores[row] * (SCALE * LOG2E) - base)
-                total += weights
-                mixed += weights * prods[row * size : (row + 1) * size]
-            fade = jnp.exp2(old - high)
-            out[0:1, lanes] = high
-            out[1:2, lanes] = out[1:2, lanes] * fade + total.sum(axis=0, keepdims=True)
-            out[2:3, lanes] = out[2:3, lanes] * fade + mixed.sum(axis=0, keepdims=True)
+                block = masked(product, steps, lim, level, row, lanes).reshape(shape)
+                part = prods[row * TILE : (row + 1) * TILE].reshape(shape)
+                top = jnp.maximum(high, block.max(axis=0) * (SCALE * LOG2E))
+                base = jnp.maximum(top, FLOOR)
+                weights = jnp.exp2(block * (SCALE * LOG2E) - base[None])
+                fade = jnp.exp2(high - top)
+                total = total * fade + weights.sum(axis=0)
+                mixed = mixed * fade + (weights * part).sum(axis=0)
+                high = top
+            acc[0:8, lanes] = high
+            acc[8:16, lanes] = total
+            acc[16:24, lanes] = mixed
             return carry
 
         lax.fori_loop(scalars[level], SIDE, unit_stats, 0)
+    high = acc[0:8, :].max(axis=0, keepdims=True)
+    fade = jnp.exp2(acc[0:8, :] - high)
+    out[...] = jnp.zeros_like(out)
+    out[0:1, :] = high
+    out[1:2, :] = (acc[8:16, :] * fade).sum(axis=0, keepdims=True)
+    out[2:3, :] = (acc[16:24, :] * fade).sum(axis=0, keepdims=True)
 
 
 def source_grads_kernel(scalars, lim, own, other, mine, theirs, kv0, kv1, kv2, kv3, *refs):
@@ -121,7 +121,7 @@
 
         def unit_grads(unit, carry):
             lanes = unit_lanes(unit)
-            steps = source_steps(scalars, range(SIDE))
+            steps = source_steps(scalars)
             x = unit_rows(own, other, unit, QUERY)
             g = unit_rows(own, other, unit, GRAD)
             scores = dot(source_rows(kvs, level, 0), x, 1, 1) * (SCALE * LOG2E) - shift[0:1, lanes]
@@ -177,22 +177,21 @@
 PARAMS = pltpu.CompilerParams(vmem_limit_bytes=LIMIT)
 
 
-def cost(chunks, dots):
-    flops = 10 * len(chunks) * dots * 2 * PIECE * SIDE * WIDE * DIM
+def cost(dots):
+    flops = 10 * dots * 2 * WIDE * WIDE * DIM
     return pl.CostEstimate(flops=flops, bytes_accessed=2**20, transcendentals=0)
 
 
-def row_stats(chunks, scalars, lim, own, other, kvs, previous):
-    operands = [scalars, lim, own, other] + [kvs[c] for c in chunks]
-    if previous is not None:
-        operands.append(previous)
-    return pl.pallas_call(
-        functools.partial(stats_kernel, chunks, previous is None),
+def row_stats(scalars, lim, own, other, kvs):
+    operands = (scalars, lim, own, other, *kvs)
+    return pl.pallas_call(
+        stats_kernel,
         out_shape=jax.ShapeDtypeStruct((8, ROWS), jnp.float32),
         in_specs=[SMEM] + [VMEM] * (len(operands) - 1),
         out_specs=VMEM,
-        compiler_params=PARAMS,
-        cost_estimate=cost(chunks, 4),
+        scratch_shapes=[pltpu.VMEM((24, ROWS), jnp.float32)],
+        compiler_params=PARAMS,
+        cost_estimate=cost(4),
         name="stats",
     )(*operands)
 
@@ -213,7 +212,7 @@
             pltpu.VMEM((WIDE, DIM), jnp.float32),
         ],
         compiler_params=PARAMS,
-        cost_estimate=cost((0, 1, 2, 3), 4),
+        cost_estimate=cost(4),
         name="source_grads",
     )(*operands)
 
@@ -227,7 +226,7 @@
         out_specs=[VMEM] * 2,
         scratch_shapes=[pltpu.VMEM((ROWS, DIM), jnp.float32)],
         compiler_params=PARAMS,
-        cost_estimate=cost((0, 1, 2, 3), 1),
+        cost_estimate=cost(1),
         name="query_grads",
     )(scalars, *kvs, lows)
 
@@ -243,25 +242,24 @@
     )(sums, keep, returned)
 
 
-def gather_kernel(*refs):
+def by_head_kernel(*refs):
     out = refs[-1]
-    for tile in range(TILES):
-        low = 0
-        for ref in refs[:-1]:
-            high = low + ref.shape[0]
+    low = 0
+    for ref in refs[:-1]:
+        high = low + ref.shape[0]
+        for tile in range(TILES):
             wide = ref.shape[1] > DIM
             out[tile, low:high, :] = ref[:, tile * DIM : (tile + 1) * DIM] if wide else ref[...]
-            low = high
+        low = high
 
 
 def by_head(*arrays):
     rows = sum(a.shape[0] for a in arrays)
     return pl.pallas_call(
-        gather_kernel,
+        by_head_kernel,
         out_shape=jax.ShapeDtypeStruct((TILES, rows, DIM), jnp.bfloat16),
         in_specs=[VMEM] * len(arrays),
         out_specs=VMEM,
-        compiler_params=PARAMS,
         name="by_head",
     )(*arrays)
 
@@ -344,7 +342,7 @@
     lim = lim.reshape(TILES, ROWS)
 
     common = (scalars, lim, own, other)
-    mine = row_stats((0, 1, 2, 3), *common, kvs, None)
+    mine = row_stats(*common, kvs)
     theirs = swap_cores(mine)
     common += (mine, theirs, kvs)
     part0, part1, part2, part3, lows = source_grads(*common)

time: 98.6 us -> 96.4 us (0.978); the launches traced: 97.2 us -> 96.1 us
  local copies, waits for them, and re-layouts: 6.1 us -> 2.4 us
  starting transfers between devices: 27.6 us -> 24.8 us
  waiting for transfers between devices: 23.4 us -> 25.4 us
  blocking collectives: 15.7 us -> 17.5 us
  Pallas kernels: 22.1 us -> 23.3 us
    unnamed x9 -> x1, local copies, waits for them, and re-layouts: 3.9 us -> 0.2 us
    ppermute x6, starting transfers between devices: 13.6 us -> 10.8 us  [along(): return lax.ppermute(a, 'tgt', [(i, target(i)) for i in range(TILES)])]
    all_to_all x1, blocking collectives: 15.7 us -> 17.5 us  [exchange(): lax.all_to_all(a, ('tgt', 'src'), 0, 0, axis_index_groups=GROUPS, tiled=T...]
    ppermute x6, waiting for transfers between devices: 6.67 us -> 8.34 us  [along(): return lax.ppermute(a, 'tgt', [(i, target(i)) for i in range(TILES)])]
    pallas_call x3, Pallas kernels: 8.08 us -> 9.32 us  [the longest x1 5.66 us: row_stats(): pl.pallas_call(stats_kernel, out_shape=jax.ShapeDtypeStruct((8, ROWS), jn...]
  transfers between devices with their start and end apart: 11 -> 11, of which waited for: 7 -> 7; matrix products, arithmetic and copies ran while one was open for 4% -> 5% of each run, Pallas kernels for 5% -> 6%
where the time goes in v3:
time: 96.4 us; the launch traced here: 96.1 us
  waiting for transfers between devices  25.4 us (26%)
  starting transfers between devices  24.8 us (26%)
  Pallas kernels  23.3 us (24%)
  blocking collectives  17.5 us (18%)
  local copies, waits for them, and re-layouts  2.4 us (2%)
  other arithmetic  2.01 us (2%)
    all_to_all x1, blocking collectives, exchange(): lax.all_to_all(a, ('tgt', 'src'), 0, 0, axis_index_groups=GROUPS, tiled=T...  17.5 us
    all_to_all x2, waiting for transfers between devices, exchange(): lax.all_to_all(a, ('tgt', 'src'), 0, 0, axis_index_groups=GROUPS, tiled=T...  14.1 us
    all_to_all x2, starting transfers between devices, exchange(): lax.all_to_all(a, ('tgt', 'src'), 0, 0, axis_index_groups=GROUPS, tiled=T...  13.8 us
    ppermute x6, starting transfers between devices, along(): return lax.ppermute(a, 'tgt', [(i, target(i)) for i in range(TILES)])  10.8 us
    pallas_call x1, Pallas kernels, source_grads(): pl.pallas_call(source_grads_kernel, out_shape=[piece] * SIDE + [lows], in...  8.73 us
    ppermute x6, waiting for transfers between devices, along(): return lax.ppermute(a, 'tgt', [(i, target(i)) for i in range(TILES)])  8.34 us
    pallas_call x1, Pallas kernels, row_stats(): pl.pallas_call(stats_kernel, out_shape=jax.ShapeDtypeStruct((8, ROWS), jn...  5.66 us
    pallas_call x1, Pallas kernels, query_grads(): pl.pallas_call(query_grads_kernel, out_shape=[jax.ShapeDtypeStruct(shape,...  4.24 us
  transfers between devices with their start and end apart: 11, of which 7 were waited for; matrix products, arithmetic and copies ran while one was open for 5% of the time, Pallas kernels for 6%

profile of v3, /device:TPU:32, one launch (start us, length us, event | category | flops | bytes accessed | tf_op | source)
XLA Modules:
  0.0 96.1 jit_solution(18065285725660862477)
XLA Ops:
  0.6 1.7 %by_head.3 = bf16[16,64,128]{2,1,0:T(8,128)(2,1)} custom-call(bf16[32,2048]{1,0:T(8,128)(2,1)} %refs_0_.3, bf16[32,2048]{1,0:T(8,128)(2,1)} %refs_1_.3), custom_call_target="tpu_custom_call" | custom-call | tf_op jit(solution)/shard_map/by_head/pallas_call | solution.py:258
  2.3 8.7 %all-to-all-start.1 = ((bf16[16,64,128]{2,1,0:T(8,128)(2,1)}), bf16[16,64,128]{2,1,0:T(8,128)(2,1)S(1)}, u32[]{:S(2)}, u32[]{:S(2)}) async-start(bf16[16,64,128]{2,1,0:T(8,128)(2,1)} %by_head.3), calls=%async_computation.1 | async-start | bytes 524288 | tf_op jit(solution)/shard_map/all_to_all | solution.py:299
  11.0 0.8 convert_bitcast_fusion
  11.8 0.6 fusion.4.refs_2_
  12.4 1.9 %by_head.2 = bf16[16,144,128]{2,1,0:T(8,128)(2,1)} custom-call(bf16[64,2048]{1,0:T(8,128)(2,1)} %refs_0_.2, bf16[64,2048]{1,0:T(8,128)(2,1)} %refs_1_.2, bf16[16,128]{1,0:T(8,128)(2,1)} %fusion.4.refs_2_), custom_call_target="tpu_custom_call" | custom-call | tf_op jit(solution)/shard_map/by_head/pallas_call | solution.py:258
  14.3 6.0 %all-to-all-done.1.kv0 = bf16[16,64,128]{2,1,0:T(8,128)(2,1)S(1)} async-done(((bf16[16,64,128]{2,1,0:T(8,128)(2,1)}), bf16[16,64,128]{2,1,0:T(8,128)(2,1)S(1)}, u32[]{:S(2)}, u32[]{:S(2)}) %all-to-all-start.1) | async-done | bytes 262176 | tf_op jit(solution)/shard_map/all_to_all | solution.py:299
  20.3 5.1 %all-to-all-start = ((bf16[16,144,128]{2,1,0:T(8,128)(2,1)}), bf16[16,144,128]{2,1,0:T(8,128)(2,1)S(1)}, u32[]{:S(2)}, u32[]{:S(2)}) async-start(bf16[16,144,128]{2,1,0:T(8,128)(2,1)} %by_head.2), calls=%async_computation | async-start | bytes 1179648 | tf_op jit(solution)/shard_map/all_to_all | solution.py:299
  25.7 1.1 %reshape.73 = s32[4,4,4,4,2,4]{2,1,0,5,4,3:T(4,128)S(1)} reshape(s32[64,32]{0,1:T(8,128)} %param.11) | data formatting | bytes 16384 | tf_op jit(solution)/shard_map/reshape | solution.py:338
  26.8 0.2 copy.19
  27.0 0.2 copy.15
  27.3 0.1 broadcast_in_dim.29
  27.5 0.1 slice_reduce_fusion.1
  27.7 3.1 %collective-permute-start.3 = (bf16[16,64,128]{2,1,0:T(8,128)(2,1)S(1)}, bf16[16,64,128]{2,1,0:T(8,128)(2,1)S(1)}, u32[]{:S(2)}, u32[]{:S(2)}) collective-permute-start(bf16[16,64,128]{2,1,0:T(8,128)(2,1)S(1)} %all-to-all-done.1.kv0), channel_id=1, source_target_pairs={{0,32},{16,48},{32,0},{48,16},{64,96},{80,112},{96,64},{112,80},{1... | collective-permute-start | bytes 786440 | tf_op jit(solution)/shard_map/ppermute | solution.py:310
  30.8 1.1 %collective-permute-start.2 = (bf16[16,64,128]{2,1,0:T(8,128)(2,1)S(1)}, bf16[16,64,128]{2,1,0:T(8,128)(2,1)S(1)}, u32[]{:S(2)}, u32[]{:S(2)}) collective-permute-start(bf16[16,64,128]{2,1,0:T(8,128)(2,1)S(1)} %all-to-all-done.1.kv0), channel_id=1, source_target_pairs={{0,48},{16,0},{32,16},{48,32},{64,112},{80,64},{96,80},{112,96},{1... | collective-permute-start | bytes 786440 | tf_op jit(solution)/shard_map/ppermute | solution.py:310
  31.9 0.9 collective-permute-start.1
  32.8 8.0 %all-to-all-done.own = bf16[16,144,128]{2,1,0:T(8,128)(2,1)S(1)} async-done(((bf16[16,144,128]{2,1,0:T(8,128)(2,1)}), bf16[16,144,128]{2,1,0:T(8,128)(2,1)S(1)}, u32[]{:S(2)}, u32[]{:S(2)}) %all-to-all-start) | async-done | bytes 589856 | tf_op jit(solution)/shard_map/all_to_all | solution.py:299
  40.9 0.2 slice_reduce_fusion
  41.1 0.2 convert_reduce_fusion
  41.6 0.1 collective-permute-done.2.kv2
  41.7 1.7 %collective-permute-done.other = bf16[16,144,128]{2,1,0:T(8,128)(2,1)S(1)} collective-permute-done((bf16[16,144,128]{2,1,0:T(8,128)(2,1)S(1)}, bf16[16,144,128]{2,1,0:T(8,128)(2,1)S(1)}, u32[]{:S(2)}, u32[]{:S(2)}) %collective-permute-start) | collective-permute-done | bytes 589856 | tf_op jit(solution)/shard_map/ppermute | solution.py:303
  43.4 5.7 %stats.1.mine = f32[8,2048]{1,0:T(8,128)S(1)} custom-call(s32[8]{0:T(128)S(1)} %concatenate.12.scalars, s32[16,2048]{1,0:T(8,128)S(1)} %select_subtract_fusion.lim, bf16[16,144,128]{2,1,0:T(8,128)(2,1)S(1)} %all-to-all-done.own, bf16[16,144,128]{2,1,0:T(8,128)(2,1)S(1)} %collective-permute-done.other, bf16[16,64,128]{2,1,0:T(8,128)(2,1)S(1)} %all-to-all-done.1.kv0, ...), custom_call_target="tpu_custom_call" | custom-call | flops 2684354560 | bytes 1048576 | tf_op jit(solution)/shard_map/stats/pallas_call | solution.py:187
  49.1 0.1 collective-permute-start.4
  49.2 1.2 %collective-permute-done.4.theirs = f32[8,2048]{1,0:T(8,128)S(1)} collective-permute-done((f32[8,2048]{1,0:T(8,128)S(1)}, f32[8,2048]{1,0:T(8,128)S(1)}, u32[]{:S(2)}, u32[]{:S(2)}) %collective-permute-start.4) | collective-permute-done | bytes 65568 | tf_op jit(solution)/shard_map/ppermute | solution.py:303
  50.4 8.7 %source_grads.1 = (bf16[16,64,128]{2,1,0:T(8,128)(2,1)S(1)}, bf16[16,64,128]{2,1,0:T(8,128)(2,1)S(1)}, bf16[16,64,128]{2,1,0:T(8,128)(2,1)S(1)}, bf16[16,64,128]...) custom-call(s32[8]{0:T(128)S(1)} %concatenate.12.scalars, s32[16,2048]{1,0:T(8,128)S(1)} %select_subtract_fusion.lim, ...), custom_call_target="tpu_custom_call" | custom-call | flops 2684354560 | bytes 1048576 | tf_op jit(solution)/shard_map/source_grads/pallas_call | solution.py:203
  59.2 4.1 %collective-permute-start.5 = (bf16[16,64,128]{2,1,0:T(8,128)(2,1)S(1)}, bf16[16,64,128]{2,1,0:T(8,128)(2,1)S(1)}, u32[]{:S(2)}, u32[]{:S(2)}) collective-permute-start(bf16[16,64,128]{2,1,0:T(8,128)(2,1)S(1)} %get-tuple-element.14), channel_id=1, source_target_pairs={{0,48},{16,0},{32,16},{48,32},{64,112},{80,64},{96,80},{112,96},{1... | collective-permute-start | bytes 786440 | tf_op jit(solution)/shard_map/ppermute | solution.py:310
  63.3 1.6 %collective-permute-start.7 = (bf16[16,64,128]{2,1,0:T(8,128)(2,1)S(1)}, bf16[16,64,128]{2,1,0:T(8,128)(2,1)S(1)}, u32[]{:S(2)}, u32[]{:S(2)}) collective-permute-start(bf16[16,64,128]{2,1,0:T(8,128)(2,1)S(1)} %get-tuple-element.16), channel_id=1, source_target_pairs={{0,32},{16,48},{32,0},{48,16},{64,96},{80,112},{96,64},{112,80},{1... | collective-permute-start | bytes 786440 | tf_op jit(solution)/shard_map/ppermute | solution.py:310
  64.8 4.2 %query_grads.1 = (f32[16,64,128]{2,1,0:T(8,128)S(1)}, bf16[16,64,128]{2,1,0:T(8,128)(2,1)S(1)}) custom-call(s32[8]{0:T(128)S(1)} %concatenate.12.scalars, bf16[16,64,128]{2,1,0:T(8,128)(2,1)S(1)} %all-to-all-done.1.kv0, bf16[16,64,128]{2,1,0:T(8,128)(2,1)S(1)} %collective-permute-done.1.kv1, bf16[16,64,128]{2,1,0:T(8,128)(2,1)S(1)} %collective-permute-done.2.kv2, ...), custom_call_target="tpu_custom_call" | custom-call | flops 671088640 | bytes 1048576 | tf_op jit(solution)/shard_map/query_grads/pallas_call | solution.py:222
  69.2 4.8 %collective-permute-done.5 = bf16[16,64,128]{2,1,0:T(8,128)(2,1)S(1)} collective-permute-done((bf16[16,64,128]{2,1,0:T(8,128)(2,1)S(1)}, bf16[16,64,128]{2,1,0:T(8,128)(2,1)S(1)}, u32[]{:S(2)}, u32[]{:S(2)}) %collective-permute-start.5) | collective-permute-done | bytes 262176 | tf_op jit(solution)/shard_map/ppermute | solution.py:310
  74.0 3.4 %collective-permute-done.6 = bf16[16,64,128]{2,1,0:T(8,128)(2,1)S(1)} collective-permute-done((bf16[16,64,128]{2,1,0:T(8,128)(2,1)S(1)}, bf16[16,64,128]{2,1,0:T(8,128)(2,1)S(1)}, u32[]{:S(2)}, u32[]{:S(2)}) %collective-permute-start.6) | collective-permute-done | bytes 262176 | tf_op jit(solution)/shard_map/ppermute | solution.py:310
  77.4 0.2 add_convert_fusion.sums
  77.7 17.5 %all_to_all.15.heads = bf16[16,128,128]{2,1,0:T(8,128)(2,1)S(1)} all-to-all(bf16[16,128,128]{2,1,0:T(8,128)(2,1)S(1)} %pack.1), channel_id=1, replica_groups={{0,64,128,192,4,68,132,196,8,72,136,200,12,76,140,204},{2,66,130,194,6,..., dimensions={0} | all-to-all | bytes 1048576 | tf_op jit(solution)/shard_map/all_to_all | solution.py:299
  95.2 0.9 by_row.1
  (26 shorter events, 1.0 us)
Async XLA Ops:
  2.3 18.0 %all-to-all-start.1 = ((bf16[16,64,128]{2,1,0:T(8,128)(2,1)}), bf16[16,64,128]{2,1,0:T(8,128)(2,1)S(1)}, u32[]{:S(2)}, u32[]{:S(2)}) async-start(bf16[16,64,128]{2,1,0:T(8,128)(2,1)} %by_head.3), calls=%async_computation.1 | async-start | bytes 524288 | tf_op jit(solution)/shard_map/all_to_all | solution.py:299
  20.3 20.5 %all-to-all-start = ((bf16[16,144,128]{2,1,0:T(8,128)(2,1)}), bf16[16,144,128]{2,1,0:T(8,128)(2,1)S(1)}, u32[]{:S(2)}, u32[]{:S(2)}) async-start(bf16[16,144,128]{2,1,0:T(8,128)(2,1)} %by_head.2), calls=%async_computation | async-start | bytes 1179648 | tf_op jit(solution)/shard_map/all_to_all | solution.py:299
  27.7 13.9 %collective-permute-start.3 = (bf16[16,64,128]{2,1,0:T(8,128)(2,1)S(1)}, bf16[16,64,128]{2,1,0:T(8,128)(2,1)S(1)}, u32[]{:S(2)}, u32[]{:S(2)}) collective-permute-start(bf16[16,64,128]{2,1,0:T(8,128)(2,1)S(1)} %all-to-all-done.1.kv0), channel_id=1, source_target_pairs={{0,32},{16,48},{32,0},{48,16},{64,96},{80,112},{96,64},{112,80},{1... | collective-permute-start | bytes 786440 | tf_op jit(solution)/shard_map/ppermute | solution.py:310
  30.8 10.9 %collective-permute-start.2 = (bf16[16,64,128]{2,1,0:T(8,128)(2,1)S(1)}, bf16[16,64,128]{2,1,0:T(8,128)(2,1)S(1)}, u32[]{:S(2)}, u32[]{:S(2)}) collective-permute-start(bf16[16,64,128]{2,1,0:T(8,128)(2,1)S(1)} %all-to-all-done.1.kv0), channel_id=1, source_target_pairs={{0,48},{16,0},{32,16},{48,32},{64,112},{80,64},{96,80},{112,96},{1... | collective-permute-start | bytes 786440 | tf_op jit(solution)/shard_map/ppermute | solution.py:310
  31.9 9.8 %collective-permute-start.1 = (bf16[16,64,128]{2,1,0:T(8,128)(2,1)S(1)}, bf16[16,64,128]{2,1,0:T(8,128)(2,1)S(1)}, u32[]{:S(2)}, u32[]{:S(2)}) collective-permute-start(bf16[16,64,128]{2,1,0:T(8,128)(2,1)S(1)} %all-to-all-done.1.kv0), channel_id=1, source_target_pairs={{0,16},{16,32},{32,48},{48,0},{64,80},{80,96},{96,112},{112,64},{1... | collective-permute-start | bytes 786440 | tf_op jit(solution)/shard_map/ppermute | solution.py:310
  41.4 2.0 %collective-permute-start = (bf16[16,144,128]{2,1,0:T(8,128)(2,1)S(1)}, bf16[16,144,128]{2,1,0:T(8,128)(2,1)S(1)}, u32[]{:S(2)}, u32[]{:S(2)}) collective-permute-start(bf16[16,144,128]{2,1,0:T(8,128)(2,1)S(1)} %all-to-all-done.own), channel_id=1, source_target_pairs={{0,2},{2,0},{4,6},{6,4},{8,10},{10,8},{12,14},{14,12},{1,3},{3,1},... | collective-permute-start | bytes 1769480 | tf_op jit(solution)/shard_map/ppermute | solution.py:303
  49.1 1.3 %collective-permute-start.4 = (f32[8,2048]{1,0:T(8,128)S(1)}, f32[8,2048]{1,0:T(8,128)S(1)}, u32[]{:S(2)}, u32[]{:S(2)}) collective-permute-start(f32[8,2048]{1,0:T(8,128)S(1)} %stats.1.mine), channel_id=1, source_target_pairs={{0,2},{2,0},{4,6},{6,4},{8,10},{10,8},{12,14},{14,12},{1,3},{3,1},... | collective-permute-start | bytes 196616 | tf_op jit(solution)/shard_map/ppermute | solution.py:303
  59.2 14.8 %collective-permute-start.5 = (bf16[16,64,128]{2,1,0:T(8,128)(2,1)S(1)}, bf16[16,64,128]{2,1,0:T(8,128)(2,1)S(1)}, u32[]{:S(2)}, u32[]{:S(2)}) collective-permute-start(bf16[16,64,128]{2,1,0:T(8,128)(2,1)S(1)} %get-tuple-element.14), channel_id=1, source_target_pairs={{0,48},{16,0},{32,16},{48,32},{64,112},{80,64},{96,80},{112,96},{1... | collective-permute-start | bytes 786440 | tf_op jit(solution)/shard_map/ppermute | solution.py:310
  63.3 14.1 %collective-permute-start.6 = (bf16[16,64,128]{2,1,0:T(8,128)(2,1)S(1)}, bf16[16,64,128]{2,1,0:T(8,128)(2,1)S(1)}, u32[]{:S(2)}, u32[]{:S(2)}) collective-permute-start(bf16[16,64,128]{2,1,0:T(8,128)(2,1)S(1)} %get-tuple-element.15), channel_id=1, source_target_pairs={{0,16},{16,32},{32,48},{48,0},{64,80},{80,96},{96,112},{112,64},{1... | collective-permute-start | bytes 786440 | tf_op jit(solution)/shard_map/ppermute | solution.py:310
  63.3 14.1 %collective-permute-start.7 = (bf16[16,64,128]{2,1,0:T(8,128)(2,1)S(1)}, bf16[16,64,128]{2,1,0:T(8,128)(2,1)S(1)}, u32[]{:S(2)}, u32[]{:S(2)}) collective-permute-start(bf16[16,64,128]{2,1,0:T(8,128)(2,1)S(1)} %get-tuple-element.16), channel_id=1, source_target_pairs={{0,32},{16,48},{32,0},{48,16},{64,96},{80,112},{96,64},{112,80},{1... | collective-permute-start | bytes 786440 | tf_op jit(solution)/shard_map/ppermute | solution.py:310
  69.1 8.5 %collective-permute-start.8 = (bf16[16,64,128]{2,1,0:T(8,128)(2,1)S(1)}, bf16[16,64,128]{2,1,0:T(8,128)(2,1)S(1)}, u32[]{:S(2)}, u32[]{:S(2)}) collective-permute-start(bf16[16,64,128]{2,1,0:T(8,128)(2,1)S(1)} %get-tuple-element.19), channel_id=1, source_target_pairs={{0,2},{2,0},{4,6},{6,4},{8,10},{10,8},{12,14},{14,12},{1,3},{3,1},... | collective-permute-start | bytes 786440 | tf_op jit(solution)/shard_map/ppermute | solution.py:303

commit v4 on v3

--- a/solution.py
+++ b/solution.py
@@ -12,6 +12,7 @@
 SIDE = 4
 TILES = SIDE * SIDE
 WIDE = SIDE * TILE
+PART = WIDE // 2
 ROWS = TILES * TILE
 HALF = TILE // 2
 PIECE = 32
@@ -22,7 +23,7 @@
 FLOOR = -1e29
 SCALE = float(DIM) ** -0.5
 LOG2E = 1.4426950408889634
-LIMIT = 32 * 1024 * 1024
+LIMIT = 8 * 1024 * 1024
 
 
 def dot(a, b, left, right):
@@ -38,9 +39,9 @@
     return jnp.concatenate(parts, axis=0)
 
 
-def source_rows(kvs, level, low):
+def source_rows(kvs, level, low, count=SIDE):
     parts = []
-    for row in range(SIDE):
+    for row in range(count):
         for kv in kvs:
             parts.append(kv[SIDE * level + row, low : low + PIECE, :])
     return jnp.concatenate(parts, axis=0)
@@ -60,39 +61,46 @@
     return pl.ds(pl.multiple_of(unit * WIDE, WIDE), WIDE)
 
 
-def stats_kernel(scalars, lim, own, other, kv0, kv1, kv2, kv3, out, acc):
+def for_units(scalars, level, body):
+    first, whole = scalars[level], scalars[2 * SIDE + level]
+    lax.fori_loop(first, whole, functools.partial(body, 1), 0)
+    lax.fori_loop(whole, SIDE, functools.partial(body, SIDE), 0)
+
+
+def stats_kernel(scalars, lim, own, other, kv0, kv1, kv2, kv3, out, logits, acc):
     kvs = (kv0, kv1, kv2, kv3)
     acc[...] = jnp.zeros_like(acc)
     acc[0:8, :] = jnp.full((8, ROWS), MASKED, jnp.float32)
     for level in range(SIDE):
 
-        def unit_stats(unit, carry):
+        def unit_stats(count, unit, carry):
             lanes = unit_lanes(unit)
             steps = source_steps(scalars)
             x = unit_rows(own, other, unit, QUERY)
             g = unit_rows(own, other, unit, GRAD)
-            product = dot(source_rows(kvs, level, 0), x, 1, 1)
-            prods = dot(source_rows(kvs, level, PIECE), g, 1, 1)
+            product = dot(source_rows(kvs, level, 0, count), x, 1, 1)
+            mixture = dot(source_rows(kvs, level, PIECE, count), g, 1, 1)
             high = acc[0:8, lanes]
             total = acc[8:16, lanes]
             mixed = acc[16:24, lanes]
             shape = (TILE // 8, 8, WIDE)
-            for row in range(SIDE):
-                block = masked(product, steps, lim, level, row, lanes).reshape(shape)
-                part = prods[row * TILE : (row + 1) * TILE].reshape(shape)
-                top = jnp.maximum(high, block.max(axis=0) * (SCALE * LOG2E))
+            for row in range(count):
+                rows = slice(row * TILE, (row + 1) * TILE)
+                block = masked(product, steps, lim, level, row, lanes) * (SCALE * LOG2E)
+                logits[SIDE * level + unit, rows] = block
+                top = jnp.maximum(high, block.reshape(shape).max(axis=0))
                 base = jnp.maximum(top, FLOOR)
-                weights = jnp.exp2(block * (SCALE * LOG2E) - base[None])
+                weights = jnp.exp2(block.reshape(shape) - base[None])
                 fade = jnp.exp2(high - top)
                 total = total * fade + weights.sum(axis=0)
-                mixed = mixed * fade + (weights * part).sum(axis=0)
+                mixed = mixed * fade + (weights * mixture[rows].reshape(shape)).sum(axis=0)
                 high = top
             acc[0:8, lanes] = high
             acc[8:16, lanes] = total
             acc[16:24, lanes] = mixed
             return carry
 
-        lax.fori_loop(scalars[level], SIDE, unit_stats, 0)
+        for_units(scalars, level, unit_stats)
     high = acc[0:8, :].max(axis=0, keepdims=True)
     fade = jnp.exp2(acc[0:8, :] - high)
     out[...] = jnp.zeros_like(out)
@@ -101,7 +109,9 @@
     out[2:3, :] = (acc[16:24, :] * fade).sum(axis=0, keepdims=True)
 
 
-def source_grads_kernel(scalars, lim, own, other, mine, theirs, kv0, kv1, kv2, kv3, *refs):
+def source_grads_kernel(
+    scalars, own, other, mine, theirs, logits, kv0, kv1, kv2, kv3, *refs
+):
     kvs = (kv0, kv1, kv2, kv3)
     outs, (lows, shift, delta, key_acc, value_acc) = refs[:SIDE], refs[SIDE:]
     for tile in range(TILES):
@@ -119,26 +129,34 @@
         key_acc[...] = jnp.zeros_like(key_acc)
         value_acc[...] = jnp.zeros_like(value_acc)
 
-        def unit_grads(unit, carry):
-            lanes = unit_lanes(unit)
-            steps = source_steps(scalars)
+        def unit_grads(count, unit, carry):
             x = unit_rows(own, other, unit, QUERY)
             g = unit_rows(own, other, unit, GRAD)
-            scores = dot(source_rows(kvs, level, 0), x, 1, 1) * (SCALE * LOG2E) - shift[0:1, lanes]
-            prods = dot(source_rows(kvs, level, PIECE), g, 1, 1) - delta[0:1, lanes]
-            highs = []
-            parts = []
-            for row in range(SIDE):
-                probs = jnp.exp2(masked(scores, steps, lim, level, row, lanes))
-                highs.append(probs.astype(jnp.bfloat16))
-                parts.append((probs * prods[row * TILE : (row + 1) * TILE]).astype(jnp.bfloat16))
-            low = jnp.concatenate(parts, axis=0)
-            lows[SIDE * level + unit] = low
-            value_acc[...] += dot(jnp.concatenate(highs, axis=0), g, 1, 0)
-            key_acc[...] += dot(low, x, 1, 0)
+            values = source_rows(kvs, level, PIECE, count)
+            key_sum = value_sum = 0.0
+            for begin in range(0, WIDE, PART):
+                lanes = pl.ds(pl.multiple_of(unit * WIDE + begin, PART), PART)
+                x_part = x[begin : begin + PART]
+                g_part = g[begin : begin + PART]
+                columns = slice(begin, begin + PART)
+                prods = dot(values, g_part, 1, 1) - delta[0:1, lanes]
+                highs = []
+                parts = []
+                for row in range(count):
+                    rows = slice(row * TILE, (row + 1) * TILE)
+                    block = logits[SIDE * level + unit, rows, columns]
+                    probs = jnp.exp2(block - shift[0:1, lanes])
+                    highs.append(probs.astype(jnp.bfloat16))
+                    parts.append((probs * prods[rows]).astype(jnp.bfloat16))
+                low = jnp.concatenate(parts, axis=0)
+                lows[SIDE * level + unit, : count * TILE, begin : begin + PART] = low
+                value_sum += dot(jnp.concatenate(highs, axis=0), g_part, 1, 0)
+                key_sum += dot(low, x_part, 1, 0)
+            key_acc[: count * TILE] += key_sum
+            value_acc[: count * TILE] += value_sum
             return carry
 
-        lax.fori_loop(scalars[level], SIDE, unit_grads, 0)
+        for_units(scalars, level, unit_grads)
         for row in range(SIDE):
             for index, out in enumerate(outs):
                 begin = row * TILE + index * PIECE
@@ -153,12 +171,12 @@
     acc[...] = jnp.zeros_like(acc)
     for level in range(SIDE):
 
-        def unit_grads(unit, carry):
-            keys = source_rows(kvs, level, 0)
-            acc[unit_lanes(unit), :] += dot(lows[SIDE * level + unit], keys, 0, 0)
+        def unit_grads(count, unit, carry):
+            low = lows[SIDE * level + unit, : count * TILE]
+            acc[unit_lanes(unit), :] += dot(low, source_rows(kvs, level, 0, count), 0, 0)
             return carry
 
-        lax.fori_loop(scalars[level], SIDE, unit_grads, 0)
+        for_units(scalars, level, unit_grads)
     for unit in range(SIDE):
         for level in range(SIDE):
             begin = (SIDE * unit + level) * TILE
@@ -186,9 +204,10 @@
     operands = (scalars, lim, own, other, *kvs)
     return pl.pallas_call(
         stats_kernel,
-        out_shape=jax.ShapeDtypeStruct((8, ROWS), jnp.float32),
+        out_shape=[jax.ShapeDtypeStruct((8, ROWS), jnp.float32)]
+        + [jax.ShapeDtypeStruct((TILES, WIDE, WIDE), jnp.float32)],
         in_specs=[SMEM] + [VMEM] * (len(operands) - 1),
-        out_specs=VMEM,
+        out_specs=[VMEM] * 2,
         scratch_shapes=[pltpu.VMEM((24, ROWS), jnp.float32)],
         compiler_params=PARAMS,
         cost_estimate=cost(4),
@@ -196,10 +215,9 @@
     )(*operands)
 
 
-def source_grads(scalars, lim, own, other, mine, theirs, kvs):
+def source_grads(*operands):
     piece = jax.ShapeDtypeStruct((TILES, 2 * PIECE, DIM), jnp.bfloat16)
     lows = jax.ShapeDtypeStruct((TILES, WIDE, WIDE), jnp.bfloat16)
-    operands = (scalars, lim, own, other, mine, theirs, *kvs)
     return pl.pallas_call(
         source_grads_kernel,
         out_shape=[piece] * SIDE + [lows],
@@ -331,8 +349,9 @@
     )
     tops = reads[TILES - SIDE :, -1]
     first = jnp.sum(tops[None, :] <= begins[:, :1], axis=1)
+    whole = jnp.sum(tops[None, :] <= begins[:, 1:2], axis=1)
     offsets = jnp.stack([(column - k) % SIDE * PIECE for k in (0, 1, 3, 2)])
-    scalars = jnp.concatenate([first, offsets]).astype(jnp.int32)
+    scalars = jnp.concatenate([first, offsets, whole]).astype(jnp.int32)
     ordered = jnp.where(core == 0, reads, jnp.roll(reads, HALF, axis=1))
     ordered = ordered.reshape(SIDE, SIDE, TILE).transpose(1, 0, 2)
     flags = block_mask.reshape(SIDE, SIDE, SIDE, SIDE, 2, SIDE)
@@ -341,11 +360,11 @@
     lim = jnp.where(flags[..., None] == 1, ordered[None, None], 0) - begins[:, :, None, None, None]
     lim = lim.reshape(TILES, ROWS)
 
-    common = (scalars, lim, own, other)
-    mine = row_stats(*common, kvs)
+    mine, logits = row_stats(scalars, lim, own, other, kvs)
     theirs = swap_cores(mine)
-    common += (mine, theirs, kvs)
-    part0, part1, part2, part3, lows = source_grads(*common)
+    part0, part1, part2, part3, lows = source_grads(
+        scalars, own, other, mine, theirs, logits, *kvs
+    )
     got3, got1, got2 = along(part3, 2), along(part1, 3), along(part2, 1)
     keep, send = query_grads(scalars, kvs, lows)
     returned = swap_cores(send)

time: 96.4 us -> 95.6 us (level)
  Pallas kernels: 23.3 us -> 21.9 us
    pallas_call x1, Pallas kernels: 8.73 us -> 7.13 us  [source_grads(): pl.pallas_call(source_grads_kernel, out_shape=[piece] * SIDE + [lows], in...]
  transfers between devices with their start and end apart: 11 -> 11, of which waited for: 7 -> 7; matrix products, arithmetic and copies ran while one was open for 5% -> 5% of each run, Pallas kernels for 6% -> 7%
where the time goes in v4:
time: 95.6 us; the launch traced here: 95.1 us
  waiting for transfers between devices  25.1 us (26%)
  starting transfers between devices  24.9 us (26%)
  Pallas kernels  21.9 us (23%)
  blocking collectives  17.8 us (19%)
  local copies, waits for them, and re-layouts  2.47 us (3%)
  other arithmetic  2.04 us (2%)
    all_to_all x1, blocking collectives, exchange(): lax.all_to_all(a, ('tgt', 'src'), 0, 0, axis_index_groups=GROUPS, tiled=T...  17.8 us
    all_to_all x2, waiting for transfers between devices, exchange(): lax.all_to_all(a, ('tgt', 'src'), 0, 0, axis_index_groups=GROUPS, tiled=T...  14 us
    all_to_all x2, starting transfers between devices, exchange(): lax.all_to_all(a, ('tgt', 'src'), 0, 0, axis_index_groups=GROUPS, tiled=T...  13.8 us
    ppermute x6, starting transfers between devices, along(): return lax.ppermute(a, 'tgt', [(i, target(i)) for i in range(TILES)])  10.9 us
    ppermute x6, waiting for transfers between devices, along(): return lax.ppermute(a, 'tgt', [(i, target(i)) for i in range(TILES)])  8.21 us
    pallas_call x1, Pallas kernels, source_grads(): pl.pallas_call(source_grads_kernel, out_shape=[piece] * SIDE + [lows], in...  7.13 us
    pallas_call x1, Pallas kernels, row_stats(): pl.pallas_call(stats_kernel, out_shape=[jax.ShapeDtypeStruct((8, ROWS), j...  5.85 us
    pallas_call x1, Pallas kernels, query_grads(): pl.pallas_call(query_grads_kernel, out_shape=[jax.ShapeDtypeStruct(shape,...  4.33 us
  transfers between devices with their start and end apart: 11, of which 7 were waited for; matrix products, arithmetic and copies ran while one was open for 5% of the time, Pallas kernels for 7%

profile of v4, /device:TPU:32, one launch (start us, length us, event | category | flops | bytes accessed | tf_op | source)
XLA Modules:
  0.0 95.1 jit_solution(9056500090194299161)
XLA Ops:
  0.6 1.7 %by_head.3 = bf16[16,64,128]{2,1,0:T(8,128)(2,1)} custom-call(bf16[32,2048]{1,0:T(8,128)(2,1)} %refs_0_.3, bf16[32,2048]{1,0:T(8,128)(2,1)} %refs_1_.3), custom_call_target="tpu_custom_call" | custom-call | tf_op jit(solution)/shard_map/by_head/pallas_call | solution.py:276
  2.3 8.7 %all-to-all-start.1 = ((bf16[16,64,128]{2,1,0:T(8,128)(2,1)}), bf16[16,64,128]{2,1,0:T(8,128)(2,1)S(1)}, u32[]{:S(2)}, u32[]{:S(2)}) async-start(bf16[16,64,128]{2,1,0:T(8,128)(2,1)} %by_head.3), calls=%async_computation.1 | async-start | bytes 524288 | tf_op jit(solution)/shard_map/all_to_all | solution.py:317
  11.0 0.8 convert_bitcast_fusion
  11.8 0.6 fusion.4.refs_2_
  12.4 1.9 %by_head.2 = bf16[16,144,128]{2,1,0:T(8,128)(2,1)} custom-call(bf16[64,2048]{1,0:T(8,128)(2,1)} %refs_0_.2, bf16[64,2048]{1,0:T(8,128)(2,1)} %refs_1_.2, bf16[16,128]{1,0:T(8,128)(2,1)} %fusion.4.refs_2_), custom_call_target="tpu_custom_call" | custom-call | tf_op jit(solution)/shard_map/by_head/pallas_call | solution.py:276
  14.3 6.0 %all-to-all-done.1.kv0 = bf16[16,64,128]{2,1,0:T(8,128)(2,1)S(1)} async-done(((bf16[16,64,128]{2,1,0:T(8,128)(2,1)}), bf16[16,64,128]{2,1,0:T(8,128)(2,1)S(1)}, u32[]{:S(2)}, u32[]{:S(2)}) %all-to-all-start.1) | async-done | bytes 262176 | tf_op jit(solution)/shard_map/all_to_all | solution.py:317
  20.3 5.1 %all-to-all-start = ((bf16[16,144,128]{2,1,0:T(8,128)(2,1)}), bf16[16,144,128]{2,1,0:T(8,128)(2,1)S(1)}, u32[]{:S(2)}, u32[]{:S(2)}) async-start(bf16[16,144,128]{2,1,0:T(8,128)(2,1)} %by_head.2), calls=%async_computation | async-start | bytes 1179648 | tf_op jit(solution)/shard_map/all_to_all | solution.py:317
  25.7 1.1 %reshape.73 = s32[4,4,4,4,2,4]{2,1,0,5,4,3:T(4,128)S(1)} reshape(s32[64,32]{0,1:T(8,128)} %param.11) | data formatting | bytes 16384 | tf_op jit(solution)/shard_map/reshape | solution.py:357
  26.8 0.2 copy.19
  27.0 0.2 copy.15
  27.3 0.1 broadcast_in_dim.29
  27.5 0.2 slice_reduce_fusion.1
  27.7 3.1 %collective-permute-start.3 = (bf16[16,64,128]{2,1,0:T(8,128)(2,1)S(1)}, bf16[16,64,128]{2,1,0:T(8,128)(2,1)S(1)}, u32[]{:S(2)}, u32[]{:S(2)}) collective-permute-start(bf16[16,64,128]{2,1,0:T(8,128)(2,1)S(1)} %all-to-all-done.1.kv0), channel_id=1, source_target_pairs={{0,32},{16,48},{32,0},{48,16},{64,96},{80,112},{96,64},{112,80},{1... | collective-permute-start | bytes 786440 | tf_op jit(solution)/shard_map/ppermute | solution.py:328
  30.8 1.1 %collective-permute-start.2 = (bf16[16,64,128]{2,1,0:T(8,128)(2,1)S(1)}, bf16[16,64,128]{2,1,0:T(8,128)(2,1)S(1)}, u32[]{:S(2)}, u32[]{:S(2)}) collective-permute-start(bf16[16,64,128]{2,1,0:T(8,128)(2,1)S(1)} %all-to-all-done.1.kv0), channel_id=1, source_target_pairs={{0,48},{16,0},{32,16},{48,32},{64,112},{80,64},{96,80},{112,96},{1... | collective-permute-start | bytes 786440 | tf_op jit(solution)/shard_map/ppermute | solution.py:328
  32.0 0.9 collective-permute-start.1
  32.9 8.0 %all-to-all-done.own = bf16[16,144,128]{2,1,0:T(8,128)(2,1)S(1)} async-done(((bf16[16,144,128]{2,1,0:T(8,128)(2,1)}), bf16[16,144,128]{2,1,0:T(8,128)(2,1)S(1)}, u32[]{:S(2)}, u32[]{:S(2)}) %all-to-all-start) | async-done | bytes 589856 | tf_op jit(solution)/shard_map/all_to_all | solution.py:317
  40.9 0.2 slice_reduce_fusion
  41.1 0.2 convert_reduce_fusion
  41.6 0.1 collective-permute-done.2.kv2
  41.8 1.7 %collective-permute-done.other = bf16[16,144,128]{2,1,0:T(8,128)(2,1)S(1)} collective-permute-done((bf16[16,144,128]{2,1,0:T(8,128)(2,1)S(1)}, bf16[16,144,128]{2,1,0:T(8,128)(2,1)S(1)}, u32[]{:S(2)}, u32[]{:S(2)}) %collective-permute-start) | collective-permute-done | bytes 589856 | tf_op jit(solution)/shard_map/ppermute | solution.py:321
  43.5 5.8 %stats.1 = (f32[8,2048]{1,0:T(8,128)S(1)}, f32[16,512,512]{2,1,0:T(8,128)S(1)}) custom-call(s32[12]{0:T(128)S(1)} %concatenate.12.scalars, s32[16,2048]{1,0:T(8,128)S(1)} %select_subtract_fusion.lim, bf16[16,144,128]{2,1,0:T(8,128)(2,1)S(1)} %all-to-all-done.own, bf16[16,144,128]{2,1,0:T(8,128)(2,1)S(1)} %collective-permute-done.other, ...), custom_call_target="tpu_custom_call" | custom-call | flops 2684354560 | bytes 1048576 | tf_op jit(solution)/shard_map/stats/pallas_call | solution.py:205
  49.3 0.1 collective-permute-start.4
  49.4 1.2 %collective-permute-done.4.theirs = f32[8,2048]{1,0:T(8,128)S(1)} collective-permute-done((f32[8,2048]{1,0:T(8,128)S(1)}, f32[8,2048]{1,0:T(8,128)S(1)}, u32[]{:S(2)}, u32[]{:S(2)}) %collective-permute-start.4) | collective-permute-done | bytes 65568 | tf_op jit(solution)/shard_map/ppermute | solution.py:321
  50.7 7.1 %source_grads.1 = (bf16[16,64,128]{2,1,0:T(8,128)(2,1)S(1)}, bf16[16,64,128]{2,1,0:T(8,128)(2,1)S(1)}, bf16[16,64,128]{2,1,0:T(8,128)(2,1)S(1)}, bf16[16,64,128]...) custom-call(s32[12]{0:T(128)S(1)} %concatenate.12.scalars, bf16[16,144,128]{2,1,0:T(8,128)(2,1)S(1)} %all-to-all-done.own, ...), custom_call_target="tpu_custom_call" | custom-call | flops 2684354560 | bytes 1048576 | tf_op jit(solution)/shard_map/source_grads/pallas_call | solution.py:221
  57.8 4.0 %collective-permute-start.5 = (bf16[16,64,128]{2,1,0:T(8,128)(2,1)S(1)}, bf16[16,64,128]{2,1,0:T(8,128)(2,1)S(1)}, u32[]{:S(2)}, u32[]{:S(2)}) collective-permute-start(bf16[16,64,128]{2,1,0:T(8,128)(2,1)S(1)} %get-tuple-element.18), channel_id=1, source_target_pairs={{0,48},{16,0},{32,16},{48,32},{64,112},{80,64},{96,80},{112,96},{1... | collective-permute-start | bytes 786440 | tf_op jit(solution)/shard_map/ppermute | solution.py:328
  61.8 1.7 %collective-permute-start.7 = (bf16[16,64,128]{2,1,0:T(8,128)(2,1)S(1)}, bf16[16,64,128]{2,1,0:T(8,128)(2,1)S(1)}, u32[]{:S(2)}, u32[]{:S(2)}) collective-permute-start(bf16[16,64,128]{2,1,0:T(8,128)(2,1)S(1)} %get-tuple-element.20), channel_id=1, source_target_pairs={{0,32},{16,48},{32,0},{48,16},{64,96},{80,112},{96,64},{112,80},{1... | collective-permute-start | bytes 786440 | tf_op jit(solution)/shard_map/ppermute | solution.py:328
  63.5 4.3 %query_grads.1 = (f32[16,64,128]{2,1,0:T(8,128)S(1)}, bf16[16,64,128]{2,1,0:T(8,128)(2,1)S(1)}) custom-call(s32[12]{0:T(128)S(1)} %concatenate.12.scalars, bf16[16,64,128]{2,1,0:T(8,128)(2,1)S(1)} %all-to-all-done.1.kv0, bf16[16,64,128]{2,1,0:T(8,128)(2,1)S(1)} %collective-permute-done.1.kv1, bf16[16,64,128]{2,1,0:T(8,128)(2,1)S(1)} %collective-permute-done.2.kv2, ...), custom_call_target="tpu_custom_call" | custom-call | flops 671088640 | bytes 1048576 | tf_op jit(solution)/shard_map/query_grads/pallas_call | solution.py:240
  68.0 4.7 %collective-permute-done.5 = bf16[16,64,128]{2,1,0:T(8,128)(2,1)S(1)} collective-permute-done((bf16[16,64,128]{2,1,0:T(8,128)(2,1)S(1)}, bf16[16,64,128]{2,1,0:T(8,128)(2,1)S(1)}, u32[]{:S(2)}, u32[]{:S(2)}) %collective-permute-start.5) | collective-permute-done | bytes 262176 | tf_op jit(solution)/shard_map/ppermute | solution.py:328
  72.6 3.4 %collective-permute-done.6 = bf16[16,64,128]{2,1,0:T(8,128)(2,1)S(1)} collective-permute-done((bf16[16,64,128]{2,1,0:T(8,128)(2,1)S(1)}, bf16[16,64,128]{2,1,0:T(8,128)(2,1)S(1)}, u32[]{:S(2)}, u32[]{:S(2)}) %collective-permute-start.6) | collective-permute-done | bytes 262176 | tf_op jit(solution)/shard_map/ppermute | solution.py:328
  76.1 0.2 add_convert_fusion.sums
  76.3 17.8 %all_to_all.15.heads = bf16[16,128,128]{2,1,0:T(8,128)(2,1)S(1)} all-to-all(bf16[16,128,128]{2,1,0:T(8,128)(2,1)S(1)} %pack.1), channel_id=1, replica_groups={{0,64,128,192,4,68,132,196,8,72,136,200,12,76,140,204},{2,66,130,194,6,..., dimensions={0} | all-to-all | bytes 1048576 | tf_op jit(solution)/shard_map/all_to_all | solution.py:317
  94.2 0.9 by_row.1
  (26 shorter events, 1.0 us)
Async XLA Ops:
  2.3 18.0 %all-to-all-start.1 = ((bf16[16,64,128]{2,1,0:T(8,128)(2,1)}), bf16[16,64,128]{2,1,0:T(8,128)(2,1)S(1)}, u32[]{:S(2)}, u32[]{:S(2)}) async-start(bf16[16,64,128]{2,1,0:T(8,128)(2,1)} %by_head.3), calls=%async_computation.1 | async-start | bytes 524288 | tf_op jit(solution)/shard_map/all_to_all | solution.py:317
  20.3 20.5 %all-to-all-start = ((bf16[16,144,128]{2,1,0:T(8,128)(2,1)}), bf16[16,144,128]{2,1,0:T(8,128)(2,1)S(1)}, u32[]{:S(2)}, u32[]{:S(2)}) async-start(bf16[16,144,128]{2,1,0:T(8,128)(2,1)} %by_head.2), calls=%async_computation | async-start | bytes 1179648 | tf_op jit(solution)/shard_map/all_to_all | solution.py:317
  27.7 13.9 %collective-permute-start.3 = (bf16[16,64,128]{2,1,0:T(8,128)(2,1)S(1)}, bf16[16,64,128]{2,1,0:T(8,128)(2,1)S(1)}, u32[]{:S(2)}, u32[]{:S(2)}) collective-permute-start(bf16[16,64,128]{2,1,0:T(8,128)(2,1)S(1)} %all-to-all-done.1.kv0), channel_id=1, source_target_pairs={{0,32},{16,48},{32,0},{48,16},{64,96},{80,112},{96,64},{112,80},{1... | collective-permute-start | bytes 786440 | tf_op jit(solution)/shard_map/ppermute | solution.py:328
  30.8 10.9 %collective-permute-start.2 = (bf16[16,64,128]{2,1,0:T(8,128)(2,1)S(1)}, bf16[16,64,128]{2,1,0:T(8,128)(2,1)S(1)}, u32[]{:S(2)}, u32[]{:S(2)}) collective-permute-start(bf16[16,64,128]{2,1,0:T(8,128)(2,1)S(1)} %all-to-all-done.1.kv0), channel_id=1, source_target_pairs={{0,48},{16,0},{32,16},{48,32},{64,112},{80,64},{96,80},{112,96},{1... | collective-permute-start | bytes 786440 | tf_op jit(solution)/shard_map/ppermute | solution.py:328
  32.0 9.8 %collective-permute-start.1 = (bf16[16,64,128]{2,1,0:T(8,128)(2,1)S(1)}, bf16[16,64,128]{2,1,0:T(8,128)(2,1)S(1)}, u32[]{:S(2)}, u32[]{:S(2)}) collective-permute-start(bf16[16,64,128]{2,1,0:T(8,128)(2,1)S(1)} %all-to-all-done.1.kv0), channel_id=1, source_target_pairs={{0,16},{16,32},{32,48},{48,0},{64,80},{80,96},{96,112},{112,64},{1... | collective-permute-start | bytes 786440 | tf_op jit(solution)/shard_map/ppermute | solution.py:328
  41.4 2.0 %collective-permute-start = (bf16[16,144,128]{2,1,0:T(8,128)(2,1)S(1)}, bf16[16,144,128]{2,1,0:T(8,128)(2,1)S(1)}, u32[]{:S(2)}, u32[]{:S(2)}) collective-permute-start(bf16[16,144,128]{2,1,0:T(8,128)(2,1)S(1)} %all-to-all-done.own), channel_id=1, source_target_pairs={{0,2},{2,0},{4,6},{6,4},{8,10},{10,8},{12,14},{14,12},{1,3},{3,1},... | collective-permute-start | bytes 1769480 | tf_op jit(solution)/shard_map/ppermute | solution.py:321
  49.3 1.3 %collective-permute-start.4 = (f32[8,2048]{1,0:T(8,128)S(1)}, f32[8,2048]{1,0:T(8,128)S(1)}, u32[]{:S(2)}, u32[]{:S(2)}) collective-permute-start(f32[8,2048]{1,0:T(8,128)S(1)} %get-tuple-element.15.mine), channel_id=1, source_target_pairs={{0,2},{2,0},{4,6},{6,4},{8,10},{10,8},{12,14},{14,12},{1,3},{3,1},... | collective-permute-start | bytes 196616 | tf_op jit(solution)/shard_map/ppermute | solution.py:321
  57.8 14.8 %collective-permute-start.5 = (bf16[16,64,128]{2,1,0:T(8,128)(2,1)S(1)}, bf16[16,64,128]{2,1,0:T(8,128)(2,1)S(1)}, u32[]{:S(2)}, u32[]{:S(2)}) collective-permute-start(bf16[16,64,128]{2,1,0:T(8,128)(2,1)S(1)} %get-tuple-element.18), channel_id=1, source_target_pairs={{0,48},{16,0},{32,16},{48,32},{64,112},{80,64},{96,80},{112,96},{1... | collective-permute-start | bytes 786440 | tf_op jit(solution)/shard_map/ppermute | solution.py:328
  61.8 14.2 %collective-permute-start.6 = (bf16[16,64,128]{2,1,0:T(8,128)(2,1)S(1)}, bf16[16,64,128]{2,1,0:T(8,128)(2,1)S(1)}, u32[]{:S(2)}, u32[]{:S(2)}) collective-permute-start(bf16[16,64,128]{2,1,0:T(8,128)(2,1)S(1)} %get-tuple-element.19), channel_id=1, source_target_pairs={{0,16},{16,32},{32,48},{48,0},{64,80},{80,96},{96,112},{112,64},{1... | collective-permute-start | bytes 786440 | tf_op jit(solution)/shard_map/ppermute | solution.py:328
  61.8 14.2 %collective-permute-start.7 = (bf16[16,64,128]{2,1,0:T(8,128)(2,1)S(1)}, bf16[16,64,128]{2,1,0:T(8,128)(2,1)S(1)}, u32[]{:S(2)}, u32[]{:S(2)}) collective-permute-start(bf16[16,64,128]{2,1,0:T(8,128)(2,1)S(1)} %get-tuple-element.20), channel_id=1, source_target_pairs={{0,32},{16,48},{32,0},{48,16},{64,96},{80,112},{96,64},{112,80},{1... | collective-permute-start | bytes 786440 | tf_op jit(solution)/shard_map/ppermute | solution.py:328
  67.9 8.4 %collective-permute-start.8 = (bf16[16,64,128]{2,1,0:T(8,128)(2,1)S(1)}, bf16[16,64,128]{2,1,0:T(8,128)(2,1)S(1)}, u32[]{:S(2)}, u32[]{:S(2)}) collective-permute-start(bf16[16,64,128]{2,1,0:T(8,128)(2,1)S(1)} %get-tuple-element.23), channel_id=1, source_target_pairs={{0,2},{2,0},{4,6},{6,4},{8,10},{10,8},{12,14},{14,12},{1,3},{3,1},... | collective-permute-start | bytes 786440 | tf_op jit(solution)/shard_map/ppermute | solution.py:321

commit v5 on v4

--- a/solution.py
+++ b/solution.py
@@ -23,7 +23,7 @@
 FLOOR = -1e29
 SCALE = float(DIM) ** -0.5
 LOG2E = 1.4426950408889634
-LIMIT = 8 * 1024 * 1024
+LIMIT = 4 * 1024 * 1024
 
 
 def dot(a, b, left, right):
@@ -67,7 +67,7 @@
     lax.fori_loop(whole, SIDE, functools.partial(body, SIDE), 0)
 
 
-def stats_kernel(scalars, lim, own, other, kv0, kv1, kv2, kv3, out, logits, acc):
+def stats_kernel(scalars, lim, own, other, kv0, kv1, kv2, kv3, out, logits, prods, acc):
     kvs = (kv0, kv1, kv2, kv3)
     acc[...] = jnp.zeros_like(acc)
     acc[0:8, :] = jnp.full((8, ROWS), MASKED, jnp.float32)
@@ -88,6 +88,7 @@
                 rows = slice(row * TILE, (row + 1) * TILE)
                 block = masked(product, steps, lim, level, row, lanes) * (SCALE * LOG2E)
                 logits[SIDE * level + unit, rows] = block
+                prods[SIDE * level + unit, rows] = mixture[rows]
                 top = jnp.maximum(high, block.reshape(shape).max(axis=0))
                 base = jnp.maximum(top, FLOOR)
                 weights = jnp.exp2(block.reshape(shape) - base[None])
@@ -109,10 +110,7 @@
     out[2:3, :] = (acc[16:24, :] * fade).sum(axis=0, keepdims=True)
 
 
-def source_grads_kernel(
-    scalars, own, other, mine, theirs, logits, kv0, kv1, kv2, kv3, *refs
-):
-    kvs = (kv0, kv1, kv2, kv3)
+def source_grads_kernel(scalars, own, other, mine, theirs, logits, prods, *refs):
     outs, (lows, shift, delta, key_acc, value_acc) = refs[:SIDE], refs[SIDE:]
     for tile in range(TILES):
         lanes = slice(tile * TILE, (tile + 1) * TILE)
@@ -132,22 +130,19 @@
         def unit_grads(count, unit, carry):
             x = unit_rows(own, other, unit, QUERY)
             g = unit_rows(own, other, unit, GRAD)
-            values = source_rows(kvs, level, PIECE, count)
             key_sum = value_sum = 0.0
             for begin in range(0, WIDE, PART):
                 lanes = pl.ds(pl.multiple_of(unit * WIDE + begin, PART), PART)
                 x_part = x[begin : begin + PART]
                 g_part = g[begin : begin + PART]
                 columns = slice(begin, begin + PART)
-                prods = dot(values, g_part, 1, 1) - delta[0:1, lanes]
                 highs = []
                 parts = []
                 for row in range(count):
-                    rows = slice(row * TILE, (row + 1) * TILE)
-                    block = logits[SIDE * level + unit, rows, columns]
-                    probs = jnp.exp2(block - shift[0:1, lanes])
+                    place = (SIDE * level + unit, slice(row * TILE, (row + 1) * TILE), columns)
+                    probs = jnp.exp2(logits[place] - shift[0:1, lanes])
                     highs.append(probs.astype(jnp.bfloat16))
-                    parts.append((probs * prods[rows]).astype(jnp.bfloat16))
+                    parts.append((probs * (prods[place] - delta[0:1, lanes])).astype(jnp.bfloat16))
                 low = jnp.concatenate(parts, axis=0)
                 lows[SIDE * level + unit, : count * TILE, begin : begin + PART] = low
                 value_sum += dot(jnp.concatenate(highs, axis=0), g_part, 1, 0)
@@ -205,9 +200,9 @@
     return pl.pallas_call(
         stats_kernel,
         out_shape=[jax.ShapeDtypeStruct((8, ROWS), jnp.float32)]
-        + [jax.ShapeDtypeStruct((TILES, WIDE, WIDE), jnp.float32)],
+        + [jax.ShapeDtypeStruct((TILES, WIDE, WIDE), jnp.float32)] * 2,
         in_specs=[SMEM] + [VMEM] * (len(operands) - 1),
-        out_specs=[VMEM] * 2,
+        out_specs=[VMEM] * 3,
         scratch_shapes=[pltpu.VMEM((24, ROWS), jnp.float32)],
         compiler_params=PARAMS,
         cost_estimate=cost(4),
@@ -360,10 +355,10 @@
     lim = jnp.where(flags[..., None] == 1, ordered[None, None], 0) - begins[:, :, None, None, None]
     lim = lim.reshape(TILES, ROWS)
 
-    mine, logits = row_stats(scalars, lim, own, other, kvs)
+    mine, logits, prods = row_stats(scalars, lim, own, other, kvs)
     theirs = swap_cores(mine)
     part0, part1, part2, part3, lows = source_grads(
-        scalars, own, other, mine, theirs, logits, *kvs
+        scalars, own, other, mine, theirs, logits, prods
     )
     got3, got1, got2 = along(part3, 2), along(part1, 3), along(part2, 1)
     keep, send = query_grads(scalars, kvs, lows)

time: 95.6 us -> 94.6 us (0.990)
  Pallas kernels: 21.9 us -> 20.9 us
    pallas_call x1, Pallas kernels: 7.13 us -> 6.17 us  [source_grads(): pl.pallas_call(source_grads_kernel, out_shape=[piece] * SIDE + [lows], in...]
where the time goes in v5:
time: 94.6 us; the launch traced here: 94.2 us
  waiting for transfers between devices  25.3 us (27%)
  starting transfers between devices  24.2 us (26%)
  Pallas kernels  20.9 us (22%)
  blocking collectives  18.6 us (20%)
  local copies, waits for them, and re-layouts  2.47 us (3%)
  other arithmetic  2.04 us (2%)
    all_to_all x1, blocking collectives, exchange(): lax.all_to_all(a, ('tgt', 'src'), 0, 0, axis_index_groups=GROUPS, tiled=T...  18.6 us
    all_to_all x2, waiting for transfers between devices, exchange(): lax.all_to_all(a, ('tgt', 'src'), 0, 0, axis_index_groups=GROUPS, tiled=T...  14 us
    all_to_all x2, starting transfers between devices, exchange(): lax.all_to_all(a, ('tgt', 'src'), 0, 0, axis_index_groups=GROUPS, tiled=T...  13.8 us
    ppermute x6, starting transfers between devices, along(): return lax.ppermute(a, 'tgt', [(i, target(i)) for i in range(TILES)])  10.3 us
    ppermute x6, waiting for transfers between devices, along(): return lax.ppermute(a, 'tgt', [(i, target(i)) for i in range(TILES)])  8.32 us
    pallas_call x1, Pallas kernels, source_grads(): pl.pallas_call(source_grads_kernel, out_shape=[piece] * SIDE + [lows], in...  6.17 us
    pallas_call x1, Pallas kernels, row_stats(): pl.pallas_call(stats_kernel, out_shape=[jax.ShapeDtypeStruct((8, ROWS), j...  5.74 us
    pallas_call x1, Pallas kernels, query_grads(): pl.pallas_call(query_grads_kernel, out_shape=[jax.ShapeDtypeStruct(shape,...  4.33 us
  transfers between devices with their start and end apart: 11, of which 7 were waited for; matrix products, arithmetic and copies ran while one was open for 5% of the time, Pallas kernels for 7%

profile of v5, /device:TPU:32, one launch (start us, length us, event | category | flops | bytes accessed | tf_op | source)
XLA Modules:
  0.0 94.2 jit_solution(12562382048002277762)
XLA Ops:
  0.6 1.7 %by_head.3 = bf16[16,64,128]{2,1,0:T(8,128)(2,1)} custom-call(bf16[32,2048]{1,0:T(8,128)(2,1)} %refs_0_.3, bf16[32,2048]{1,0:T(8,128)(2,1)} %refs_1_.3), custom_call_target="tpu_custom_call" | custom-call | tf_op jit(solution)/shard_map/by_head/pallas_call | solution.py:271
  2.3 8.7 %all-to-all-start.1 = ((bf16[16,64,128]{2,1,0:T(8,128)(2,1)}), bf16[16,64,128]{2,1,0:T(8,128)(2,1)S(1)}, u32[]{:S(2)}, u32[]{:S(2)}) async-start(bf16[16,64,128]{2,1,0:T(8,128)(2,1)} %by_head.3), calls=%async_computation.1 | async-start | bytes 524288 | tf_op jit(solution)/shard_map/all_to_all | solution.py:312
  11.0 0.8 convert_bitcast_fusion
  11.8 0.6 fusion.4.refs_2_
  12.4 1.9 %by_head.2 = bf16[16,144,128]{2,1,0:T(8,128)(2,1)} custom-call(bf16[64,2048]{1,0:T(8,128)(2,1)} %refs_0_.2, bf16[64,2048]{1,0:T(8,128)(2,1)} %refs_1_.2, bf16[16,128]{1,0:T(8,128)(2,1)} %fusion.4.refs_2_), custom_call_target="tpu_custom_call" | custom-call | tf_op jit(solution)/shard_map/by_head/pallas_call | solution.py:271
  14.3 6.0 %all-to-all-done.1.kv0 = bf16[16,64,128]{2,1,0:T(8,128)(2,1)S(1)} async-done(((bf16[16,64,128]{2,1,0:T(8,128)(2,1)}), bf16[16,64,128]{2,1,0:T(8,128)(2,1)S(1)}, u32[]{:S(2)}, u32[]{:S(2)}) %all-to-all-start.1) | async-done | bytes 262176 | tf_op jit(solution)/shard_map/all_to_all | solution.py:312
  20.3 5.1 %all-to-all-start = ((bf16[16,144,128]{2,1,0:T(8,128)(2,1)}), bf16[16,144,128]{2,1,0:T(8,128)(2,1)S(1)}, u32[]{:S(2)}, u32[]{:S(2)}) async-start(bf16[16,144,128]{2,1,0:T(8,128)(2,1)} %by_head.2), calls=%async_computation | async-start | bytes 1179648 | tf_op jit(solution)/shard_map/all_to_all | solution.py:312
  25.7 1.1 %reshape.73 = s32[4,4,4,4,2,4]{2,1,0,5,4,3:T(4,128)S(1)} reshape(s32[64,32]{0,1:T(8,128)} %param.11) | data formatting | bytes 16384 | tf_op jit(solution)/shard_map/reshape | solution.py:352
  26.8 0.2 copy.19
  27.0 0.2 copy.15
  27.3 0.1 broadcast_in_dim.29
  27.5 0.2 slice_reduce_fusion.1
  27.7 3.1 %collective-permute-start.3 = (bf16[16,64,128]{2,1,0:T(8,128)(2,1)S(1)}, bf16[16,64,128]{2,1,0:T(8,128)(2,1)S(1)}, u32[]{:S(2)}, u32[]{:S(2)}) collective-permute-start(bf16[16,64,128]{2,1,0:T(8,128)(2,1)S(1)} %all-to-all-done.1.kv0), channel_id=1, source_target_pairs={{0,32},{16,48},{32,0},{48,16},{64,96},{80,112},{96,64},{112,80},{1... | collective-permute-start | bytes 786440 | tf_op jit(solution)/shard_map/ppermute | solution.py:323
  30.8 1.1 %collective-permute-start.2 = (bf16[16,64,128]{2,1,0:T(8,128)(2,1)S(1)}, bf16[16,64,128]{2,1,0:T(8,128)(2,1)S(1)}, u32[]{:S(2)}, u32[]{:S(2)}) collective-permute-start(bf16[16,64,128]{2,1,0:T(8,128)(2,1)S(1)} %all-to-all-done.1.kv0), channel_id=1, source_target_pairs={{0,48},{16,0},{32,16},{48,32},{64,112},{80,64},{96,80},{112,96},{1... | collective-permute-start | bytes 786440 | tf_op jit(solution)/shard_map/ppermute | solution.py:323
  32.0 0.9 collective-permute-start.1
  32.9 8.0 %all-to-all-done.own = bf16[16,144,128]{2,1,0:T(8,128)(2,1)S(1)} async-done(((bf16[16,144,128]{2,1,0:T(8,128)(2,1)}), bf16[16,144,128]{2,1,0:T(8,128)(2,1)S(1)}, u32[]{:S(2)}, u32[]{:S(2)}) %all-to-all-start) | async-done | bytes 589856 | tf_op jit(solution)/shard_map/all_to_all | solution.py:312
  40.9 0.2 slice_reduce_fusion
  41.1 0.2 convert_reduce_fusion
  41.6 0.1 collective-permute-done.2.kv2
  41.8 1.7 %collective-permute-done.other = bf16[16,144,128]{2,1,0:T(8,128)(2,1)S(1)} collective-permute-done((bf16[16,144,128]{2,1,0:T(8,128)(2,1)S(1)}, bf16[16,144,128]{2,1,0:T(8,128)(2,1)S(1)}, u32[]{:S(2)}, u32[]{:S(2)}) %collective-permute-start) | collective-permute-done | bytes 589856 | tf_op jit(solution)/shard_map/ppermute | solution.py:316
  43.5 5.7 %stats.1 = (f32[8,2048]{1,0:T(8,128)S(1)}, f32[16,512,512]{2,1,0:T(8,128)S(1)}, f32[16,512,512]{2,1,0:T(8,128)S(1)}) custom-call(s32[12]{0:T(128)S(1)} %concatenate.12.scalars, s32[16,2048]{1,0:T(8,128)S(1)} %select_subtract_fusion.lim, bf16[16,144,128]{2,1,0:T(8,128)(2,1)S(1)} %all-to-all-done.own, bf16[16,144,128]{2,1,0:T(8,128)(2,1)S(1)} %collective-permute-done.other, ...), custom_call_target="tpu_custom_call" | custom-call | flops 2684354560 | bytes 1048576 | tf_op jit(solution)/shard_map/stats/pallas_call | solution.py:200
  49.3 1.2 %collective-permute-done.4.theirs = f32[8,2048]{1,0:T(8,128)S(1)} collective-permute-done((f32[8,2048]{1,0:T(8,128)S(1)}, f32[8,2048]{1,0:T(8,128)S(1)}, u32[]{:S(2)}, u32[]{:S(2)}) %collective-permute-start.4) | collective-permute-done | bytes 65568 | tf_op jit(solution)/shard_map/ppermute | solution.py:316
  50.5 6.2 %source_grads.1 = (bf16[16,64,128]{2,1,0:T(8,128)(2,1)S(1)}, bf16[16,64,128]{2,1,0:T(8,128)(2,1)S(1)}, bf16[16,64,128]{2,1,0:T(8,128)(2,1)S(1)}, bf16[16,64,128]...) custom-call(s32[12]{0:T(128)S(1)} %concatenate.12.scalars, bf16[16,144,128]{2,1,0:T(8,128)(2,1)S(1)} %all-to-all-done.own, ...), custom_call_target="tpu_custom_call" | custom-call | flops 2684354560 | bytes 1048576 | tf_op jit(solution)/shard_map/source_grads/pallas_call | solution.py:216
  56.7 2.8 %collective-permute-start.5 = (bf16[16,64,128]{2,1,0:T(8,128)(2,1)S(1)}, bf16[16,64,128]{2,1,0:T(8,128)(2,1)S(1)}, u32[]{:S(2)}, u32[]{:S(2)}) collective-permute-start(bf16[16,64,128]{2,1,0:T(8,128)(2,1)S(1)} %get-tuple-element.20), channel_id=1, source_target_pairs={{0,48},{16,0},{32,16},{48,32},{64,112},{80,64},{96,80},{112,96},{1... | collective-permute-start | bytes 786440 | tf_op jit(solution)/shard_map/ppermute | solution.py:323
  59.5 2.3 %collective-permute-start.7 = (bf16[16,64,128]{2,1,0:T(8,128)(2,1)S(1)}, bf16[16,64,128]{2,1,0:T(8,128)(2,1)S(1)}, u32[]{:S(2)}, u32[]{:S(2)}) collective-permute-start(bf16[16,64,128]{2,1,0:T(8,128)(2,1)S(1)} %get-tuple-element.22), channel_id=1, source_target_pairs={{0,32},{16,48},{32,0},{48,16},{64,96},{80,112},{96,64},{112,80},{1... | collective-permute-start | bytes 786440 | tf_op jit(solution)/shard_map/ppermute | solution.py:323
  61.8 4.3 %query_grads.1 = (f32[16,64,128]{2,1,0:T(8,128)S(1)}, bf16[16,64,128]{2,1,0:T(8,128)(2,1)S(1)}) custom-call(s32[12]{0:T(128)S(1)} %concatenate.12.scalars, bf16[16,64,128]{2,1,0:T(8,128)(2,1)S(1)} %all-to-all-done.1.kv0, bf16[16,64,128]{2,1,0:T(8,128)(2,1)S(1)} %collective-permute-done.1.kv1, bf16[16,64,128]{2,1,0:T(8,128)(2,1)S(1)} %collective-permute-done.2.kv2, ...), custom_call_target="tpu_custom_call" | custom-call | flops 671088640 | bytes 1048576 | tf_op jit(solution)/shard_map/query_grads/pallas_call | solution.py:235
  66.2 0.1 collective-permute-start.8
  66.3 4.8 %collective-permute-done.5 = bf16[16,64,128]{2,1,0:T(8,128)(2,1)S(1)} collective-permute-done((bf16[16,64,128]{2,1,0:T(8,128)(2,1)S(1)}, bf16[16,64,128]{2,1,0:T(8,128)(2,1)S(1)}, u32[]{:S(2)}, u32[]{:S(2)}) %collective-permute-start.5) | collective-permute-done | bytes 262176 | tf_op jit(solution)/shard_map/ppermute | solution.py:323
  71.0 3.4 %collective-permute-done.6 = bf16[16,64,128]{2,1,0:T(8,128)(2,1)S(1)} collective-permute-done((bf16[16,64,128]{2,1,0:T(8,128)(2,1)S(1)}, bf16[16,64,128]{2,1,0:T(8,128)(2,1)S(1)}, u32[]{:S(2)}, u32[]{:S(2)}) %collective-permute-start.6) | collective-permute-done | bytes 262176 | tf_op jit(solution)/shard_map/ppermute | solution.py:323
  74.5 0.2 add_convert_fusion.sums
  74.7 18.6 %all_to_all.15.heads = bf16[16,128,128]{2,1,0:T(8,128)(2,1)S(1)} all-to-all(bf16[16,128,128]{2,1,0:T(8,128)(2,1)S(1)} %pack.1), channel_id=1, replica_groups={{0,64,128,192,4,68,132,196,8,72,136,200,12,76,140,204},{2,66,130,194,6,..., dimensions={0} | all-to-all | bytes 1048576 | tf_op jit(solution)/shard_map/all_to_all | solution.py:312
  93.3 0.9 by_row.1
  (26 shorter events, 1.0 us)
Async XLA Ops:
  2.3 18.0 %all-to-all-start.1 = ((bf16[16,64,128]{2,1,0:T(8,128)(2,1)}), bf16[16,64,128]{2,1,0:T(8,128)(2,1)S(1)}, u32[]{:S(2)}, u32[]{:S(2)}) async-start(bf16[16,64,128]{2,1,0:T(8,128)(2,1)} %by_head.3), calls=%async_computation.1 | async-start | bytes 524288 | tf_op jit(solution)/shard_map/all_to_all | solution.py:312
  20.3 20.5 %all-to-all-start = ((bf16[16,144,128]{2,1,0:T(8,128)(2,1)}), bf16[16,144,128]{2,1,0:T(8,128)(2,1)S(1)}, u32[]{:S(2)}, u32[]{:S(2)}) async-start(bf16[16,144,128]{2,1,0:T(8,128)(2,1)} %by_head.2), calls=%async_computation | async-start | bytes 1179648 | tf_op jit(solution)/shard_map/all_to_all | solution.py:312
  27.7 13.9 %collective-permute-start.3 = (bf16[16,64,128]{2,1,0:T(8,128)(2,1)S(1)}, bf16[16,64,128]{2,1,0:T(8,128)(2,1)S(1)}, u32[]{:S(2)}, u32[]{:S(2)}) collective-permute-start(bf16[16,64,128]{2,1,0:T(8,128)(2,1)S(1)} %all-to-all-done.1.kv0), channel_id=1, source_target_pairs={{0,32},{16,48},{32,0},{48,16},{64,96},{80,112},{96,64},{112,80},{1... | collective-permute-start | bytes 786440 | tf_op jit(solution)/shard_map/ppermute | solution.py:323
  30.8 10.9 %collective-permute-start.2 = (bf16[16,64,128]{2,1,0:T(8,128)(2,1)S(1)}, bf16[16,64,128]{2,1,0:T(8,128)(2,1)S(1)}, u32[]{:S(2)}, u32[]{:S(2)}) collective-permute-start(bf16[16,64,128]{2,1,0:T(8,128)(2,1)S(1)} %all-to-all-done.1.kv0), channel_id=1, source_target_pairs={{0,48},{16,0},{32,16},{48,32},{64,112},{80,64},{96,80},{112,96},{1... | collective-permute-start | bytes 786440 | tf_op jit(solution)/shard_map/ppermute | solution.py:323
  32.0 9.8 %collective-permute-start.1 = (bf16[16,64,128]{2,1,0:T(8,128)(2,1)S(1)}, bf16[16,64,128]{2,1,0:T(8,128)(2,1)S(1)}, u32[]{:S(2)}, u32[]{:S(2)}) collective-permute-start(bf16[16,64,128]{2,1,0:T(8,128)(2,1)S(1)} %all-to-all-done.1.kv0), channel_id=1, source_target_pairs={{0,16},{16,32},{32,48},{48,0},{64,80},{80,96},{96,112},{112,64},{1... | collective-permute-start | bytes 786440 | tf_op jit(solution)/shard_map/ppermute | solution.py:323
  41.4 2.0 %collective-permute-start = (bf16[16,144,128]{2,1,0:T(8,128)(2,1)S(1)}, bf16[16,144,128]{2,1,0:T(8,128)(2,1)S(1)}, u32[]{:S(2)}, u32[]{:S(2)}) collective-permute-start(bf16[16,144,128]{2,1,0:T(8,128)(2,1)S(1)} %all-to-all-done.own), channel_id=1, source_target_pairs={{0,2},{2,0},{4,6},{6,4},{8,10},{10,8},{12,14},{14,12},{1,3},{3,1},... | collective-permute-start | bytes 1769480 | tf_op jit(solution)/shard_map/ppermute | solution.py:316
  49.2 1.3 %collective-permute-start.4 = (f32[8,2048]{1,0:T(8,128)S(1)}, f32[8,2048]{1,0:T(8,128)S(1)}, u32[]{:S(2)}, u32[]{:S(2)}) collective-permute-start(f32[8,2048]{1,0:T(8,128)S(1)} %get-tuple-element.16.mine), channel_id=1, source_target_pairs={{0,2},{2,0},{4,6},{6,4},{8,10},{10,8},{12,14},{14,12},{1,3},{3,1},... | collective-permute-start | bytes 196616 | tf_op jit(solution)/shard_map/ppermute | solution.py:316
  56.7 14.3 %collective-permute-start.5 = (bf16[16,64,128]{2,1,0:T(8,128)(2,1)S(1)}, bf16[16,64,128]{2,1,0:T(8,128)(2,1)S(1)}, u32[]{:S(2)}, u32[]{:S(2)}) collective-permute-start(bf16[16,64,128]{2,1,0:T(8,128)(2,1)S(1)} %get-tuple-element.20), channel_id=1, source_target_pairs={{0,48},{16,0},{32,16},{48,32},{64,112},{80,64},{96,80},{112,96},{1... | collective-permute-start | bytes 786440 | tf_op jit(solution)/shard_map/ppermute | solution.py:323
  59.5 14.9 %collective-permute-start.6 = (bf16[16,64,128]{2,1,0:T(8,128)(2,1)S(1)}, bf16[16,64,128]{2,1,0:T(8,128)(2,1)S(1)}, u32[]{:S(2)}, u32[]{:S(2)}) collective-permute-start(bf16[16,64,128]{2,1,0:T(8,128)(2,1)S(1)} %get-tuple-element.21), channel_id=1, source_target_pairs={{0,16},{16,32},{32,48},{48,0},{64,80},{80,96},{96,112},{112,64},{1... | collective-permute-start | bytes 786440 | tf_op jit(solution)/shard_map/ppermute | solution.py:323
  59.5 14.9 %collective-permute-start.7 = (bf16[16,64,128]{2,1,0:T(8,128)(2,1)S(1)}, bf16[16,64,128]{2,1,0:T(8,128)(2,1)S(1)}, u32[]{:S(2)}, u32[]{:S(2)}) collective-permute-start(bf16[16,64,128]{2,1,0:T(8,128)(2,1)S(1)} %get-tuple-element.22), channel_id=1, source_target_pairs={{0,32},{16,48},{32,0},{48,16},{64,96},{80,112},{96,64},{112,80},{1... | collective-permute-start | bytes 786440 | tf_op jit(solution)/shard_map/ppermute | solution.py:323
  66.2 8.5 %collective-permute-start.8 = (bf16[16,64,128]{2,1,0:T(8,128)(2,1)S(1)}, bf16[16,64,128]{2,1,0:T(8,128)(2,1)S(1)}, u32[]{:S(2)}, u32[]{:S(2)}) collective-permute-start(bf16[16,64,128]{2,1,0:T(8,128)(2,1)S(1)} %get-tuple-element.25), channel_id=1, source_target_pairs={{0,2},{2,0},{4,6},{6,4},{8,10},{10,8},{12,14},{14,12},{1,3},{3,1},... | collective-permute-start | bytes 786440 | tf_op jit(solution)/shard_map/ppermute | solution.py:316

commit v6 on v5

--- a/solution.py
+++ b/solution.py
@@ -330,7 +330,11 @@
 
     reads = lax.dynamic_slice_in_dim(read_points, level * TILE, TILE)
     digits = jnp.stack([reads // 64, reads % 64]).astype(jnp.bfloat16)
+    flags = block_mask.reshape(SIDE, SIDE, SIDE, SIDE, 2, SIDE)
+    flags = lax.dynamic_index_in_dim(flags, column, 1, False)
+    flags = lax.dynamic_index_in_dim(flags, core, 3, False).transpose(2, 3, 0, 1)
     digits = jnp.pad(digits, ((0, 14), (0, 0)))
+    digits, flags = lax.optimization_barrier((digits, flags))
     kv = exchange(by_head(keys, values))
     kvs = [kv] + [along(kv, k) for k in (1, 3, 2)]
     own = exchange(by_head(queries, out_grad, digits))
@@ -349,9 +353,6 @@
     scalars = jnp.concatenate([first, offsets, whole]).astype(jnp.int32)
     ordered = jnp.where(core == 0, reads, jnp.roll(reads, HALF, axis=1))
     ordered = ordered.reshape(SIDE, SIDE, TILE).transpose(1, 0, 2)
-    flags = block_mask.reshape(SIDE, SIDE, SIDE, SIDE, 2, SIDE)
-    flags = lax.dynamic_index_in_dim(flags, column, 1, False)
-    flags = lax.dynamic_index_in_dim(flags, core, 3, False).transpose(2, 3, 0, 1)
     lim = jnp.where(flags[..., None] == 1, ordered[None, None], 0) - begins[:, :, None, None, None]
     lim = lim.reshape(TILES, ROWS)
 

time: 94.6 us -> 94 us (level)
  transfers between devices with their start and end apart: 11 -> 11, of which waited for: 7 -> 6; matrix products, arithmetic and copies ran while one was open for 5% -> 4% of each run, Pallas kernels for 7% -> 7%
where the time goes in v6:
time: 94 us; the launch traced here: 93.6 us
  waiting for transfers between devices  25.9 us (28%)
  starting transfers between devices  24.2 us (26%)
  Pallas kernels  20.9 us (22%)
  blocking collectives  17.8 us (19%)
  other arithmetic  2.04 us (2%)
  local copies, waits for them, and re-layouts  2.04 us (2%)
    all_to_all x1, blocking collectives, exchange(): lax.all_to_all(a, ('tgt', 'src'), 0, 0, axis_index_groups=GROUPS, tiled=T...  17.8 us
    all_to_all x2, waiting for transfers between devices, exchange(): lax.all_to_all(a, ('tgt', 'src'), 0, 0, axis_index_groups=GROUPS, tiled=T...  14.4 us
    all_to_all x2, starting transfers between devices, exchange(): lax.all_to_all(a, ('tgt', 'src'), 0, 0, axis_index_groups=GROUPS, tiled=T...  13.8 us
    ppermute x6, starting transfers between devices, along(): return lax.ppermute(a, 'tgt', [(i, target(i)) for i in range(TILES)])  10.3 us
    ppermute x6, waiting for transfers between devices, along(): return lax.ppermute(a, 'tgt', [(i, target(i)) for i in range(TILES)])  8.45 us
    pallas_call x1, Pallas kernels, source_grads(): pl.pallas_call(source_grads_kernel, out_shape=[piece] * SIDE + [lows], in...  6.17 us
    pallas_call x1, Pallas kernels, row_stats(): pl.pallas_call(stats_kernel, out_shape=[jax.ShapeDtypeStruct((8, ROWS), j...  5.74 us
    pallas_call x1, Pallas kernels, query_grads(): pl.pallas_call(query_grads_kernel, out_shape=[jax.ShapeDtypeStruct(shape,...  4.33 us
  transfers between devices with their start and end apart: 11, of which 6 were waited for; matrix products, arithmetic and copies ran while one was open for 4% of the time, Pallas kernels for 7%

profile of v6, /device:TPU:32, one launch (start us, length us, event | category | flops | bytes accessed | tf_op | source)
XLA Modules:
  0.0 93.6 jit_solution(1426279007979134264)
XLA Ops:
  0.6 1.7 %by_head.3 = bf16[16,64,128]{2,1,0:T(8,128)(2,1)} custom-call(bf16[32,2048]{1,0:T(8,128)(2,1)} %refs_0_.3, bf16[32,2048]{1,0:T(8,128)(2,1)} %refs_1_.3), custom_call_target="tpu_custom_call" | custom-call | tf_op jit(solution)/shard_map/by_head/pallas_call | solution.py:271
  2.3 8.7 %all-to-all-start.1 = ((bf16[16,64,128]{2,1,0:T(8,128)(2,1)}), bf16[16,64,128]{2,1,0:T(8,128)(2,1)S(1)}, u32[]{:S(2)}, u32[]{:S(2)}) async-start(bf16[16,64,128]{2,1,0:T(8,128)(2,1)} %by_head.3), calls=%async_computation.1 | async-start | bytes 524288 | tf_op jit(solution)/shard_map/all_to_all | solution.py:312
  11.0 0.8 convert_bitcast_fusion
  11.8 1.1 %reshape.71 = s32[4,4,4,4,2,4]{2,1,0,5,4,3:T(4,128)S(1)} reshape(s32[64,32]{0,1:T(8,128)} %param.11) | data formatting | bytes 16384 | tf_op jit(solution)/shard_map/reshape | solution.py:333
  12.8 0.6 fusion.4.refs_2_
  13.5 1.9 %by_head.2 = bf16[16,144,128]{2,1,0:T(8,128)(2,1)} custom-call(bf16[64,2048]{1,0:T(8,128)(2,1)} %refs_0_.2, bf16[64,2048]{1,0:T(8,128)(2,1)} %refs_1_.2, bf16[16,128]{1,0:T(8,128)(2,1)} %fusion.4.refs_2_), custom_call_target="tpu_custom_call" | custom-call | tf_op jit(solution)/shard_map/by_head/pallas_call | solution.py:271
  15.4 4.9 %all-to-all-done.1.kv0 = bf16[16,64,128]{2,1,0:T(8,128)(2,1)S(1)} async-done(((bf16[16,64,128]{2,1,0:T(8,128)(2,1)}), bf16[16,64,128]{2,1,0:T(8,128)(2,1)S(1)}, u32[]{:S(2)}, u32[]{:S(2)}) %all-to-all-start.1) | async-done | bytes 262176 | tf_op jit(solution)/shard_map/all_to_all | solution.py:312
  20.3 5.1 %all-to-all-start = ((bf16[16,144,128]{2,1,0:T(8,128)(2,1)}), bf16[16,144,128]{2,1,0:T(8,128)(2,1)S(1)}, u32[]{:S(2)}, u32[]{:S(2)}) async-start(bf16[16,144,128]{2,1,0:T(8,128)(2,1)} %by_head.2), calls=%async_computation | async-start | bytes 1179648 | tf_op jit(solution)/shard_map/all_to_all | solution.py:312
  25.6 0.1 add.122
  25.7 0.1 broadcast_in_dim.29
  26.0 0.2 slice_reduce_fusion.1
  26.2 3.1 %collective-permute-start.3 = (bf16[16,64,128]{2,1,0:T(8,128)(2,1)S(1)}, bf16[16,64,128]{2,1,0:T(8,128)(2,1)S(1)}, u32[]{:S(2)}, u32[]{:S(2)}) collective-permute-start(bf16[16,64,128]{2,1,0:T(8,128)(2,1)S(1)} %all-to-all-done.1.kv0), channel_id=1, source_target_pairs={{0,32},{16,48},{32,0},{48,16},{64,96},{80,112},{96,64},{112,80},{1... | collective-permute-start | bytes 786440 | tf_op jit(solution)/shard_map/ppermute | solution.py:323
  29.3 1.1 %collective-permute-start.2 = (bf16[16,64,128]{2,1,0:T(8,128)(2,1)S(1)}, bf16[16,64,128]{2,1,0:T(8,128)(2,1)S(1)}, u32[]{:S(2)}, u32[]{:S(2)}) collective-permute-start(bf16[16,64,128]{2,1,0:T(8,128)(2,1)S(1)} %all-to-all-done.1.kv0), channel_id=1, source_target_pairs={{0,48},{16,0},{32,16},{48,32},{64,112},{80,64},{96,80},{112,96},{1... | collective-permute-start | bytes 786440 | tf_op jit(solution)/shard_map/ppermute | solution.py:323
  30.4 0.9 collective-permute-start.1
  31.3 9.5 %all-to-all-done.own = bf16[16,144,128]{2,1,0:T(8,128)(2,1)S(1)} async-done(((bf16[16,144,128]{2,1,0:T(8,128)(2,1)}), bf16[16,144,128]{2,1,0:T(8,128)(2,1)S(1)}, u32[]{:S(2)}, u32[]{:S(2)}) %all-to-all-start) | async-done | bytes 589856 | tf_op jit(solution)/shard_map/all_to_all | solution.py:312
  40.9 0.2 slice_reduce_fusion
  41.1 0.2 convert_reduce_fusion
  41.3 0.1 concatenate.12.scalars
  41.7 1.8 %collective-permute-done.other = bf16[16,144,128]{2,1,0:T(8,128)(2,1)S(1)} collective-permute-done((bf16[16,144,128]{2,1,0:T(8,128)(2,1)S(1)}, bf16[16,144,128]{2,1,0:T(8,128)(2,1)S(1)}, u32[]{:S(2)}, u32[]{:S(2)}) %collective-permute-start) | collective-permute-done | bytes 589856 | tf_op jit(solution)/shard_map/ppermute | solution.py:316
  43.5 5.7 %stats.1 = (f32[8,2048]{1,0:T(8,128)S(1)}, f32[16,512,512]{2,1,0:T(8,128)S(1)}, f32[16,512,512]{2,1,0:T(8,128)S(1)}) custom-call(s32[12]{0:T(128)S(1)} %concatenate.12.scalars, s32[16,2048]{1,0:T(8,128)S(1)} %select_subtract_fusion.lim, bf16[16,144,128]{2,1,0:T(8,128)(2,1)S(1)} %all-to-all-done.own, bf16[16,144,128]{2,1,0:T(8,128)(2,1)S(1)} %collective-permute-done.other, ...), custom_call_target="tpu_custom_call" | custom-call | flops 2684354560 | bytes 1048576 | tf_op jit(solution)/shard_map/stats/pallas_call | solution.py:200
  49.2 0.1 collective-permute-start.4
  49.3 1.2 %collective-permute-done.4.theirs = f32[8,2048]{1,0:T(8,128)S(1)} collective-permute-done((f32[8,2048]{1,0:T(8,128)S(1)}, f32[8,2048]{1,0:T(8,128)S(1)}, u32[]{:S(2)}, u32[]{:S(2)}) %collective-permute-start.4) | collective-permute-done | bytes 65568 | tf_op jit(solution)/shard_map/ppermute | solution.py:316
  50.5 6.2 %source_grads.1 = (bf16[16,64,128]{2,1,0:T(8,128)(2,1)S(1)}, bf16[16,64,128]{2,1,0:T(8,128)(2,1)S(1)}, bf16[16,64,128]{2,1,0:T(8,128)(2,1)S(1)}, bf16[16,64,128]...) custom-call(s32[12]{0:T(128)S(1)} %concatenate.12.scalars, bf16[16,144,128]{2,1,0:T(8,128)(2,1)S(1)} %all-to-all-done.own, ...), custom_call_target="tpu_custom_call" | custom-call | flops 2684354560 | bytes 1048576 | tf_op jit(solution)/shard_map/source_grads/pallas_call | solution.py:216
  56.7 3.3 %collective-permute-start.5 = (bf16[16,64,128]{2,1,0:T(8,128)(2,1)S(1)}, bf16[16,64,128]{2,1,0:T(8,128)(2,1)S(1)}, u32[]{:S(2)}, u32[]{:S(2)}) collective-permute-start(bf16[16,64,128]{2,1,0:T(8,128)(2,1)S(1)} %get-tuple-element.24), channel_id=1, source_target_pairs={{0,48},{16,0},{32,16},{48,32},{64,112},{80,64},{96,80},{112,96},{1... | collective-permute-start | bytes 786440 | tf_op jit(solution)/shard_map/ppermute | solution.py:323
  60.0 1.8 %collective-permute-start.7 = (bf16[16,64,128]{2,1,0:T(8,128)(2,1)S(1)}, bf16[16,64,128]{2,1,0:T(8,128)(2,1)S(1)}, u32[]{:S(2)}, u32[]{:S(2)}) collective-permute-start(bf16[16,64,128]{2,1,0:T(8,128)(2,1)S(1)} %get-tuple-element.26), channel_id=1, source_target_pairs={{0,32},{16,48},{32,0},{48,16},{64,96},{80,112},{96,64},{112,80},{1... | collective-permute-start | bytes 786440 | tf_op jit(solution)/shard_map/ppermute | solution.py:323
  61.8 4.3 %query_grads.1 = (f32[16,64,128]{2,1,0:T(8,128)S(1)}, bf16[16,64,128]{2,1,0:T(8,128)(2,1)S(1)}) custom-call(s32[12]{0:T(128)S(1)} %concatenate.12.scalars, bf16[16,64,128]{2,1,0:T(8,128)(2,1)S(1)} %all-to-all-done.1.kv0, bf16[16,64,128]{2,1,0:T(8,128)(2,1)S(1)} %collective-permute-done.1.kv1, bf16[16,64,128]{2,1,0:T(8,128)(2,1)S(1)} %collective-permute-done.2.kv2, ...), custom_call_target="tpu_custom_call" | custom-call | flops 671088640 | bytes 1048576 | tf_op jit(solution)/shard_map/query_grads/pallas_call | solution.py:235
  66.2 0.1 collective-permute-start.8
  66.3 5.0 %collective-permute-done.5 = bf16[16,64,128]{2,1,0:T(8,128)(2,1)S(1)} collective-permute-done((bf16[16,64,128]{2,1,0:T(8,128)(2,1)S(1)}, bf16[16,64,128]{2,1,0:T(8,128)(2,1)S(1)}, u32[]{:S(2)}, u32[]{:S(2)}) %collective-permute-start.5) | collective-permute-done | bytes 262176 | tf_op jit(solution)/shard_map/ppermute | solution.py:323
  71.3 3.4 %collective-permute-done.6 = bf16[16,64,128]{2,1,0:T(8,128)(2,1)S(1)} collective-permute-done((bf16[16,64,128]{2,1,0:T(8,128)(2,1)S(1)}, bf16[16,64,128]{2,1,0:T(8,128)(2,1)S(1)}, u32[]{:S(2)}, u32[]{:S(2)}) %collective-permute-start.6) | collective-permute-done | bytes 262176 | tf_op jit(solution)/shard_map/ppermute | solution.py:323
  74.7 0.2 add_convert_fusion.sums
  75.0 17.8 %all_to_all.15.heads = bf16[16,128,128]{2,1,0:T(8,128)(2,1)S(1)} all-to-all(bf16[16,128,128]{2,1,0:T(8,128)(2,1)S(1)} %pack.1), channel_id=1, replica_groups={{0,64,128,192,4,68,132,196,8,72,136,200,12,76,140,204},{2,66,130,194,6,..., dimensions={0} | all-to-all | bytes 1048576 | tf_op jit(solution)/shard_map/all_to_all | solution.py:312
  92.7 0.9 by_row.1
  (24 shorter events, 0.7 us)
Async XLA Ops:
  2.3 18.0 %all-to-all-start.1 = ((bf16[16,64,128]{2,1,0:T(8,128)(2,1)}), bf16[16,64,128]{2,1,0:T(8,128)(2,1)S(1)}, u32[]{:S(2)}, u32[]{:S(2)}) async-start(bf16[16,64,128]{2,1,0:T(8,128)(2,1)} %by_head.3), calls=%async_computation.1 | async-start | bytes 524288 | tf_op jit(solution)/shard_map/all_to_all | solution.py:312
  20.3 20.5 %all-to-all-start = ((bf16[16,144,128]{2,1,0:T(8,128)(2,1)}), bf16[16,144,128]{2,1,0:T(8,128)(2,1)S(1)}, u32[]{:S(2)}, u32[]{:S(2)}) async-start(bf16[16,144,128]{2,1,0:T(8,128)(2,1)} %by_head.2), calls=%async_computation | async-start | bytes 1179648 | tf_op jit(solution)/shard_map/all_to_all | solution.py:312
  26.2 15.4 %collective-permute-start.3 = (bf16[16,64,128]{2,1,0:T(8,128)(2,1)S(1)}, bf16[16,64,128]{2,1,0:T(8,128)(2,1)S(1)}, u32[]{:S(2)}, u32[]{:S(2)}) collective-permute-start(bf16[16,64,128]{2,1,0:T(8,128)(2,1)S(1)} %all-to-all-done.1.kv0), channel_id=1, source_target_pairs={{0,32},{16,48},{32,0},{48,16},{64,96},{80,112},{96,64},{112,80},{1... | collective-permute-start | bytes 786440 | tf_op jit(solution)/shard_map/ppermute | solution.py:323
  29.3 12.4 %collective-permute-start.2 = (bf16[16,64,128]{2,1,0:T(8,128)(2,1)S(1)}, bf16[16,64,128]{2,1,0:T(8,128)(2,1)S(1)}, u32[]{:S(2)}, u32[]{:S(2)}) collective-permute-start(bf16[16,64,128]{2,1,0:T(8,128)(2,1)S(1)} %all-to-all-done.1.kv0), channel_id=1, source_target_pairs={{0,48},{16,0},{32,16},{48,32},{64,112},{80,64},{96,80},{112,96},{1... | collective-permute-start | bytes 786440 | tf_op jit(solution)/shard_map/ppermute | solution.py:323
  30.4 11.2 %collective-permute-start.1 = (bf16[16,64,128]{2,1,0:T(8,128)(2,1)S(1)}, bf16[16,64,128]{2,1,0:T(8,128)(2,1)S(1)}, u32[]{:S(2)}, u32[]{:S(2)}) collective-permute-start(bf16[16,64,128]{2,1,0:T(8,128)(2,1)S(1)} %all-to-all-done.1.kv0), channel_id=1, source_target_pairs={{0,16},{16,32},{32,48},{48,0},{64,80},{80,96},{96,112},{112,64},{1... | collective-permute-start | bytes 786440 | tf_op jit(solution)/shard_map/ppermute | solution.py:323
  41.4 2.0 %collective-permute-start = (bf16[16,144,128]{2,1,0:T(8,128)(2,1)S(1)}, bf16[16,144,128]{2,1,0:T(8,128)(2,1)S(1)}, u32[]{:S(2)}, u32[]{:S(2)}) collective-permute-start(bf16[16,144,128]{2,1,0:T(8,128)(2,1)S(1)} %all-to-all-done.own), channel_id=1, source_target_pairs={{0,2},{2,0},{4,6},{6,4},{8,10},{10,8},{12,14},{14,12},{1,3},{3,1},... | collective-permute-start | bytes 1769480 | tf_op jit(solution)/shard_map/ppermute | solution.py:316
  49.2 1.3 %collective-permute-start.4 = (f32[8,2048]{1,0:T(8,128)S(1)}, f32[8,2048]{1,0:T(8,128)S(1)}, u32[]{:S(2)}, u32[]{:S(2)}) collective-permute-start(f32[8,2048]{1,0:T(8,128)S(1)} %get-tuple-element.20.mine), channel_id=1, source_target_pairs={{0,2},{2,0},{4,6},{6,4},{8,10},{10,8},{12,14},{14,12},{1,3},{3,1},... | collective-permute-start | bytes 196616 | tf_op jit(solution)/shard_map/ppermute | solution.py:316
  56.7 14.6 %collective-permute-start.5 = (bf16[16,64,128]{2,1,0:T(8,128)(2,1)S(1)}, bf16[16,64,128]{2,1,0:T(8,128)(2,1)S(1)}, u32[]{:S(2)}, u32[]{:S(2)}) collective-permute-start(bf16[16,64,128]{2,1,0:T(8,128)(2,1)S(1)} %get-tuple-element.24), channel_id=1, source_target_pairs={{0,48},{16,0},{32,16},{48,32},{64,112},{80,64},{96,80},{112,96},{1... | collective-permute-start | bytes 786440 | tf_op jit(solution)/shard_map/ppermute | solution.py:323
  60.0 14.7 %collective-permute-start.6 = (bf16[16,64,128]{2,1,0:T(8,128)(2,1)S(1)}, bf16[16,64,128]{2,1,0:T(8,128)(2,1)S(1)}, u32[]{:S(2)}, u32[]{:S(2)}) collective-permute-start(bf16[16,64,128]{2,1,0:T(8,128)(2,1)S(1)} %get-tuple-element.25), channel_id=1, source_target_pairs={{0,16},{16,32},{32,48},{48,0},{64,80},{80,96},{96,112},{112,64},{1... | collective-permute-start | bytes 786440 | tf_op jit(solution)/shard_map/ppermute | solution.py:323
  60.0 14.7 %collective-permute-start.7 = (bf16[16,64,128]{2,1,0:T(8,128)(2,1)S(1)}, bf16[16,64,128]{2,1,0:T(8,128)(2,1)S(1)}, u32[]{:S(2)}, u32[]{:S(2)}) collective-permute-start(bf16[16,64,128]{2,1,0:T(8,128)(2,1)S(1)} %get-tuple-element.26), channel_id=1, source_target_pairs={{0,32},{16,48},{32,0},{48,16},{64,96},{80,112},{96,64},{112,80},{1... | collective-permute-start | bytes 786440 | tf_op jit(solution)/shard_map/ppermute | solution.py:323
  66.2 8.7 %collective-permute-start.8 = (bf16[16,64,128]{2,1,0:T(8,128)(2,1)S(1)}, bf16[16,64,128]{2,1,0:T(8,128)(2,1)S(1)}, u32[]{:S(2)}, u32[]{:S(2)}) collective-permute-start(bf16[16,64,128]{2,1,0:T(8,128)(2,1)S(1)} %get-tuple-element.29), channel_id=1, source_target_pairs={{0,2},{2,0},{4,6},{6,4},{8,10},{10,8},{12,14},{14,12},{1,3},{3,1},... | collective-permute-start | bytes 786440 | tf_op jit(solution)/shard_map/ppermute | solution.py:316

commit v7 on v6

--- a/solution.py
+++ b/solution.py
@@ -180,8 +180,11 @@
             send[tile] = (acc[begin + HALF : begin + TILE, :] * SCALE).astype(jnp.bfloat16)
 
 
-def pack_kernel(sums, keep, returned, out):
-    out[:, : 2 * PIECE, :] = sums[...]
+def pack_kernel(part0, part1, part2, part3, keep, returned, out):
+    sums = part0[...].astype(jnp.float32)
+    for part in (part1, part2, part3):
+        sums += part[...].astype(jnp.float32)
+    out[:, : 2 * PIECE, :] = sums.astype(jnp.bfloat16)
     out[:, 2 * PIECE :, :] = (keep[...] + returned[...].astype(jnp.float32)).astype(jnp.bfloat16)
 
 
@@ -244,15 +247,15 @@
     )(scalars, *kvs, lows)
 
 
-def pack_result(sums, keep, returned):
+def pack_result(*operands):
     return pl.pallas_call(
         pack_kernel,
         out_shape=jax.ShapeDtypeStruct((TILES, 2 * PIECE + HALF, DIM), jnp.bfloat16),
-        in_specs=[VMEM] * 3,
+        in_specs=[VMEM] * 6,
         out_specs=VMEM,
         compiler_params=PARAMS,
         name="pack",
-    )(sums, keep, returned)
+    )(*operands)
 
 
 def by_head_kernel(*refs):
@@ -364,8 +367,7 @@
     got3, got1, got2 = along(part3, 2), along(part1, 3), along(part2, 1)
     keep, send = query_grads(scalars, kvs, lows)
     returned = swap_cores(send)
-    sums = functools.reduce(jnp.add, [p.astype(jnp.float32) for p in (part0, got1, got2, got3)])
-    result = pack_result(sums.astype(jnp.bfloat16), keep, returned)
+    result = pack_result(part0, got1, got2, got3, keep, returned)
     key_grad, value_grad, query_grad = by_row(exchange(result))
     return query_grad, key_grad, value_grad
 

time: 94 us -> 93.9 us (level)
  no operation moved by 1% of the time
where the time goes in v7:
time: 93.9 us; the launch traced here: 93.6 us
  waiting for transfers between devices  25.7 us (27%)
  starting transfers between devices  24.2 us (26%)
  Pallas kernels  21 us (22%)
  blocking collectives  18.1 us (19%)
  local copies, waits for them, and re-layouts  2.04 us (2%)
  other arithmetic  1.86 us (2%)
    all_to_all x1, blocking collectives, exchange(): lax.all_to_all(a, ('tgt', 'src'), 0, 0, axis_index_groups=GROUPS, tiled=T...  18.1 us
    all_to_all x2, waiting for transfers between devices, exchange(): lax.all_to_all(a, ('tgt', 'src'), 0, 0, axis_index_groups=GROUPS, tiled=T...  14.4 us
    all_to_all x2, starting transfers between devices, exchange(): lax.all_to_all(a, ('tgt', 'src'), 0, 0, axis_index_groups=GROUPS, tiled=T...  13.8 us
    ppermute x6, starting transfers between devices, along(): return lax.ppermute(a, 'tgt', [(i, target(i)) for i in range(TILES)])  10.3 us
    ppermute x6, waiting for transfers between devices, along(): return lax.ppermute(a, 'tgt', [(i, target(i)) for i in range(TILES)])  8.19 us
    pallas_call x1, Pallas kernels, source_grads(): pl.pallas_call(source_grads_kernel, out_shape=[piece] * SIDE + [lows], in...  6.17 us
    pallas_call x1, Pallas kernels, row_stats(): pl.pallas_call(stats_kernel, out_shape=[jax.ShapeDtypeStruct((8, ROWS), j...  5.74 us
    pallas_call x1, Pallas kernels, query_grads(): pl.pallas_call(query_grads_kernel, out_shape=[jax.ShapeDtypeStruct(shape,...  4.33 us
  transfers between devices with their start and end apart: 11, of which 6 were waited for; matrix products, arithmetic and copies ran while one was open for 4% of the time, Pallas kernels for 7%

profile of v7, /device:TPU:32, one launch (start us, length us, event | category | flops | bytes accessed | tf_op | source)
XLA Modules:
  0.0 93.6 jit_solution(5046481326561654940)
XLA Ops:
  0.6 1.7 %by_head.3 = bf16[16,64,128]{2,1,0:T(8,128)(2,1)} custom-call(bf16[32,2048]{1,0:T(8,128)(2,1)} %refs_0_.3, bf16[32,2048]{1,0:T(8,128)(2,1)} %refs_1_.3), custom_call_target="tpu_custom_call" | custom-call | tf_op jit(solution)/shard_map/by_head/pallas_call | solution.py:274
  2.3 8.7 %all-to-all-start.1 = ((bf16[16,64,128]{2,1,0:T(8,128)(2,1)}), bf16[16,64,128]{2,1,0:T(8,128)(2,1)S(1)}, u32[]{:S(2)}, u32[]{:S(2)}) async-start(bf16[16,64,128]{2,1,0:T(8,128)(2,1)} %by_head.3), calls=%async_computation.1 | async-start | bytes 524288 | tf_op jit(solution)/shard_map/all_to_all | solution.py:315
  11.0 0.8 convert_bitcast_fusion
  11.8 1.1 %reshape.71 = s32[4,4,4,4,2,4]{2,1,0,5,4,3:T(4,128)S(1)} reshape(s32[64,32]{0,1:T(8,128)} %param.11) | data formatting | bytes 16384 | tf_op jit(solution)/shard_map/reshape | solution.py:336
  12.8 0.6 fusion.4.refs_2_
  13.5 1.9 %by_head.2 = bf16[16,144,128]{2,1,0:T(8,128)(2,1)} custom-call(bf16[64,2048]{1,0:T(8,128)(2,1)} %refs_0_.2, bf16[64,2048]{1,0:T(8,128)(2,1)} %refs_1_.2, bf16[16,128]{1,0:T(8,128)(2,1)} %fusion.4.refs_2_), custom_call_target="tpu_custom_call" | custom-call | tf_op jit(solution)/shard_map/by_head/pallas_call | solution.py:274
  15.4 4.9 %all-to-all-done.1.kv0 = bf16[16,64,128]{2,1,0:T(8,128)(2,1)S(1)} async-done(((bf16[16,64,128]{2,1,0:T(8,128)(2,1)}), bf16[16,64,128]{2,1,0:T(8,128)(2,1)S(1)}, u32[]{:S(2)}, u32[]{:S(2)}) %all-to-all-start.1) | async-done | bytes 262176 | tf_op jit(solution)/shard_map/all_to_all | solution.py:315
  20.3 5.1 %all-to-all-start = ((bf16[16,144,128]{2,1,0:T(8,128)(2,1)}), bf16[16,144,128]{2,1,0:T(8,128)(2,1)S(1)}, u32[]{:S(2)}, u32[]{:S(2)}) async-start(bf16[16,144,128]{2,1,0:T(8,128)(2,1)} %by_head.2), calls=%async_computation | async-start | bytes 1179648 | tf_op jit(solution)/shard_map/all_to_all | solution.py:315
  25.6 0.1 add.113
  25.7 0.1 broadcast_in_dim.29
  26.0 0.2 slice_reduce_fusion.1
  26.2 3.1 %collective-permute-start.3 = (bf16[16,64,128]{2,1,0:T(8,128)(2,1)S(1)}, bf16[16,64,128]{2,1,0:T(8,128)(2,1)S(1)}, u32[]{:S(2)}, u32[]{:S(2)}) collective-permute-start(bf16[16,64,128]{2,1,0:T(8,128)(2,1)S(1)} %all-to-all-done.1.kv0), channel_id=1, source_target_pairs={{0,32},{16,48},{32,0},{48,16},{64,96},{80,112},{96,64},{112,80},{1... | collective-permute-start | bytes 786440 | tf_op jit(solution)/shard_map/ppermute | solution.py:326
  29.3 1.1 %collective-permute-start.2 = (bf16[16,64,128]{2,1,0:T(8,128)(2,1)S(1)}, bf16[16,64,128]{2,1,0:T(8,128)(2,1)S(1)}, u32[]{:S(2)}, u32[]{:S(2)}) collective-permute-start(bf16[16,64,128]{2,1,0:T(8,128)(2,1)S(1)} %all-to-all-done.1.kv0), channel_id=1, source_target_pairs={{0,48},{16,0},{32,16},{48,32},{64,112},{80,64},{96,80},{112,96},{1... | collective-permute-start | bytes 786440 | tf_op jit(solution)/shard_map/ppermute | solution.py:326
  30.4 0.9 collective-permute-start.1
  31.3 9.5 %all-to-all-done.own = bf16[16,144,128]{2,1,0:T(8,128)(2,1)S(1)} async-done(((bf16[16,144,128]{2,1,0:T(8,128)(2,1)}), bf16[16,144,128]{2,1,0:T(8,128)(2,1)S(1)}, u32[]{:S(2)}, u32[]{:S(2)}) %all-to-all-start) | async-done | bytes 589856 | tf_op jit(solution)/shard_map/all_to_all | solution.py:315
  40.9 0.2 slice_reduce_fusion
  41.1 0.2 convert_reduce_fusion
  41.3 0.1 concatenate.12.scalars
  41.7 1.8 %collective-permute-done.other = bf16[16,144,128]{2,1,0:T(8,128)(2,1)S(1)} collective-permute-done((bf16[16,144,128]{2,1,0:T(8,128)(2,1)S(1)}, bf16[16,144,128]{2,1,0:T(8,128)(2,1)S(1)}, u32[]{:S(2)}, u32[]{:S(2)}) %collective-permute-start) | collective-permute-done | bytes 589856 | tf_op jit(solution)/shard_map/ppermute | solution.py:319
  43.5 5.7 %stats.1 = (f32[8,2048]{1,0:T(8,128)S(1)}, f32[16,512,512]{2,1,0:T(8,128)S(1)}, f32[16,512,512]{2,1,0:T(8,128)S(1)}) custom-call(s32[12]{0:T(128)S(1)} %concatenate.12.scalars, s32[16,2048]{1,0:T(8,128)S(1)} %select_subtract_fusion.lim, bf16[16,144,128]{2,1,0:T(8,128)(2,1)S(1)} %all-to-all-done.own, bf16[16,144,128]{2,1,0:T(8,128)(2,1)S(1)} %collective-permute-done.other, ...), custom_call_target="tpu_custom_call" | custom-call | flops 2684354560 | bytes 1048576 | tf_op jit(solution)/shard_map/stats/pallas_call | solution.py:203
  49.2 0.1 collective-permute-start.4
  49.3 1.2 %collective-permute-done.4.theirs = f32[8,2048]{1,0:T(8,128)S(1)} collective-permute-done((f32[8,2048]{1,0:T(8,128)S(1)}, f32[8,2048]{1,0:T(8,128)S(1)}, u32[]{:S(2)}, u32[]{:S(2)}) %collective-permute-start.4) | collective-permute-done | bytes 65568 | tf_op jit(solution)/shard_map/ppermute | solution.py:319
  50.5 6.2 %source_grads.1 = (bf16[16,64,128]{2,1,0:T(8,128)(2,1)S(1)}, bf16[16,64,128]{2,1,0:T(8,128)(2,1)S(1)}, bf16[16,64,128]{2,1,0:T(8,128)(2,1)S(1)}, bf16[16,64,128]...) custom-call(s32[12]{0:T(128)S(1)} %concatenate.12.scalars, bf16[16,144,128]{2,1,0:T(8,128)(2,1)S(1)} %all-to-all-done.own, ...), custom_call_target="tpu_custom_call" | custom-call | flops 2684354560 | bytes 1048576 | tf_op jit(solution)/shard_map/source_grads/pallas_call | solution.py:219
  56.7 2.8 %collective-permute-start.5 = (bf16[16,64,128]{2,1,0:T(8,128)(2,1)S(1)}, bf16[16,64,128]{2,1,0:T(8,128)(2,1)S(1)}, u32[]{:S(2)}, u32[]{:S(2)}) collective-permute-start(bf16[16,64,128]{2,1,0:T(8,128)(2,1)S(1)} %get-tuple-element.24), channel_id=1, source_target_pairs={{0,48},{16,0},{32,16},{48,32},{64,112},{80,64},{96,80},{112,96},{1... | collective-permute-start | bytes 786440 | tf_op jit(solution)/shard_map/ppermute | solution.py:326
  59.5 2.3 %collective-permute-start.7 = (bf16[16,64,128]{2,1,0:T(8,128)(2,1)S(1)}, bf16[16,64,128]{2,1,0:T(8,128)(2,1)S(1)}, u32[]{:S(2)}, u32[]{:S(2)}) collective-permute-start(bf16[16,64,128]{2,1,0:T(8,128)(2,1)S(1)} %get-tuple-element.26), channel_id=1, source_target_pairs={{0,32},{16,48},{32,0},{48,16},{64,96},{80,112},{96,64},{112,80},{1... | collective-permute-start | bytes 786440 | tf_op jit(solution)/shard_map/ppermute | solution.py:326
  61.8 4.3 %query_grads.1 = (f32[16,64,128]{2,1,0:T(8,128)S(1)}, bf16[16,64,128]{2,1,0:T(8,128)(2,1)S(1)}) custom-call(s32[12]{0:T(128)S(1)} %concatenate.12.scalars, bf16[16,64,128]{2,1,0:T(8,128)(2,1)S(1)} %all-to-all-done.1.kv0, bf16[16,64,128]{2,1,0:T(8,128)(2,1)S(1)} %collective-permute-done.1.kv1, bf16[16,64,128]{2,1,0:T(8,128)(2,1)S(1)} %collective-permute-done.2.kv2, ...), custom_call_target="tpu_custom_call" | custom-call | flops 671088640 | bytes 1048576 | tf_op jit(solution)/shard_map/query_grads/pallas_call | solution.py:238
  66.2 0.1 collective-permute-start.8
  66.3 4.8 %collective-permute-done.5.part1 = bf16[16,64,128]{2,1,0:T(8,128)(2,1)S(1)} collective-permute-done((bf16[16,64,128]{2,1,0:T(8,128)(2,1)S(1)}, bf16[16,64,128]{2,1,0:T(8,128)(2,1)S(1)}, u32[]{:S(2)}, u32[]{:S(2)}) %collective-permute-start.5) | collective-permute-done | bytes 262176 | tf_op jit(solution)/shard_map/ppermute | solution.py:326
  71.0 3.4 %collective-permute-done.6.part2 = bf16[16,64,128]{2,1,0:T(8,128)(2,1)S(1)} collective-permute-done((bf16[16,64,128]{2,1,0:T(8,128)(2,1)S(1)}, bf16[16,64,128]{2,1,0:T(8,128)(2,1)S(1)}, u32[]{:S(2)}, u32[]{:S(2)}) %collective-permute-start.6) | collective-permute-done | bytes 262176 | tf_op jit(solution)/shard_map/ppermute | solution.py:326
  74.5 0.2 pack.1
  74.6 18.1 %all_to_all.15.heads = bf16[16,128,128]{2,1,0:T(8,128)(2,1)S(1)} all-to-all(bf16[16,128,128]{2,1,0:T(8,128)(2,1)S(1)} %pack.1), channel_id=1, replica_groups={{0,64,128,192,4,68,132,196,8,72,136,200,12,76,140,204},{2,66,130,194,6,..., dimensions={0} | all-to-all | bytes 1048576 | tf_op jit(solution)/shard_map/all_to_all | solution.py:315
  92.7 0.9 by_row.1
  (23 shorter events, 0.6 us)
Async XLA Ops:
  2.3 18.0 %all-to-all-start.1 = ((bf16[16,64,128]{2,1,0:T(8,128)(2,1)}), bf16[16,64,128]{2,1,0:T(8,128)(2,1)S(1)}, u32[]{:S(2)}, u32[]{:S(2)}) async-start(bf16[16,64,128]{2,1,0:T(8,128)(2,1)} %by_head.3), calls=%async_computation.1 | async-start | bytes 524288 | tf_op jit(solution)/shard_map/all_to_all | solution.py:315
  20.3 20.5 %all-to-all-start = ((bf16[16,144,128]{2,1,0:T(8,128)(2,1)}), bf16[16,144,128]{2,1,0:T(8,128)(2,1)S(1)}, u32[]{:S(2)}, u32[]{:S(2)}) async-start(bf16[16,144,128]{2,1,0:T(8,128)(2,1)} %by_head.2), calls=%async_computation | async-start | bytes 1179648 | tf_op jit(solution)/shard_map/all_to_all | solution.py:315
  26.2 15.4 %collective-permute-start.3 = (bf16[16,64,128]{2,1,0:T(8,128)(2,1)S(1)}, bf16[16,64,128]{2,1,0:T(8,128)(2,1)S(1)}, u32[]{:S(2)}, u32[]{:S(2)}) collective-permute-start(bf16[16,64,128]{2,1,0:T(8,128)(2,1)S(1)} %all-to-all-done.1.kv0), channel_id=1, source_target_pairs={{0,32},{16,48},{32,0},{48,16},{64,96},{80,112},{96,64},{112,80},{1... | collective-permute-start | bytes 786440 | tf_op jit(solution)/shard_map/ppermute | solution.py:326
  29.3 12.4 %collective-permute-start.2 = (bf16[16,64,128]{2,1,0:T(8,128)(2,1)S(1)}, bf16[16,64,128]{2,1,0:T(8,128)(2,1)S(1)}, u32[]{:S(2)}, u32[]{:S(2)}) collective-permute-start(bf16[16,64,128]{2,1,0:T(8,128)(2,1)S(1)} %all-to-all-done.1.kv0), channel_id=1, source_target_pairs={{0,48},{16,0},{32,16},{48,32},{64,112},{80,64},{96,80},{112,96},{1... | collective-permute-start | bytes 786440 | tf_op jit(solution)/shard_map/ppermute | solution.py:326
  30.4 11.2 %collective-permute-start.1 = (bf16[16,64,128]{2,1,0:T(8,128)(2,1)S(1)}, bf16[16,64,128]{2,1,0:T(8,128)(2,1)S(1)}, u32[]{:S(2)}, u32[]{:S(2)}) collective-permute-start(bf16[16,64,128]{2,1,0:T(8,128)(2,1)S(1)} %all-to-all-done.1.kv0), channel_id=1, source_target_pairs={{0,16},{16,32},{32,48},{48,0},{64,80},{80,96},{96,112},{112,64},{1... | collective-permute-start | bytes 786440 | tf_op jit(solution)/shard_map/ppermute | solution.py:326
  41.4 2.0 %collective-permute-start = (bf16[16,144,128]{2,1,0:T(8,128)(2,1)S(1)}, bf16[16,144,128]{2,1,0:T(8,128)(2,1)S(1)}, u32[]{:S(2)}, u32[]{:S(2)}) collective-permute-start(bf16[16,144,128]{2,1,0:T(8,128)(2,1)S(1)} %all-to-all-done.own), channel_id=1, source_target_pairs={{0,2},{2,0},{4,6},{6,4},{8,10},{10,8},{12,14},{14,12},{1,3},{3,1},... | collective-permute-start | bytes 1769480 | tf_op jit(solution)/shard_map/ppermute | solution.py:319
  49.2 1.3 %collective-permute-start.4 = (f32[8,2048]{1,0:T(8,128)S(1)}, f32[8,2048]{1,0:T(8,128)S(1)}, u32[]{:S(2)}, u32[]{:S(2)}) collective-permute-start(f32[8,2048]{1,0:T(8,128)S(1)} %get-tuple-element.20.mine), channel_id=1, source_target_pairs={{0,2},{2,0},{4,6},{6,4},{8,10},{10,8},{12,14},{14,12},{1,3},{3,1},... | collective-permute-start | bytes 196616 | tf_op jit(solution)/shard_map/ppermute | solution.py:319
  56.7 14.3 %collective-permute-start.5 = (bf16[16,64,128]{2,1,0:T(8,128)(2,1)S(1)}, bf16[16,64,128]{2,1,0:T(8,128)(2,1)S(1)}, u32[]{:S(2)}, u32[]{:S(2)}) collective-permute-start(bf16[16,64,128]{2,1,0:T(8,128)(2,1)S(1)} %get-tuple-element.24), channel_id=1, source_target_pairs={{0,48},{16,0},{32,16},{48,32},{64,112},{80,64},{96,80},{112,96},{1... | collective-permute-start | bytes 786440 | tf_op jit(solution)/shard_map/ppermute | solution.py:326
  59.5 14.9 %collective-permute-start.6 = (bf16[16,64,128]{2,1,0:T(8,128)(2,1)S(1)}, bf16[16,64,128]{2,1,0:T(8,128)(2,1)S(1)}, u32[]{:S(2)}, u32[]{:S(2)}) collective-permute-start(bf16[16,64,128]{2,1,0:T(8,128)(2,1)S(1)} %get-tuple-element.25), channel_id=1, source_target_pairs={{0,16},{16,32},{32,48},{48,0},{64,80},{80,96},{96,112},{112,64},{1... | collective-permute-start | bytes 786440 | tf_op jit(solution)/shard_map/ppermute | solution.py:326
  59.5 14.9 %collective-permute-start.7 = (bf16[16,64,128]{2,1,0:T(8,128)(2,1)S(1)}, bf16[16,64,128]{2,1,0:T(8,128)(2,1)S(1)}, u32[]{:S(2)}, u32[]{:S(2)}) collective-permute-start(bf16[16,64,128]{2,1,0:T(8,128)(2,1)S(1)} %get-tuple-element.26), channel_id=1, source_target_pairs={{0,32},{16,48},{32,0},{48,16},{64,96},{80,112},{96,64},{112,80},{1... | collective-permute-start | bytes 786440 | tf_op jit(solution)/shard_map/ppermute | solution.py:326
  66.2 8.3 %collective-permute-start.8 = (bf16[16,64,128]{2,1,0:T(8,128)(2,1)S(1)}, bf16[16,64,128]{2,1,0:T(8,128)(2,1)S(1)}, u32[]{:S(2)}, u32[]{:S(2)}) collective-permute-start(bf16[16,64,128]{2,1,0:T(8,128)(2,1)S(1)} %get-tuple-element.29), channel_id=1, source_target_pairs={{0,2},{2,0},{4,6},{6,4},{8,10},{10,8},{12,14},{14,12},{1,3},{3,1},... | collective-permute-start | bytes 786440 | tf_op jit(solution)/shard_map/ppermute | solution.py:319
